TPU v7x, 32 devices: a whole 2x2x4 slice. The times are simulated.
32 devices in a mesh: groups: 2 (over y), seq: 8 (over z, x), head: 2 (over core).
Axes of the slice: x: 2, y: 2, z: 4, core: 2. Of those that a mesh axis runs over, the one named last changes fastest.
Arguments:
- big_queries: bfloat16 [512, 4096], P(('groups', 'seq'), 'head'), parts along dimension 0, may hold values from -160 to 160
- big_keys: bfloat16 [512, 4096], P(('groups', 'seq'), 'head'), parts along dimension 0, may hold values from -8 to 8
- big_values: bfloat16 [512, 4096], P(('groups', 'seq'), 'head'), parts along dimension 0, may hold values from -6 to 6
- small_queries: bfloat16 [512, 1024], P(('groups', 'seq', 'head')), parts along dimension 0, may hold values from -160 to 160
- small_keys: bfloat16 [512, 1024], P(('groups', 'seq', 'head')), parts along dimension 0, may hold values from -8 to 8
- small_values: bfloat16 [512, 1024], P(('groups', 'seq', 'head')), parts along dimension 0, may hold values from -6 to 6
- big_readout: bfloat16 [4096, 64], P('head'), may hold values from -0.75 to 0.75
- small_readout: bfloat16 [1024, 64], replicated, may hold values from -1.5 to 1.5
- guidance: float32 [2], P('groups'), parts along dimension 0, may hold values from 1 to 4
Outputs:
- guided: float32 [256, 128], P(('groups', 'seq')), parts along dimension 0
There are 2 independent parts, one for each index of `groups`. A program takes and returns all parts, laid end to end along the dimension named above; an argument that names none is the same for every part. Nothing has to cross between parts.
All inputs are finite; a program needn't handle non-finite values.
Results may differ from a plain program's by a relative error of at most 0.0035.
Values may be sent and summed in bfloat16 or wider, within the bound.
No kernel may reach another device: no remote copies, remote signals or barrier semaphores. Data moves between devices by JAX's collectives and lax.ppermute only.
A program may use at most 64 MiB of HBM per device.

v0:
```python
import math

import jax
import jax.numpy as jnp
from jax import lax
from jax.sharding import PartitionSpec as P

DH = 128


def split_heads(matrix, blocks, parts):
    rows_here, columns = matrix.shape
    shaped = matrix.reshape(blocks, rows_here // blocks, parts, columns // parts)
    shaped = jnp.transpose(shaped, (0, 2, 1, 3))
    return shaped.reshape(blocks * parts, rows_here // blocks, columns // parts)


def copy_heads(matrix, blocks, parts):
    rows_here, columns = matrix.shape
    shaped = jnp.transpose(matrix.reshape(rows_here, parts, columns // parts), (1, 0, 2))
    shaped = jnp.broadcast_to(shaped[None], (blocks, parts, rows_here, columns // parts))
    return shaped.reshape(blocks * parts, rows_here, columns // parts)


def join_heads(stacked, blocks, parts):
    pieces, rows_here, columns = stacked.shape
    shaped = stacked.reshape(blocks, parts, rows_here, columns)
    shaped = jnp.transpose(shaped, (0, 2, 1, 3))
    return shaped.reshape(blocks * rows_here, parts * columns)


def attend(query_rows, key_rows, value_rows):
    query_count = query_rows.shape[0]
    heads_here = query_rows.shape[1] // DH
    key_count = key_rows.shape[0]
    block_height = math.gcd(query_count, 256)
    block_count = query_count // block_height
    query_blocks = query_rows.reshape(block_count, block_height, heads_here, DH)
    key_split = key_rows.reshape(key_count, heads_here, DH)
    value_split = value_rows.reshape(key_count, heads_here, DH)
    score_scale = 1.0 / math.sqrt(DH)

    def one_block(query_block):
        scores = (
            jnp.einsum("qgd,kgd->gqk", query_block, key_split, preferred_element_type=jnp.float32)
            * score_scale
        )
        row_max = jnp.max(scores, axis=2, keepdims=True)
        probs = jnp.exp(scores - row_max)
        totals = jnp.sum(probs, axis=2, keepdims=True)
        weights = probs.astype(jnp.bfloat16)
        accumulated = jnp.einsum(
            "gqk,kgd->gqd", weights, value_split, preferred_element_type=jnp.float32
        )
        attended = accumulated / totals
        attended = jnp.transpose(attended, (1, 0, 2)).reshape(block_height, heads_here * DH)
        return attended.astype(jnp.bfloat16)

    outputs = lax.map(one_block, query_blocks)
    return outputs.reshape(query_count, heads_here * DH)


def shards(
    big_queries,
    big_keys,
    big_values,
    small_queries,
    small_keys,
    small_values,
    big_readout,
    small_readout,
    guidance,
):
    seq_count = lax.axis_size("seq")
    big_heads = big_queries.shape[1] // DH
    big_group = max(big_heads // seq_count, 1)
    big_blocks = max(seq_count // big_heads, 1)
    big_parts = big_heads // big_group
    query_rows = lax.all_to_all(
        split_heads(big_queries, big_blocks, big_parts),
        "seq",
        split_axis=0,
        concat_axis=1,
        tiled=True,
    )[0]
    key_copies, value_copies = (
        lax.all_to_all(
            copy_heads(big_keys, big_blocks, big_parts),
            "seq",
            split_axis=0,
            concat_axis=1,
            tiled=True,
        ),
        lax.all_to_all(
            copy_heads(big_values, big_blocks, big_parts),
            "seq",
            split_axis=0,
            concat_axis=1,
            tiled=True,
        ),
    )
    key_rows = key_copies[0]
    value_rows = value_copies[0]
    big_out = attend(query_rows, key_rows, value_rows)
    big_back = lax.all_to_all(big_out[None], "seq", split_axis=1, concat_axis=0, tiled=True)
    big_attention = join_heads(big_back, big_blocks, big_parts)
    big_partial = jnp.dot(big_attention, big_readout, preferred_element_type=jnp.float32)
    small_heads = small_queries.shape[1] // DH
    small_group = max(small_heads // seq_count, 1)
    small_blocks = max(seq_count // small_heads, 1)
    small_parts = small_heads // small_group
    small_query_rows = lax.all_to_all(
        split_heads(small_queries, small_blocks, small_parts),
        "seq",
        split_axis=0,
        concat_axis=1,
        tiled=True,
    )[0]
    key_copies, value_copies = (
        lax.all_to_all(
            copy_heads(small_keys, small_blocks, small_parts),
            "seq",
            split_axis=0,
            concat_axis=1,
            tiled=True,
        ),
        lax.all_to_all(
            copy_heads(small_values, small_blocks, small_parts),
            "seq",
            split_axis=0,
            concat_axis=1,
            tiled=True,
        ),
    )
    small_key_rows, small_value_rows = (
        lax.all_gather(key_copies[0], "head", axis=0, tiled=True),
        lax.all_gather(value_copies[0], "head", axis=0, tiled=True),
    )
    small_out = attend(small_query_rows, small_key_rows, small_value_rows)
    small_back = lax.all_to_all(small_out[None], "seq", split_axis=1, concat_axis=0, tiled=True)
    small_attention = join_heads(small_back, small_blocks, small_parts)
    small_latent = jnp.dot(small_attention, small_readout, preferred_element_type=jnp.float32)
    weight_value = guidance[0]
    core_index = lax.axis_index("head")
    placed = lax.dynamic_update_slice(
        jnp.zeros_like(big_partial),
        small_latent,
        (core_index * small_latent.shape[0], jnp.zeros((), jnp.int32)),
    )
    blended = lax.psum((1.0 + weight_value) * big_partial - weight_value * placed, "head")
    return blended.reshape(blended.shape[0] // 2, 2 * blended.shape[1])


def solution(mesh):
    placed = (
        P(("groups", "seq"), "head"),
        P(("groups", "seq"), "head"),
        P(("groups", "seq"), "head"),
        P(("groups", "seq", "head"), None),
        P(("groups", "seq", "head"), None),
        P(("groups", "seq", "head"), None),
        P("head", None),
        P(),
        P("groups"),
    )
    return jax.shard_map(
        shards, mesh=mesh, in_specs=placed, out_specs=P(("groups", "seq"), None), check_vma=False
    )
```

profile of v0, /device:TPU:0, one launch (start us, length us, event | category | flops | bytes accessed | tf_op | source)
XLA Modules:
  0.0 93.8 jit_solution(16511722047531669533)
XLA Ops:
  0.0 0.0 copy-start
  0.0 0.8 copy.72
  0.8 0.6 copy.60
  1.4 0.0 copy-start.5
  1.4 7.4 %all-to-all-start.6 = ((bf16[8,16,128]{2,1,0:T(8,128)(2,1)}), bf16[8,16,128]{2,1,0:T(8,128)(2,1)S(1)}, u32[]{:S(2)}, u32[]{:S(2)}) async-start(bf16[8,16,128]{2,1,0:T(8,128)(2,1)} %copy.60), calls=%async_computation.6 | async-start | bytes 65536 | tf_op jit(solution)/shard_map/all_to_all | solution.py:127
  8.8 0.0 copy-done.5
  8.8 0.0 copy-start.6
  8.8 0.7 copy-done.6
  9.6 0.6 copy.59
  10.2 0.0 copy-start.1
  10.2 5.3 %all-to-all-done.6 = bf16[8,16,128]{2,1,0:T(8,128)(2,1)S(1)} async-done(((bf16[8,16,128]{2,1,0:T(8,128)(2,1)}), bf16[8,16,128]{2,1,0:T(8,128)(2,1)S(1)}, u32[]{:S(2)}, u32[]{:S(2)}) %all-to-all-start.6) | async-done | bytes 32800 | tf_op jit(solution)/shard_map/all_to_all | solution.py:127
  15.5 3.3 %all-to-all-start.5 = ((bf16[8,16,128]{2,1,0:T(8,128)(2,1)}), bf16[8,16,128]{2,1,0:T(8,128)(2,1)S(1)}, u32[]{:S(2)}, u32[]{:S(2)}) async-start(bf16[8,16,128]{2,1,0:T(8,128)(2,1)} %copy.59), calls=%async_computation.5 | async-start | bytes 65536 | tf_op jit(solution)/shard_map/all_to_all | solution.py:120
  18.9 0.6 copy.58
  19.5 6.0 %all-to-all-done.5 = bf16[8,16,128]{2,1,0:T(8,128)(2,1)S(1)} async-done(((bf16[8,16,128]{2,1,0:T(8,128)(2,1)}), bf16[8,16,128]{2,1,0:T(8,128)(2,1)S(1)}, u32[]{:S(2)}, u32[]{:S(2)}) %all-to-all-start.5) | async-done | bytes 32800 | tf_op jit(solution)/shard_map/all_to_all | solution.py:120
  25.5 3.3 %all-to-all-start.4 = ((bf16[8,16,128]{2,1,0:T(8,128)(2,1)}), bf16[8,16,128]{2,1,0:T(8,128)(2,1)S(1)}, u32[]{:S(2)}, u32[]{:S(2)}) async-start(bf16[8,16,128]{2,1,0:T(8,128)(2,1)} %copy.58), calls=%async_computation.4 | async-start | bytes 65536 | tf_op jit(solution)/shard_map/all_to_all | solution.py:112
  28.8 0.0 copy-done.1
  28.8 0.0 copy-start.2
  28.8 0.7 copy.93
  29.5 0.3 copy-done.2
  29.8 0.0 copy-start.3
  29.8 0.7 copy.95
  30.5 0.2 copy-done.3
  30.7 0.7 copy.94
  31.4 1.8 %all_gather.7 = bf16[256,128]{1,0:T(8,128)(2,1)S(1)} all-gather(bf16[128,128]{1,0:T(8,128)(2,1)S(1)} %bitcast.91), channel_id=1, replica_groups=mesh['groups'=2,'seq'=8,'head'=2] {'head'}, dimensions={0}, use_global_device_ids=true | all-gather | bytes 98304 | tf_op jit(solution)/shard_map/all_gather | solution.py:137
  33.2 1.8 %all_gather.6 = bf16[256,128]{1,0:T(8,128)(2,1)S(1)} all-gather(bf16[128,128]{1,0:T(8,128)(2,1)S(1)} %bitcast.92), channel_id=1, replica_groups=mesh['groups'=2,'seq'=8,'head'=2] {'head'}, dimensions={0}, use_global_device_ids=true | all-gather | bytes 98304 | tf_op jit(solution)/shard_map/all_gather | solution.py:136
  35.1 0.4 all-to-all-done.4
  35.4 5.6 %all-to-all-start.1 = ((bf16[8,32,256]{2,1,0:T(8,128)(2,1)}), bf16[8,32,256]{2,1,0:T(8,128)(2,1)S(1)}, u32[]{:S(2)}, u32[]{:S(2)}) async-start(bf16[8,32,256]{2,1,0:T(8,128)(2,1)} %bitcast.75), calls=%async_computation.1 | async-start | bytes 262144 | tf_op jit(solution)/shard_map/all_to_all | solution.py:87
  41.0 0.3 fusion.19
  41.3 7.1 %all-to-all-done.1 = bf16[8,32,256]{2,1,0:T(8,128)(2,1)S(1)} async-done(((bf16[8,32,256]{2,1,0:T(8,128)(2,1)}), bf16[8,32,256]{2,1,0:T(8,128)(2,1)S(1)}, u32[]{:S(2)}, u32[]{:S(2)}) %all-to-all-start.1) | async-done | bytes 131104 | tf_op jit(solution)/shard_map/all_to_all | solution.py:87
  48.3 3.4 %all-to-all-start = ((bf16[8,32,256]{2,1,0:T(8,128)(2,1)}), bf16[8,32,256]{2,1,0:T(8,128)(2,1)S(1)}, u32[]{:S(2)}, u32[]{:S(2)}) async-start(bf16[8,32,256]{2,1,0:T(8,128)(2,1)} %bitcast.78), calls=%async_computation | async-start | bytes 262144 | tf_op jit(solution)/shard_map/all_to_all | solution.py:79
  51.7 0.2 fusion.12
  51.9 0.2 fusion.3
  52.1 0.1 copy.96
  52.2 0.5 broadcast.21
  52.7 0.8 reduce.5
  53.5 0.6 reshape.126
  54.2 4.8 %all-to-all-done = bf16[8,32,256]{2,1,0:T(8,128)(2,1)S(1)} async-done(((bf16[8,32,256]{2,1,0:T(8,128)(2,1)}), bf16[8,32,256]{2,1,0:T(8,128)(2,1)S(1)}, u32[]{:S(2)}, u32[]{:S(2)}) %all-to-all-start) | async-done | bytes 131104 | tf_op jit(solution)/shard_map/all_to_all | solution.py:79
  59.0 3.4 %all-to-all-start.2 = ((bf16[8,32,256]{2,1,0:T(8,128)(2,1)}), bf16[8,32,256]{2,1,0:T(8,128)(2,1)S(1)}, u32[]{:S(2)}, u32[]{:S(2)}) async-start(bf16[8,32,256]{2,1,0:T(8,128)(2,1)} %bitcast.77), calls=%async_computation.2 | async-start | bytes 262144 | tf_op jit(solution)/shard_map/all_to_all | solution.py:94
  62.4 0.2 fusion.18
  62.7 0.1 fusion.5
  62.8 6.9 %all-to-all-done.2 = bf16[8,32,256]{2,1,0:T(8,128)(2,1)S(1)} async-done(((bf16[8,32,256]{2,1,0:T(8,128)(2,1)}), bf16[8,32,256]{2,1,0:T(8,128)(2,1)S(1)}, u32[]{:S(2)}, u32[]{:S(2)}) %all-to-all-start.2) | async-done | bytes 131104 | tf_op jit(solution)/shard_map/all_to_all | solution.py:94
  69.7 3.3 %all-to-all-start.7 = ((bf16[8,2,1024]{2,1,0:T(2,128)(2,1)}), bf16[8,2,1024]{2,1,0:T(2,128)(2,1)S(1)}, u32[]{:S(2)}, u32[]{:S(2)}) async-start(bf16[8,2,1024]{2,1,0:T(2,128)(2,1)} %reshape.126), calls=%async_computation.7 | async-start | bytes 65536 | tf_op jit(solution)/shard_map/all_to_all | solution.py:140
  73.0 0.2 fusion.1
  73.3 0.2 copy.56
  73.5 1.4 %reduce.4 = bf16[256,256]{1,0:T(8,128)(2,1)S(1)} reduce(bf16[256,1,256]{2,1,0:T(2,128)(2,1)S(1)} %bitcast.83, bf16[]{:T(256)} %broadcast.21), dimensions={1}, to_apply=%bitcast.63.reduce_sub_computation | reduce | bytes 262146
  74.9 0.7 reshape.124
  75.6 4.0 %all-to-all-done.7 = bf16[8,2,1024]{2,1,0:T(2,128)(2,1)S(1)} async-done(((bf16[8,2,1024]{2,1,0:T(2,128)(2,1)}), bf16[8,2,1024]{2,1,0:T(2,128)(2,1)S(1)}, u32[]{:S(2)}, u32[]{:S(2)}) %all-to-all-start.7) | async-done | bytes 32800 | tf_op jit(solution)/shard_map/all_to_all | solution.py:140
  79.6 3.4 %all-to-all-start.3 = ((bf16[8,2,4096]{2,1,0:T(2,128)(2,1)}), bf16[8,2,4096]{2,1,0:T(2,128)(2,1)S(1)}, u32[]{:S(2)}, u32[]{:S(2)}) async-start(bf16[8,2,4096]{2,1,0:T(2,128)(2,1)} %reshape.124), calls=%async_computation.3 | async-start | bytes 262144 | tf_op jit(solution)/shard_map/all_to_all | solution.py:105
  83.6 0.0 copy-start.4
  83.7 0.8 copy-done.4
  84.6 0.1 convolution_dynamic-update-slice_fusion
  84.7 5.6 %all-to-all-done.3 = bf16[8,2,4096]{2,1,0:T(2,128)(2,1)S(1)} async-done(((bf16[8,2,4096]{2,1,0:T(2,128)(2,1)}), bf16[8,2,4096]{2,1,0:T(2,128)(2,1)S(1)}, u32[]{:S(2)}, u32[]{:S(2)}) %all-to-all-start.3) | async-done | bytes 131104 | tf_op jit(solution)/shard_map/all_to_all | solution.py:105
  90.3 0.1 reshape.125
  90.5 0.0 copy-done
  90.5 0.2 fusion.4
  90.7 0.1 reshape.123
  90.7 3.1 %psum.7 = f32[16,128]{1,0:T(8,128)} all-reduce(f32[16,128]{1,0:T(8,128)S(1)} %reshape.123), channel_id=1, replica_groups=mesh['groups'=2,'seq'=8,'head'=2] {'head'}, use_global_device_ids=true, to_apply=%region_4.5 | all-reduce | flops 2048 | bytes 16384 | tf_op jit(solution)/shard_map/psum | solution.py:150
  (13 shorter events, 0.2 us)
Async XLA Ops:
  0.0 90.5 %copy-start = (bf16[2048,64]{0,1:T(8,128)(2,1)S(1)}, bf16[2048,64]{0,1:T(8,128)(2,1)}, u32[]{:S(2)}) copy-start(bf16[2048,64]{0,1:T(8,128)(2,1)} %param.15) | copy-start | bytes 786436
  1.4 7.4 %copy-start.5 = (bf16[16,1024]{1,0:T(8,128)(2,1)S(1)}, bf16[16,1024]{1,0:T(8,128)(2,1)}, u32[]{:S(2)}) copy-start(bf16[16,1024]{1,0:T(8,128)(2,1)} %param.12) | copy-start | bytes 98308
  1.4 14.1 %all-to-all-start.6 = ((bf16[8,16,128]{2,1,0:T(8,128)(2,1)}), bf16[8,16,128]{2,1,0:T(8,128)(2,1)S(1)}, u32[]{:S(2)}, u32[]{:S(2)}) async-start(bf16[8,16,128]{2,1,0:T(8,128)(2,1)} %copy.60), calls=%async_computation.6 | async-start | bytes 65536 | tf_op jit(solution)/shard_map/all_to_all | solution.py:127
  8.8 0.8 copy-start.6
  10.2 18.6 %copy-start.1 = (bf16[32,2048]{1,0:T(8,128)(2,1)S(1)}, bf16[32,2048]{1,0:T(8,128)(2,1)}, u32[]{:S(2)}) copy-start(bf16[32,2048]{1,0:T(8,128)(2,1)} %param.10) | copy-start | bytes 393220
  15.5 10.0 %all-to-all-start.5 = ((bf16[8,16,128]{2,1,0:T(8,128)(2,1)}), bf16[8,16,128]{2,1,0:T(8,128)(2,1)S(1)}, u32[]{:S(2)}, u32[]{:S(2)}) async-start(bf16[8,16,128]{2,1,0:T(8,128)(2,1)} %copy.59), calls=%async_computation.5 | async-start | bytes 65536 | tf_op jit(solution)/shard_map/all_to_all | solution.py:120
  25.5 10.0 %all-to-all-start.4 = ((bf16[8,16,128]{2,1,0:T(8,128)(2,1)}), bf16[8,16,128]{2,1,0:T(8,128)(2,1)S(1)}, u32[]{:S(2)}, u32[]{:S(2)}) async-start(bf16[8,16,128]{2,1,0:T(8,128)(2,1)} %copy.58), calls=%async_computation.4 | async-start | bytes 65536 | tf_op jit(solution)/shard_map/all_to_all | solution.py:112
  28.8 1.0 %copy-start.2 = (bf16[32,2048]{1,0:T(8,128)(2,1)S(1)}, bf16[32,2048]{1,0:T(8,128)(2,1)}, u32[]{:S(2)}) copy-start(bf16[32,2048]{1,0:T(8,128)(2,1)} %param.9) | copy-start | bytes 393220
  29.8 0.9 copy-start.3
  35.4 12.9 %all-to-all-start.1 = ((bf16[8,32,256]{2,1,0:T(8,128)(2,1)}), bf16[8,32,256]{2,1,0:T(8,128)(2,1)S(1)}, u32[]{:S(2)}, u32[]{:S(2)}) async-start(bf16[8,32,256]{2,1,0:T(8,128)(2,1)} %bitcast.75), calls=%async_computation.1 | async-start | bytes 262144 | tf_op jit(solution)/shard_map/all_to_all | solution.py:87
  48.3 10.7 %all-to-all-start = ((bf16[8,32,256]{2,1,0:T(8,128)(2,1)}), bf16[8,32,256]{2,1,0:T(8,128)(2,1)S(1)}, u32[]{:S(2)}, u32[]{:S(2)}) async-start(bf16[8,32,256]{2,1,0:T(8,128)(2,1)} %bitcast.78), calls=%async_computation | async-start | bytes 262144 | tf_op jit(solution)/shard_map/all_to_all | solution.py:79
  59.0 10.7 %all-to-all-start.2 = ((bf16[8,32,256]{2,1,0:T(8,128)(2,1)}), bf16[8,32,256]{2,1,0:T(8,128)(2,1)S(1)}, u32[]{:S(2)}, u32[]{:S(2)}) async-start(bf16[8,32,256]{2,1,0:T(8,128)(2,1)} %bitcast.77), calls=%async_computation.2 | async-start | bytes 262144 | tf_op jit(solution)/shard_map/all_to_all | solution.py:94
  69.7 10.0 %all-to-all-start.7 = ((bf16[8,2,1024]{2,1,0:T(2,128)(2,1)}), bf16[8,2,1024]{2,1,0:T(2,128)(2,1)S(1)}, u32[]{:S(2)}, u32[]{:S(2)}) async-start(bf16[8,2,1024]{2,1,0:T(2,128)(2,1)} %reshape.126), calls=%async_computation.7 | async-start | bytes 65536 | tf_op jit(solution)/shard_map/all_to_all | solution.py:140
  79.6 10.7 %all-to-all-start.3 = ((bf16[8,2,4096]{2,1,0:T(2,128)(2,1)}), bf16[8,2,4096]{2,1,0:T(2,128)(2,1)S(1)}, u32[]{:S(2)}, u32[]{:S(2)}) async-start(bf16[8,2,4096]{2,1,0:T(2,128)(2,1)} %reshape.124), calls=%async_computation.3 | async-start | bytes 262144 | tf_op jit(solution)/shard_map/all_to_all | solution.py:105
  83.6 0.9 copy-start.4
where the time goes:
time: 94.8 us; the launch traced here: 93.8 us
  waiting for transfers between devices  40.1 us (42%)
  starting transfers between devices  33.1 us (35%)
  local copies, waits for them, and re-layouts  9.24 us (10%)
  blocking collectives  6.74 us (7%)
  other arithmetic  2.51 us (3%)
  matrix products  1.3 us (1%)
    all_to_all x1, starting transfers between devices, shards(): lax.all_to_all(copy_heads(small_values, small_blocks, small_parts), 'seq'...  7.38 us
    all_to_all x1, waiting for transfers between devices, shards(): lax.all_to_all(copy_heads(big_keys, big_blocks, big_parts), 'seq', split_...  7.08 us
    all_to_all x1, waiting for transfers between devices, shards(): lax.all_to_all(copy_heads(big_values, big_blocks, big_parts), 'seq', spli...  6.9 us
    all_to_all x1, waiting for transfers between devices, shards(): lax.all_to_all(copy_heads(small_keys, small_blocks, small_parts), 'seq',...  6 us
    all_to_all x1, waiting for transfers between devices, shards(): lax.all_to_all(big_out[None], 'seq', split_axis=1, concat_axis=0, tiled=T...  5.59 us
    all_to_all x1, starting transfers between devices, shards(): lax.all_to_all(copy_heads(big_keys, big_blocks, big_parts), 'seq', split_...  5.57 us
    all_to_all x1, waiting for transfers between devices, shards(): lax.all_to_all(copy_heads(small_values, small_blocks, small_parts), 'seq'...  5.29 us
    unnamed x26, local copies, waits for them, and re-layouts  4.96 us
  transfers between devices with their start and end apart: 8, of which 8 were waited for; matrix products, arithmetic and copies ran while one was open for 10% of the time, Pallas kernels for 0%

commit v1 on v0

v1 whole, which is shorter than its diff:
```python
import functools
import math

import jax
import jax.numpy as jnp
from jax import lax
from jax.experimental import pallas as pl
from jax.experimental.pallas import tpu as pltpu
from jax.sharding import PartitionSpec as P

DH = 128
BF16 = jnp.bfloat16
F32 = jnp.float32
VMEM = pl.BlockSpec(memory_space=pltpu.VMEM)
SMEM = pl.BlockSpec(memory_space=pltpu.SMEM)
NT = (((1,), (1,)), ((), ()))


def row_layout(group, tokens, small_tokens):
    rows = {}
    at = 0
    for name, count in (
        ("q", group * tokens),
        ("k", group * tokens),
        ("vr", tokens),
        ("sq", small_tokens),
        ("sk", small_tokens),
        ("svr", small_tokens),
    ):
        rows[name] = at
        at += count
    rows["all"] = at
    return rows


def pack_kernel(n, group, bq, bk, bv, sq, sk, sv, br, sr, *outs):
    tokens, small_tokens = bq.shape[0], sq.shape[0]
    lat = br.shape[0]
    rows = row_layout(group, tokens, small_tokens)
    me = lax.axis_index("seq")
    for k in range(n):
        out = outs[k]
        dest = jnp.bitwise_xor(me, k)
        values = []
        for g in range(group):
            cols = pl.ds(pl.multiple_of((dest * group + g) * DH, DH), DH)
            out[pl.ds(rows["q"] + g * tokens, tokens), :] = bq[:, cols]
            out[pl.ds(rows["k"] + g * tokens, tokens), :] = bk[:, cols]
            values.append(
                lax.dot_general(bv[:, cols], br[:, cols], NT, preferred_element_type=F32)
            )
        out[pl.ds(rows["vr"], tokens), :] = jnp.concatenate(values, axis=1).astype(BF16)
        cols = pl.ds(pl.multiple_of(dest * DH, DH), DH)
        out[pl.ds(rows["sq"], small_tokens), :] = sq[:, cols]
        out[pl.ds(rows["sk"], small_tokens), :] = sk[:, cols]
        value = lax.dot_general(sv[:, cols], sr[:, cols], NT, preferred_element_type=F32)
        value = jnp.concatenate([value, jnp.zeros((small_tokens, DH - lat), F32)], axis=1)
        out[pl.ds(rows["svr"], small_tokens), :] = value.astype(BF16)


def gather_small_kernel(n, first, count, *refs):
    out = refs[n]
    for k in range(n):
        out[pl.ds(k * count, count), :] = refs[k][pl.ds(first, count), :]


def softmax_times(queries, keys, values):
    scores = lax.dot_general(queries, keys, NT, preferred_element_type=F32)
    scores = scores * (1.0 / math.sqrt(DH))
    probs = jnp.exp(scores - jnp.max(scores, axis=1, keepdims=True))
    totals = jnp.sum(probs, axis=1, keepdims=True)
    out = jnp.dot(probs.astype(BF16), values, preferred_element_type=F32)
    return out / totals


def big_kernel(n, group, tokens, lat, rows, *refs):
    blocks, out = refs[:n], refs[n]
    read = lambda first: jnp.concatenate([b[pl.ds(first, tokens), :] for b in blocks], axis=0)
    values = read(rows["vr"])
    total = None
    for g in range(group):
        part = softmax_times(
            read(rows["q"] + g * tokens),
            read(rows["k"] + g * tokens),
            values[:, g * lat : (g + 1) * lat],
        )
        total = part if total is None else total + part
    out[:, :] = total


def small_kernel(n, tokens, small_tokens, lat, rows, copies, *refs):
    blocks = refs[:n]
    own_kv, other_kv, big, guidance, out, latent = refs[n:]
    me, core = lax.axis_index("seq"), lax.axis_index("head")
    weight = guidance[0]
    queries = jnp.concatenate([b[pl.ds(rows["sq"], small_tokens), :] for b in blocks], axis=0)
    pick = lambda kv, first: [
        kv[pl.ds(k * 2 * small_tokens + first, small_tokens), :] for k in range(n)
    ]
    keys = jnp.concatenate(pick(own_kv, 0) + pick(other_kv, 0), axis=0)
    values = jnp.concatenate(
        pick(own_kv, small_tokens) + pick(other_kv, small_tokens), axis=0
    )
    small = softmax_times(queries, keys, values[:, :lat])
    latent[:, :lat] = (1.0 + weight) * big[:, :]
    for k in range(n):
        at = pl.multiple_of(k * tokens + core * small_tokens, small_tokens)
        here = pl.ds(at, small_tokens)
        latent[here, :lat] = (
            latent[here, :lat] - weight * small[k * small_tokens : (k + 1) * small_tokens, :]
        )
    for k in range(n):
        even = latent[pl.ds(k * tokens, tokens // 2, stride=2), :lat]
        odd = latent[pl.ds(k * tokens + 1, tokens // 2, stride=2), :lat]
        block = jnp.concatenate([even, odd], axis=1).astype(out.dtype)
        dest = jnp.bitwise_xor(me, k)
        for c in range(copies):
            out[dest * copies + c] = block


def sum_kernel(x, out):
    total = x[0].astype(F32)
    for i in range(1, x.shape[0]):
        total = total + x[i].astype(F32)
    out[:, :] = total


def call(kernel, out_shape, operands, specs=None, scratch=(), cost=None):
    single = not isinstance(out_shape, (list, tuple))
    return pl.pallas_call(
        kernel,
        out_shape=out_shape,
        in_specs=specs if specs is not None else [VMEM] * len(operands),
        out_specs=VMEM if single else [VMEM] * len(out_shape),
        scratch_shapes=list(scratch),
        cost_estimate=cost,
        compiler_params=pltpu.CompilerParams(vmem_limit_bytes=32 * 1024 * 1024),
    )(*operands)


def exchange_shards(bq, bk, bv, sq, sk, sv, br, sr, guidance):
    n, cores = lax.axis_size("seq"), lax.axis_size("head")
    tokens, small_tokens = bq.shape[0], sq.shape[0]
    group = bq.shape[1] // DH // n
    lat = br.shape[1]
    rows = row_layout(group, tokens, small_tokens)
    block = jax.ShapeDtypeStruct((rows["all"], DH), BF16)
    sent = call(
        functools.partial(pack_kernel, n, group),
        [block] * n,
        (bq, bk, bv, sq, sk, sv, br.T, sr.T),
    )
    blocks = [sent[0]] + [None] * (n - 1)
    for k in range(n - 1, 0, -1):
        blocks[k] = lax.ppermute(sent[k], "seq", [(j, j ^ k) for j in range(n)])
    own_kv = call(
        functools.partial(gather_small_kernel, n, rows["sk"], 2 * small_tokens),
        jax.ShapeDtypeStruct((n * 2 * small_tokens, DH), BF16),
        blocks,
    )
    other_kv = lax.ppermute(own_kv, "head", [(c, c ^ 1) for c in range(cores)])
    big = call(
        functools.partial(big_kernel, n, group, tokens, lat, rows),
        jax.ShapeDtypeStruct((n * tokens, lat), F32),
        blocks,
        cost=pl.CostEstimate(flops=10**9, bytes_accessed=10**6, transcendentals=10**5),
    )
    partial = call(
        functools.partial(small_kernel, n, tokens, small_tokens, lat, rows, cores),
        jax.ShapeDtypeStruct((n * cores, tokens // 2, 2 * lat), BF16),
        (*blocks, own_kv, other_kv, big, guidance),
        specs=[VMEM] * (n + 3) + [SMEM],
        scratch=[pltpu.VMEM((n * tokens, DH), F32)],
    )
    terms = lax.all_to_all(partial, ("seq", "head"), split_axis=0, concat_axis=0, tiled=True)
    return call(
        sum_kernel, jax.ShapeDtypeStruct((tokens // 2, 2 * lat), F32), (terms,)
    )


def fits_exchange(mesh, bq, sq, br):
    groups, n, cores = mesh.shape["groups"], mesh.shape["seq"], mesh.shape["head"]
    tokens = bq.shape[0] // (groups * n)
    small_tokens = sq.shape[0] // (groups * n * cores)
    big_heads, small_heads = bq.shape[1] // DH // cores, sq.shape[1] // DH
    lat = br.shape[1]
    return (
        cores == 2
        and n & (n - 1) == 0
        and small_heads == n
        and big_heads % n == 0
        and big_heads // n * lat == DH
        and 2 * lat == DH
        and tokens % 32 == 0
        and small_tokens % 16 == 0
        and n * tokens <= 1024
    )


def split_heads(matrix, blocks, parts):
    rows_here, columns = matrix.shape
    shaped = matrix.reshape(blocks, rows_here // blocks, parts, columns // parts)
    shaped = jnp.transpose(shaped, (0, 2, 1, 3))
    return shaped.reshape(blocks * parts, rows_here // blocks, columns // parts)


def copy_heads(matrix, blocks, parts):
    rows_here, columns = matrix.shape
    shaped = jnp.transpose(matrix.reshape(rows_here, parts, columns // parts), (1, 0, 2))
    shaped = jnp.broadcast_to(shaped[None], (blocks, parts, rows_here, columns // parts))
    return shaped.reshape(blocks * parts, rows_here, columns // parts)


def join_heads(stacked, blocks, parts):
    pieces, rows_here, columns = stacked.shape
    shaped = stacked.reshape(blocks, parts, rows_here, columns)
    shaped = jnp.transpose(shaped, (0, 2, 1, 3))
    return shaped.reshape(blocks * rows_here, parts * columns)


def attend(query_rows, key_rows, value_rows):
    query_count = query_rows.shape[0]
    heads_here = query_rows.shape[1] // DH
    key_count = key_rows.shape[0]
    block_height = math.gcd(query_count, 256)
    block_count = query_count // block_height
    query_blocks = query_rows.reshape(block_count, block_height, heads_here, DH)
    key_split = key_rows.reshape(key_count, heads_here, DH)
    value_split = value_rows.reshape(key_count, heads_here, DH)
    score_scale = 1.0 / math.sqrt(DH)

    def one_block(query_block):
        scores = (
            jnp.einsum("qgd,kgd->gqk", query_block, key_split, preferred_element_type=F32)
            * score_scale
        )
        row_max = jnp.max(scores, axis=2, keepdims=True)
        probs = jnp.exp(scores - row_max)
        totals = jnp.sum(probs, axis=2, keepdims=True)
        weights = probs.astype(BF16)
        accumulated = jnp.einsum(
            "gqk,kgd->gqd", weights, value_split, preferred_element_type=F32
        )
        attended = accumulated / totals
        attended = jnp.transpose(attended, (1, 0, 2)).reshape(block_height, heads_here * DH)
        return attended.astype(BF16)

    outputs = lax.map(one_block, query_blocks)
    return outputs.reshape(query_count, heads_here * DH)


def seq_exchange(stacked, split, concat):
    return lax.all_to_all(stacked, "seq", split_axis=split, concat_axis=concat, tiled=True)


def run_model(queries, keys, values, shared):
    seq_count = lax.axis_size("seq")
    heads = queries.shape[1] // DH
    blocks = max(seq_count // heads, 1)
    parts = heads // max(heads // seq_count, 1)
    query_rows = seq_exchange(split_heads(queries, blocks, parts), 0, 1)[0]
    key_rows = seq_exchange(copy_heads(keys, blocks, parts), 0, 1)[0]
    value_rows = seq_exchange(copy_heads(values, blocks, parts), 0, 1)[0]
    if shared:
        key_rows = lax.all_gather(key_rows, "head", axis=0, tiled=True)
        value_rows = lax.all_gather(value_rows, "head", axis=0, tiled=True)
    out = attend(query_rows, key_rows, value_rows)
    return join_heads(seq_exchange(out[None], 1, 0), blocks, parts)


def general_shards(bq, bk, bv, sq, sk, sv, br, sr, guidance):
    big_attention = run_model(bq, bk, bv, False)
    big_partial = jnp.dot(big_attention, br, preferred_element_type=F32)
    small_attention = run_model(sq, sk, sv, True)
    small_latent = jnp.dot(small_attention, sr, preferred_element_type=F32)
    weight_value = guidance[0]
    core_index = lax.axis_index("head")
    placed = lax.dynamic_update_slice(
        jnp.zeros_like(big_partial),
        small_latent,
        (core_index * small_latent.shape[0], jnp.zeros((), jnp.int32)),
    )
    blended = lax.psum((1.0 + weight_value) * big_partial - weight_value * placed, "head")
    return blended.reshape(blended.shape[0] // 2, 2 * blended.shape[1])


def solution(mesh):
    placed = (
        P(("groups", "seq"), "head"),
        P(("groups", "seq"), "head"),
        P(("groups", "seq"), "head"),
        P(("groups", "seq", "head"), None),
        P(("groups", "seq", "head"), None),
        P(("groups", "seq", "head"), None),
        P("head", None),
        P(),
        P("groups"),
    )

    def whole(*arrays):
        fits = fits_exchange(mesh, arrays[0], arrays[3], arrays[6])
        return jax.shard_map(
            exchange_shards if fits else general_shards,
            mesh=mesh,
            in_specs=placed,
            out_specs=P(("groups", "seq"), None),
            check_vma=False,
        )(*arrays)

    return whole
```

time: 94.8 us -> 38.8 us (0.41)
  waiting for transfers between devices: 40.1 us -> 6.65 us
  starting transfers between devices: 33.1 us -> 12.5 us
  blocking collectives: 6.74 us -> 9.48 us
  other arithmetic: 2.51 us -> 0 us
  local copies, waits for them, and re-layouts: 9.24 us -> 6.84 us
  Pallas kernels: 0 us -> 2.22 us
  matrix products: 1.3 us -> 0 us
    all_to_all x8 -> x0, waiting for transfers between devices: 40.1 us -> none  [the longest x1 7.08 us: shards(): lax.all_to_all(copy_heads(big_keys, big_blocks, big_parts), 'seq', split_...]
    all_to_all x8 -> x0, starting transfers between devices: 33.1 us -> none  [the longest x1 7.38 us: shards(): lax.all_to_all(copy_heads(small_values, small_blocks, small_parts), 'seq'...]
    ppermute x0 -> x8, starting transfers between devices: none -> 12.5 us  [the longest x7 12.5 us: exchange_shards(): blocks[k] = lax.ppermute(sent[k], 'seq', [(j, j ^ k) for j in range(n)])]
    all_to_all x0 -> x1, blocking collectives: none -> 9.48 us  [exchange_shards(): lax.all_to_all(partial, ('seq', 'head'), split_axis=0, concat_axis=0, til...]
    ppermute x0 -> x8, waiting for transfers between devices: none -> 6.65 us  [the longest x7 6.13 us: exchange_shards(): blocks[k] = lax.ppermute(sent[k], 'seq', [(j, j ^ k) for j in range(n)])]
    all_gather x2 -> x0, blocking collectives: 3.68 us -> none  [the longest x1 1.84 us: shards(): lax.all_gather(key_copies[0], 'head', axis=0, tiled=True)]
    psum x1 -> x0, blocking collectives: 3.06 us -> none  [shards(): lax.psum((1.0 + weight_value) * big_partial - weight_value * placed, 'head')]
    reshape x6 -> x0, local copies, waits for them, and re-layouts: 2.69 us -> none  [the longest x2 1.32 us: copy_heads(): matrix.reshape(rows_here, parts, columns // parts)]
  transfers between devices with their start and end apart: 8 -> 8, of which waited for: 8 -> 3; matrix products, arithmetic and copies ran while one was open for 10% -> 0% of each run, Pallas kernels for 0% -> 2%
where the time goes in v1:
time: 38.8 us; the launch traced here: 38.4 us
  starting transfers between devices  12.5 us (32%)
  blocking collectives  9.48 us (24%)
  local copies, waits for them, and re-layouts  6.84 us (18%)
  waiting for transfers between devices  6.65 us (17%)
  Pallas kernels  2.22 us (6%)
  between operations  0.7 us (2%)
    ppermute x7, starting transfers between devices, exchange_shards(): blocks[k] = lax.ppermute(sent[k], 'seq', [(j, j ^ k) for j in range(n)])  12.5 us
    all_to_all x1, blocking collectives, exchange_shards(): lax.all_to_all(partial, ('seq', 'head'), split_axis=0, concat_axis=0, til...  9.48 us
    unnamed x16, local copies, waits for them, and re-layouts  6.84 us
    ppermute x7, waiting for transfers between devices, exchange_shards(): blocks[k] = lax.ppermute(sent[k], 'seq', [(j, j ^ k) for j in range(n)])  6.13 us
    pallas_call x5, Pallas kernels, call(): pl.pallas_call(kernel, out_shape=out_shape, in_specs=specs if specs is no...  2.22 us
  transfers between devices with their start and end apart: 8, of which 3 were waited for; matrix products, arithmetic and copies ran while one was open for 0% of the time, Pallas kernels for 2%

profile of v1, /device:TPU:0, one launch (start us, length us, event | category | flops | bytes accessed | tf_op | source)
XLA Modules:
  0.0 38.4 jit_solution(4744269353086274103)
XLA Ops:
  0.0 0.0 copy-start
  0.0 0.9 %copy-done = bf16[2048,64]{0,1:T(8,128)(2,1)S(1)} copy-done((bf16[2048,64]{0,1:T(8,128)(2,1)S(1)}, bf16[2048,64]{0,1:T(8,128)(2,1)}, u32[]{:S(2)}) %copy-start) | copy-done | bytes 262168
  1.0 0.0 copy-start.1
  1.0 0.9 %copy-done.1 = bf16[32,2048]{1,0:T(8,128)(2,1)S(1)} copy-done((bf16[32,2048]{1,0:T(8,128)(2,1)S(1)}, bf16[32,2048]{1,0:T(8,128)(2,1)}, u32[]{:S(2)}) %copy-start.1) | copy-done | bytes 131096
  1.9 0.0 copy-start.2
  1.9 0.9 %copy-done.2 = bf16[32,2048]{1,0:T(8,128)(2,1)S(1)} copy-done((bf16[32,2048]{1,0:T(8,128)(2,1)S(1)}, bf16[32,2048]{1,0:T(8,128)(2,1)}, u32[]{:S(2)}) %copy-start.2) | copy-done | bytes 131096
  2.8 0.0 copy-start.3
  2.8 0.9 %copy-done.3 = bf16[32,2048]{1,0:T(8,128)(2,1)S(1)} copy-done((bf16[32,2048]{1,0:T(8,128)(2,1)S(1)}, bf16[32,2048]{1,0:T(8,128)(2,1)}, u32[]{:S(2)}) %copy-start.3) | copy-done | bytes 131096
  3.7 0.0 copy-start.4
  3.7 0.9 %copy-done.4 = bf16[1024,64]{0,1:T(8,128)(2,1)S(1)} copy-done((bf16[1024,64]{0,1:T(8,128)(2,1)S(1)}, bf16[1024,64]{0,1:T(8,128)(2,1)}, u32[]{:S(2)}) %copy-start.4) | copy-done | bytes 131096
  4.6 0.0 copy-start.5
  4.6 0.8 %copy-done.5 = bf16[16,1024]{1,0:T(8,128)(2,1)S(1)} copy-done((bf16[16,1024]{1,0:T(8,128)(2,1)S(1)}, bf16[16,1024]{1,0:T(8,128)(2,1)}, u32[]{:S(2)}) %copy-start.5) | copy-done | bytes 32792
  5.3 0.0 copy-start.6
  5.3 0.8 %copy-done.6 = bf16[16,1024]{1,0:T(8,128)(2,1)S(1)} copy-done((bf16[16,1024]{1,0:T(8,128)(2,1)S(1)}, bf16[16,1024]{1,0:T(8,128)(2,1)}, u32[]{:S(2)}) %copy-start.6) | copy-done | bytes 32792
  6.1 0.0 copy-start.7
  6.1 0.8 %copy-done.7 = bf16[16,1024]{1,0:T(8,128)(2,1)S(1)} copy-done((bf16[16,1024]{1,0:T(8,128)(2,1)S(1)}, bf16[16,1024]{1,0:T(8,128)(2,1)}, u32[]{:S(2)}) %copy-start.7) | copy-done | bytes 32792
  6.8 0.4 %shard_map.91 = (bf16[208,128]{1,0:T(8,128)(2,1)S(1)}, bf16[208,128]{1,0:T(8,128)(2,1)S(1)}, bf16[208,128]{1,0:T(8,128)(2,1)S(1)}, bf16[208,128]{1,0:T(8,128)(2,...) custom-call(bf16[32,2048]{1,0:T(8,128)(2,1)S(1)} %copy-done.1, ...), custom_call_target="tpu_custom_call" | custom-call | tf_op jit(solution)/shard_map/pallas_call | solution.py:130
  7.3 3.0 %collective-permute-start = (bf16[208,128]{1,0:T(8,128)(2,1)S(1)}, bf16[208,128]{1,0:T(8,128)(2,1)S(1)}, u32[]{:S(2)}, u32[]{:S(2)}) collective-permute-start(bf16[208,128]{1,0:T(8,128)(2,1)S(1)} %get-tuple-element.14), channel_id=1, source_target_pairs={{0,2},{2,0},{4,6},{6,4},{8,10},{10,8},{12,14},{14,12},{1,3},{3,1},... | collective-permute-start | bytes 159752 | tf_op jit(solution)/shard_map/ppermute | solution.py:155
  10.2 1.6 %collective-permute-start.1 = (bf16[208,128]{1,0:T(8,128)(2,1)S(1)}, bf16[208,128]{1,0:T(8,128)(2,1)S(1)}, u32[]{:S(2)}, u32[]{:S(2)}) collective-permute-start(bf16[208,128]{1,0:T(8,128)(2,1)S(1)} %get-tuple-element.15), channel_id=1, source_target_pairs={{0,4},{2,6},{4,0},{6,2},{8,12},{10,14},{12,8},{14,10},{1,5},{3,7},... | collective-permute-start | bytes 159752 | tf_op jit(solution)/shard_map/ppermute | solution.py:155
  11.8 0.0 collective-permute-start.2
  11.8 3.0 %collective-permute-start.3 = (bf16[208,128]{1,0:T(8,128)(2,1)S(1)}, bf16[208,128]{1,0:T(8,128)(2,1)S(1)}, u32[]{:S(2)}, u32[]{:S(2)}) collective-permute-start(bf16[208,128]{1,0:T(8,128)(2,1)S(1)} %get-tuple-element.17), channel_id=1, source_target_pairs={{0,8},{2,10},{4,12},{6,14},{8,0},{10,2},{12,4},{14,6},{1,9},{3,11}... | collective-permute-start | bytes 159752 | tf_op jit(solution)/shard_map/ppermute | solution.py:155
  14.8 1.3 %collective-permute-start.4 = (bf16[208,128]{1,0:T(8,128)(2,1)S(1)}, bf16[208,128]{1,0:T(8,128)(2,1)S(1)}, u32[]{:S(2)}, u32[]{:S(2)}) collective-permute-start(bf16[208,128]{1,0:T(8,128)(2,1)S(1)} %get-tuple-element.18), channel_id=1, source_target_pairs={{0,10},{2,8},{4,14},{6,12},{8,2},{10,0},{12,6},{14,4},{1,11},{3,9}... | collective-permute-start | bytes 159752 | tf_op jit(solution)/shard_map/ppermute | solution.py:155
  16.1 0.0 collective-permute-done.refs_1_
  16.1 3.6 %collective-permute-start.5 = (bf16[208,128]{1,0:T(8,128)(2,1)S(1)}, bf16[208,128]{1,0:T(8,128)(2,1)S(1)}, u32[]{:S(2)}, u32[]{:S(2)}) collective-permute-start(bf16[208,128]{1,0:T(8,128)(2,1)S(1)} %get-tuple-element.19), channel_id=1, source_target_pairs={{0,12},{2,14},{4,8},{6,10},{8,4},{10,6},{12,0},{14,2},{1,13},{3,15... | collective-permute-start | bytes 159752 | tf_op jit(solution)/shard_map/ppermute | solution.py:155
  19.7 0.0 collective-permute-done.1.refs_2_
  19.7 0.0 collective-permute-start.6
  20.4 0.0 collective-permute-done.2.refs_3_
  20.4 0.0 collective-permute-done.3.refs_4_
  20.4 2.6 %collective-permute-done.4.refs_5_ = bf16[208,128]{1,0:T(8,128)(2,1)S(1)} collective-permute-done((bf16[208,128]{1,0:T(8,128)(2,1)S(1)}, bf16[208,128]{1,0:T(8,128)(2,1)S(1)}, u32[]{:S(2)}, u32[]{:S(2)}) %collective-permute-start.4) | collective-permute-done | bytes 53280 | tf_op jit(solution)/shard_map/ppermute | solution.py:155
  23.0 0.0 collective-permute-done.5.refs_6_
  23.0 3.5 %collective-permute-done.6.refs_7_ = bf16[208,128]{1,0:T(8,128)(2,1)S(1)} collective-permute-done((bf16[208,128]{1,0:T(8,128)(2,1)S(1)}, bf16[208,128]{1,0:T(8,128)(2,1)S(1)}, u32[]{:S(2)}, u32[]{:S(2)}) %collective-permute-start.6) | collective-permute-done | bytes 53280 | tf_op jit(solution)/shard_map/ppermute | solution.py:155
  26.5 0.0 collective-permute-start.7
  26.6 0.7 %shard_map.93.refs_10_ = f32[256,64]{1,0:T(8,128)S(1)} custom-call(bf16[208,128]{1,0:T(8,128)(2,1)S(1)} %get-tuple-element.13.refs_0_, bf16[208,128]{1,0:T(8,128)(2,1)S(1)} %collective-permute-done.refs_1_, bf16[208,128]{1,0:T(8,128)(2,1)S(1)} %collective-permute-done.1.refs_2_, bf16[208,128]{1,0:T(8,128)(2,1)S(1)} %collective-permute-done.2.refs_3_, ...), custom_call_target="tpu_custom_call" | custom-call | flops 1000000000 | bytes 1000000 | tf_op jit(solution)/shard_map/pallas_call | solution.py:130
  27.3 0.5 %collective-permute-done.7.refs_9_ = bf16[256,128]{1,0:T(8,128)(2,1)S(1)} collective-permute-done((bf16[256,128]{1,0:T(8,128)(2,1)S(1)}, bf16[256,128]{1,0:T(8,128)(2,1)S(1)}, u32[]{:S(2)}, u32[]{:S(2)}) %collective-permute-start.7) | collective-permute-done | bytes 65568 | tf_op jit(solution)/shard_map/ppermute | solution.py:161
  27.8 0.5 %shard_map.94 = bf16[16,16,128]{2,1,0:T(8,128)(2,1)S(1)} custom-call(bf16[208,128]{1,0:T(8,128)(2,1)S(1)} %get-tuple-element.13.refs_0_, bf16[208,128]{1,0:T(8,128)(2,1)S(1)} %collective-permute-done.refs_1_, bf16[208,128]{1,0:T(8,128)(2,1)S(1)} %collective-permute-done.1.refs_2_, bf16[208,128]{1,0:T(8,128)(2,1)S(1)} %collective-permute-done.2.refs_3_, ...), custom_call_target="tpu_custom_call" | custom-call | tf_op jit(solution)/shard_map/pallas_call | solution.py:130
  28.3 9.5 %all_to_all.5.x = bf16[16,16,128]{2,1,0:T(8,128)(2,1)S(1)} all-to-all(bf16[16,16,128]{2,1,0:T(8,128)(2,1)S(1)} %shard_map.94), channel_id=1, replica_groups=mesh['groups'=2,'seq'=8,'head'=2] {'seq','head'}, dimensions={0} | all-to-all | bytes 131072 | tf_op jit(solution)/shard_map/all_to_all | solution.py:175
  37.7 0.6 %shard_map.95 = f32[16,128]{1,0:T(8,128)} custom-call(bf16[16,16,128]{2,1,0:T(8,128)(2,1)S(1)} %all_to_all.5.x), custom_call_target="tpu_custom_call" | custom-call | tf_op jit(solution)/shard_map/pallas_call | solution.py:130
  (1 shorter events, 0.0 us)
Async XLA Ops:
  0.0 0.9 %copy-start = (bf16[2048,64]{0,1:T(8,128)(2,1)S(1)}, bf16[2048,64]{0,1:T(8,128)(2,1)}, u32[]{:S(2)}) copy-start(bf16[2048,64]{0,1:T(8,128)(2,1)} %param.15) | copy-start | bytes 786436
  1.0 0.9 %copy-start.1 = (bf16[32,2048]{1,0:T(8,128)(2,1)S(1)}, bf16[32,2048]{1,0:T(8,128)(2,1)}, u32[]{:S(2)}) copy-start(bf16[32,2048]{1,0:T(8,128)(2,1)} %bq.1) | copy-start | bytes 393220
  1.9 0.9 %copy-start.2 = (bf16[32,2048]{1,0:T(8,128)(2,1)S(1)}, bf16[32,2048]{1,0:T(8,128)(2,1)}, u32[]{:S(2)}) copy-start(bf16[32,2048]{1,0:T(8,128)(2,1)} %bk.1) | copy-start | bytes 393220
  2.8 0.9 %copy-start.3 = (bf16[32,2048]{1,0:T(8,128)(2,1)S(1)}, bf16[32,2048]{1,0:T(8,128)(2,1)}, u32[]{:S(2)}) copy-start(bf16[32,2048]{1,0:T(8,128)(2,1)} %bv.1) | copy-start | bytes 393220
  3.7 0.9 %copy-start.4 = (bf16[1024,64]{0,1:T(8,128)(2,1)S(1)}, bf16[1024,64]{0,1:T(8,128)(2,1)}, u32[]{:S(2)}) copy-start(bf16[1024,64]{0,1:T(8,128)(2,1)} %param.16) | copy-start | bytes 393220
  4.6 0.8 %copy-start.5 = (bf16[16,1024]{1,0:T(8,128)(2,1)S(1)}, bf16[16,1024]{1,0:T(8,128)(2,1)}, u32[]{:S(2)}) copy-start(bf16[16,1024]{1,0:T(8,128)(2,1)} %sq.1) | copy-start | bytes 98308
  5.3 0.8 %copy-start.6 = (bf16[16,1024]{1,0:T(8,128)(2,1)S(1)}, bf16[16,1024]{1,0:T(8,128)(2,1)}, u32[]{:S(2)}) copy-start(bf16[16,1024]{1,0:T(8,128)(2,1)} %sk.1) | copy-start | bytes 98308
  6.1 0.8 %copy-start.7 = (bf16[16,1024]{1,0:T(8,128)(2,1)S(1)}, bf16[16,1024]{1,0:T(8,128)(2,1)}, u32[]{:S(2)}) copy-start(bf16[16,1024]{1,0:T(8,128)(2,1)} %sv.1) | copy-start | bytes 98308
  7.3 8.8 %collective-permute-start = (bf16[208,128]{1,0:T(8,128)(2,1)S(1)}, bf16[208,128]{1,0:T(8,128)(2,1)S(1)}, u32[]{:S(2)}, u32[]{:S(2)}) collective-permute-start(bf16[208,128]{1,0:T(8,128)(2,1)S(1)} %get-tuple-element.14), channel_id=1, source_target_pairs={{0,2},{2,0},{4,6},{6,4},{8,10},{10,8},{12,14},{14,12},{1,3},{3,1},... | collective-permute-start | bytes 159752 | tf_op jit(solution)/shard_map/ppermute | solution.py:155
  10.2 9.5 %collective-permute-start.1 = (bf16[208,128]{1,0:T(8,128)(2,1)S(1)}, bf16[208,128]{1,0:T(8,128)(2,1)S(1)}, u32[]{:S(2)}, u32[]{:S(2)}) collective-permute-start(bf16[208,128]{1,0:T(8,128)(2,1)S(1)} %get-tuple-element.15), channel_id=1, source_target_pairs={{0,4},{2,6},{4,0},{6,2},{8,12},{10,14},{12,8},{14,10},{1,5},{3,7},... | collective-permute-start | bytes 159752 | tf_op jit(solution)/shard_map/ppermute | solution.py:155
  11.8 8.6 %collective-permute-start.2 = (bf16[208,128]{1,0:T(8,128)(2,1)S(1)}, bf16[208,128]{1,0:T(8,128)(2,1)S(1)}, u32[]{:S(2)}, u32[]{:S(2)}) collective-permute-start(bf16[208,128]{1,0:T(8,128)(2,1)S(1)} %get-tuple-element.16), channel_id=1, source_target_pairs={{0,6},{2,4},{4,2},{6,0},{8,14},{10,12},{12,10},{14,8},{1,7},{3,5},... | collective-permute-start | bytes 159752 | tf_op jit(solution)/shard_map/ppermute | solution.py:155
  11.8 8.6 %collective-permute-start.3 = (bf16[208,128]{1,0:T(8,128)(2,1)S(1)}, bf16[208,128]{1,0:T(8,128)(2,1)S(1)}, u32[]{:S(2)}, u32[]{:S(2)}) collective-permute-start(bf16[208,128]{1,0:T(8,128)(2,1)S(1)} %get-tuple-element.17), channel_id=1, source_target_pairs={{0,8},{2,10},{4,12},{6,14},{8,0},{10,2},{12,4},{14,6},{1,9},{3,11}... | collective-permute-start | bytes 159752 | tf_op jit(solution)/shard_map/ppermute | solution.py:155
  14.8 8.2 %collective-permute-start.4 = (bf16[208,128]{1,0:T(8,128)(2,1)S(1)}, bf16[208,128]{1,0:T(8,128)(2,1)S(1)}, u32[]{:S(2)}, u32[]{:S(2)}) collective-permute-start(bf16[208,128]{1,0:T(8,128)(2,1)S(1)} %get-tuple-element.18), channel_id=1, source_target_pairs={{0,10},{2,8},{4,14},{6,12},{8,2},{10,0},{12,6},{14,4},{1,11},{3,9}... | collective-permute-start | bytes 159752 | tf_op jit(solution)/shard_map/ppermute | solution.py:155
  16.1 6.9 %collective-permute-start.5 = (bf16[208,128]{1,0:T(8,128)(2,1)S(1)}, bf16[208,128]{1,0:T(8,128)(2,1)S(1)}, u32[]{:S(2)}, u32[]{:S(2)}) collective-permute-start(bf16[208,128]{1,0:T(8,128)(2,1)S(1)} %get-tuple-element.19), channel_id=1, source_target_pairs={{0,12},{2,14},{4,8},{6,10},{8,4},{10,6},{12,0},{14,2},{1,13},{3,15... | collective-permute-start | bytes 159752 | tf_op jit(solution)/shard_map/ppermute | solution.py:155
  19.7 6.8 %collective-permute-start.6 = (bf16[208,128]{1,0:T(8,128)(2,1)S(1)}, bf16[208,128]{1,0:T(8,128)(2,1)S(1)}, u32[]{:S(2)}, u32[]{:S(2)}) collective-permute-start(bf16[208,128]{1,0:T(8,128)(2,1)S(1)} %get-tuple-element.20), channel_id=1, source_target_pairs={{0,14},{2,12},{4,10},{6,8},{8,6},{10,4},{12,2},{14,0},{1,15},{3,13... | collective-permute-start | bytes 159752 | tf_op jit(solution)/shard_map/ppermute | solution.py:155
  26.5 1.3 %collective-permute-start.7 = (bf16[256,128]{1,0:T(8,128)(2,1)S(1)}, bf16[256,128]{1,0:T(8,128)(2,1)S(1)}, u32[]{:S(2)}, u32[]{:S(2)}) collective-permute-start(bf16[256,128]{1,0:T(8,128)(2,1)S(1)} %shard_map.92.refs_8_), channel_id=1, source_target_pairs={{0,1},{1,0},{2,3},{3,2},{4,5},{5,4},{6,7},{7,6},{8,9},{9,8},{10,11... | collective-permute-start | bytes 196616 | tf_op jit(solution)/shard_map/ppermute | solution.py:161

commit v2 on v1

--- a/solution.py
+++ b/solution.py
@@ -33,7 +33,14 @@
     return rows
 
 
-def pack_kernel(n, group, bq, bk, bv, sq, sk, sv, br, sr, *outs):
+def pack_kernel(n, group, *refs):
+    sources, outs, held, done = refs[:8], refs[8 : 8 + n], refs[8 + n : 16 + n], refs[16 + n]
+    copies = [pltpu.make_async_copy(sources[i], held[i], done.at[i]) for i in range(8)]
+    for copy in copies:
+        copy.start()
+    for copy in copies:
+        copy.wait()
+    bq, bk, bv, sq, sk, sv, br, sr = held
     tokens, small_tokens = bq.shape[0], sq.shape[0]
     lat = br.shape[0]
     rows = row_layout(group, tokens, small_tokens)
@@ -58,6 +65,10 @@
         out[pl.ds(rows["svr"], small_tokens), :] = value.astype(BF16)
 
 
+def hop_order(n):
+    return [0] + list(range(n - 1, 0, -1))
+
+
 def gather_small_kernel(n, first, count, *refs):
     out = refs[n]
     for k in range(n):
@@ -113,7 +124,7 @@
         even = latent[pl.ds(k * tokens, tokens // 2, stride=2), :lat]
         odd = latent[pl.ds(k * tokens + 1, tokens // 2, stride=2), :lat]
         block = jnp.concatenate([even, odd], axis=1).astype(out.dtype)
-        dest = jnp.bitwise_xor(me, k)
+        dest = jnp.bitwise_xor(me, hop_order(n)[k])
         for c in range(copies):
             out[dest * copies + c] = block
 
@@ -125,7 +136,7 @@
     out[:, :] = total
 
 
-def call(kernel, out_shape, operands, specs=None, scratch=(), cost=None):
+def call(kernel, out_shape, operands, specs=None, scratch=(), cost=None, vmem=16):
     single = not isinstance(out_shape, (list, tuple))
     return pl.pallas_call(
         kernel,
@@ -134,7 +145,7 @@
         out_specs=VMEM if single else [VMEM] * len(out_shape),
         scratch_shapes=list(scratch),
         cost_estimate=cost,
-        compiler_params=pltpu.CompilerParams(vmem_limit_bytes=32 * 1024 * 1024),
+        compiler_params=pltpu.CompilerParams(vmem_limit_bytes=int(vmem * 2**20)),
     )(*operands)
 
 
@@ -145,14 +156,22 @@
     lat = br.shape[1]
     rows = row_layout(group, tokens, small_tokens)
     block = jax.ShapeDtypeStruct((rows["all"], DH), BF16)
+    sources = [
+        pltpu.with_memory_space_constraint(a, pltpu.HBM)
+        for a in (bq, bk, bv, sq, sk, sv, br.T, sr.T)
+    ]
     sent = call(
         functools.partial(pack_kernel, n, group),
         [block] * n,
-        (bq, bk, bv, sq, sk, sv, br.T, sr.T),
-    )
-    blocks = [sent[0]] + [None] * (n - 1)
-    for k in range(n - 1, 0, -1):
-        blocks[k] = lax.ppermute(sent[k], "seq", [(j, j ^ k) for j in range(n)])
+        sources,
+        specs=[pl.BlockSpec(memory_space=pltpu.HBM)] * len(sources),
+        scratch=[pltpu.VMEM(a.shape, a.dtype) for a in sources]
+        + [pltpu.SemaphoreType.DMA((len(sources),))],
+    )
+    hops = hop_order(n)
+    blocks = [sent[0]]
+    for k in hops[1:]:
+        blocks.append(lax.ppermute(sent[k], "seq", [(j, j ^ k) for j in range(n)]))
     own_kv = call(
         functools.partial(gather_small_kernel, n, rows["sk"], 2 * small_tokens),
         jax.ShapeDtypeStruct((n * 2 * small_tokens, DH), BF16),

time: 38.8 us -> 32.4 us (0.84)
  local copies, waits for them, and re-layouts: 6.84 us -> 0 us
  waiting for transfers between devices: 6.65 us -> 3.58 us
  blocking collectives: 9.48 us -> 11.9 us
  Pallas kernels: 2.22 us -> 3.53 us
    unnamed x16 -> x0, local copies, waits for them, and re-layouts: 6.84 us -> none
    ppermute x7, waiting for transfers between devices: 6.13 us -> 3.06 us  [exchange_shards(): blocks.append(lax.ppermute(sent[k], 'seq', [(j, j ^ k) for j in range(n)]))]
    all_to_all x1, blocking collectives: 9.48 us -> 11.9 us  [exchange_shards(): lax.all_to_all(partial, ('seq', 'head'), split_axis=0, concat_axis=0, til...]
    pallas_call x5, Pallas kernels: 2.22 us -> 3.53 us  [call(): pl.pallas_call(kernel, out_shape=out_shape, in_specs=specs if specs is no...]
  transfers between devices with their start and end apart: 8 -> 8, of which waited for: 3 -> 6; matrix products, arithmetic and copies ran while one was open for 0% -> 0% of each run, Pallas kernels for 2% -> 2%
where the time goes in v2:
time: 32.4 us; the launch traced here: 32.2 us
  starting transfers between devices  12.5 us (39%)
  blocking collectives  11.9 us (37%)
  waiting for transfers between devices  3.58 us (11%)
  Pallas kernels  3.53 us (11%)
  between operations  0.68 us (2%)
    ppermute x7, starting transfers between devices, exchange_shards(): blocks.append(lax.ppermute(sent[k], 'seq', [(j, j ^ k) for j in range(n)]))  12.5 us
    all_to_all x1, blocking collectives, exchange_shards(): lax.all_to_all(partial, ('seq', 'head'), split_axis=0, concat_axis=0, til...  11.9 us
    pallas_call x5, Pallas kernels, call(): pl.pallas_call(kernel, out_shape=out_shape, in_specs=specs if specs is no...  3.53 us
    ppermute x7, waiting for transfers between devices, exchange_shards(): blocks.append(lax.ppermute(sent[k], 'seq', [(j, j ^ k) for j in range(n)]))  3.06 us
  transfers between devices with their start and end apart: 8, of which 6 were waited for; matrix products, arithmetic and copies ran while one was open for 0% of the time, Pallas kernels for 2%

profile of v2, /device:TPU:0, one launch (start us, length us, event | category | flops | bytes accessed | tf_op | source)
XLA Modules:
  0.0 32.2 jit_solution(8988170834018627657)
XLA Ops:
  0.0 1.7 %shard_map.91 = (bf16[208,128]{1,0:T(8,128)(2,1)S(1)}, bf16[208,128]{1,0:T(8,128)(2,1)S(1)}, bf16[208,128]{1,0:T(8,128)(2,1)S(1)}, bf16[208,128]{1,0:T(8,128)(2,...) custom-call(bf16[32,2048]{1,0:T(8,128)(2,1)} %refs_0_.1, ...), custom_call_target="tpu_custom_call" | custom-call | tf_op jit(solution)/shard_map/pallas_call | solution.py:141
  1.7 6.0 %collective-permute-start = (bf16[208,128]{1,0:T(8,128)(2,1)S(1)}, bf16[208,128]{1,0:T(8,128)(2,1)S(1)}, u32[]{:S(2)}, u32[]{:S(2)}) collective-permute-start(bf16[208,128]{1,0:T(8,128)(2,1)S(1)} %get-tuple-element.14), channel_id=1, source_target_pairs={{0,14},{2,12},{4,10},{6,8},{8,6},{10,4},{12,2},{14,0},{1,15},{3,13... | collective-permute-start | bytes 159752 | tf_op jit(solution)/shard_map/ppermute | solution.py:174
  7.8 0.2 collective-permute-start.1
  8.0 0.8 %collective-permute-start.2 = (bf16[208,128]{1,0:T(8,128)(2,1)S(1)}, bf16[208,128]{1,0:T(8,128)(2,1)S(1)}, u32[]{:S(2)}, u32[]{:S(2)}) collective-permute-start(bf16[208,128]{1,0:T(8,128)(2,1)S(1)} %get-tuple-element.16), channel_id=1, source_target_pairs={{0,10},{2,8},{4,14},{6,12},{8,2},{10,0},{12,6},{14,4},{1,11},{3,9}... | collective-permute-start | bytes 159752 | tf_op jit(solution)/shard_map/ppermute | solution.py:174
  8.8 2.0 %collective-permute-start.3 = (bf16[208,128]{1,0:T(8,128)(2,1)S(1)}, bf16[208,128]{1,0:T(8,128)(2,1)S(1)}, u32[]{:S(2)}, u32[]{:S(2)}) collective-permute-start(bf16[208,128]{1,0:T(8,128)(2,1)S(1)} %get-tuple-element.17), channel_id=1, source_target_pairs={{0,8},{2,10},{4,12},{6,14},{8,0},{10,2},{12,4},{14,6},{1,9},{3,11}... | collective-permute-start | bytes 159752 | tf_op jit(solution)/shard_map/ppermute | solution.py:174
  10.8 2.3 %collective-permute-start.4 = (bf16[208,128]{1,0:T(8,128)(2,1)S(1)}, bf16[208,128]{1,0:T(8,128)(2,1)S(1)}, u32[]{:S(2)}, u32[]{:S(2)}) collective-permute-start(bf16[208,128]{1,0:T(8,128)(2,1)S(1)} %get-tuple-element.18), channel_id=1, source_target_pairs={{0,6},{2,4},{4,2},{6,0},{8,14},{10,12},{12,10},{14,8},{1,7},{3,5},... | collective-permute-start | bytes 159752 | tf_op jit(solution)/shard_map/ppermute | solution.py:174
  13.1 0.0 collective-permute-done.refs_1_
  13.1 0.8 %collective-permute-start.5 = (bf16[208,128]{1,0:T(8,128)(2,1)S(1)}, bf16[208,128]{1,0:T(8,128)(2,1)S(1)}, u32[]{:S(2)}, u32[]{:S(2)}) collective-permute-start(bf16[208,128]{1,0:T(8,128)(2,1)S(1)} %get-tuple-element.19), channel_id=1, source_target_pairs={{0,4},{2,6},{4,0},{6,2},{8,12},{10,14},{12,8},{14,10},{1,5},{3,7},... | collective-permute-start | bytes 159752 | tf_op jit(solution)/shard_map/ppermute | solution.py:174
  13.9 0.0 collective-permute-done.1.refs_2_
  13.9 0.4 %collective-permute-start.6 = (bf16[208,128]{1,0:T(8,128)(2,1)S(1)}, bf16[208,128]{1,0:T(8,128)(2,1)S(1)}, u32[]{:S(2)}, u32[]{:S(2)}) collective-permute-start(bf16[208,128]{1,0:T(8,128)(2,1)S(1)} %get-tuple-element.20), channel_id=1, source_target_pairs={{0,2},{2,0},{4,6},{6,4},{8,10},{10,8},{12,14},{14,12},{1,3},{3,1},... | collective-permute-start | bytes 159752 | tf_op jit(solution)/shard_map/ppermute | solution.py:174
  14.9 1.1 %collective-permute-done.2.refs_3_ = bf16[208,128]{1,0:T(8,128)(2,1)S(1)} collective-permute-done((bf16[208,128]{1,0:T(8,128)(2,1)S(1)}, bf16[208,128]{1,0:T(8,128)(2,1)S(1)}, u32[]{:S(2)}, u32[]{:S(2)}) %collective-permute-start.2) | collective-permute-done | bytes 53280 | tf_op jit(solution)/shard_map/ppermute | solution.py:174
  16.1 0.9 %collective-permute-done.3.refs_4_ = bf16[208,128]{1,0:T(8,128)(2,1)S(1)} collective-permute-done((bf16[208,128]{1,0:T(8,128)(2,1)S(1)}, bf16[208,128]{1,0:T(8,128)(2,1)S(1)}, u32[]{:S(2)}, u32[]{:S(2)}) %collective-permute-start.3) | collective-permute-done | bytes 53280 | tf_op jit(solution)/shard_map/ppermute | solution.py:174
  17.0 0.4 %collective-permute-done.4.refs_5_ = bf16[208,128]{1,0:T(8,128)(2,1)S(1)} collective-permute-done((bf16[208,128]{1,0:T(8,128)(2,1)S(1)}, bf16[208,128]{1,0:T(8,128)(2,1)S(1)}, u32[]{:S(2)}, u32[]{:S(2)}) %collective-permute-start.4) | collective-permute-done | bytes 53280 | tf_op jit(solution)/shard_map/ppermute | solution.py:174
  17.4 0.2 collective-permute-done.5.refs_6_
  17.6 0.4 %collective-permute-done.6.refs_7_ = bf16[208,128]{1,0:T(8,128)(2,1)S(1)} collective-permute-done((bf16[208,128]{1,0:T(8,128)(2,1)S(1)}, bf16[208,128]{1,0:T(8,128)(2,1)S(1)}, u32[]{:S(2)}, u32[]{:S(2)}) %collective-permute-start.6) | collective-permute-done | bytes 53280 | tf_op jit(solution)/shard_map/ppermute | solution.py:174
  18.0 0.0 collective-permute-start.7
  18.0 0.7 %shard_map.93.refs_10_ = f32[256,64]{1,0:T(8,128)S(1)} custom-call(bf16[208,128]{1,0:T(8,128)(2,1)S(1)} %get-tuple-element.13.refs_0_, bf16[208,128]{1,0:T(8,128)(2,1)S(1)} %collective-permute-done.refs_1_, bf16[208,128]{1,0:T(8,128)(2,1)S(1)} %collective-permute-done.1.refs_2_, bf16[208,128]{1,0:T(8,128)(2,1)S(1)} %collective-permute-done.2.refs_3_, ...), custom_call_target="tpu_custom_call" | custom-call | flops 1000000000 | bytes 1000000 | tf_op jit(solution)/shard_map/pallas_call | solution.py:141
  18.7 0.5 %collective-permute-done.7.refs_9_ = bf16[256,128]{1,0:T(8,128)(2,1)S(1)} collective-permute-done((bf16[256,128]{1,0:T(8,128)(2,1)S(1)}, bf16[256,128]{1,0:T(8,128)(2,1)S(1)}, u32[]{:S(2)}, u32[]{:S(2)}) %collective-permute-start.7) | collective-permute-done | bytes 65568 | tf_op jit(solution)/shard_map/ppermute | solution.py:180
  19.3 0.5 %shard_map.94 = bf16[16,16,128]{2,1,0:T(8,128)(2,1)S(1)} custom-call(bf16[208,128]{1,0:T(8,128)(2,1)S(1)} %get-tuple-element.13.refs_0_, bf16[208,128]{1,0:T(8,128)(2,1)S(1)} %collective-permute-done.refs_1_, bf16[208,128]{1,0:T(8,128)(2,1)S(1)} %collective-permute-done.1.refs_2_, bf16[208,128]{1,0:T(8,128)(2,1)S(1)} %collective-permute-done.2.refs_3_, ...), custom_call_target="tpu_custom_call" | custom-call | tf_op jit(solution)/shard_map/pallas_call | solution.py:141
  19.7 11.9 %all_to_all.5.x = bf16[16,16,128]{2,1,0:T(8,128)(2,1)S(1)} all-to-all(bf16[16,16,128]{2,1,0:T(8,128)(2,1)S(1)} %shard_map.94), channel_id=1, replica_groups=mesh['groups'=2,'seq'=8,'head'=2] {'seq','head'}, dimensions={0} | all-to-all | bytes 131072 | tf_op jit(solution)/shard_map/all_to_all | solution.py:194
  31.6 0.6 %shard_map.95 = f32[16,128]{1,0:T(8,128)} custom-call(bf16[16,16,128]{2,1,0:T(8,128)(2,1)S(1)} %all_to_all.5.x), custom_call_target="tpu_custom_call" | custom-call | tf_op jit(solution)/shard_map/pallas_call | solution.py:141
  (1 shorter events, 0.0 us)
Async XLA Ops:
  1.7 11.3 %collective-permute-start = (bf16[208,128]{1,0:T(8,128)(2,1)S(1)}, bf16[208,128]{1,0:T(8,128)(2,1)S(1)}, u32[]{:S(2)}, u32[]{:S(2)}) collective-permute-start(bf16[208,128]{1,0:T(8,128)(2,1)S(1)} %get-tuple-element.14), channel_id=1, source_target_pairs={{0,14},{2,12},{4,10},{6,8},{8,6},{10,4},{12,2},{14,0},{1,15},{3,13... | collective-permute-start | bytes 159752 | tf_op jit(solution)/shard_map/ppermute | solution.py:174
  7.8 6.1 %collective-permute-start.1 = (bf16[208,128]{1,0:T(8,128)(2,1)S(1)}, bf16[208,128]{1,0:T(8,128)(2,1)S(1)}, u32[]{:S(2)}, u32[]{:S(2)}) collective-permute-start(bf16[208,128]{1,0:T(8,128)(2,1)S(1)} %get-tuple-element.15), channel_id=1, source_target_pairs={{0,12},{2,14},{4,8},{6,10},{8,4},{10,6},{12,0},{14,2},{1,13},{3,15... | collective-permute-start | bytes 159752 | tf_op jit(solution)/shard_map/ppermute | solution.py:174
  8.0 8.1 %collective-permute-start.2 = (bf16[208,128]{1,0:T(8,128)(2,1)S(1)}, bf16[208,128]{1,0:T(8,128)(2,1)S(1)}, u32[]{:S(2)}, u32[]{:S(2)}) collective-permute-start(bf16[208,128]{1,0:T(8,128)(2,1)S(1)} %get-tuple-element.16), channel_id=1, source_target_pairs={{0,10},{2,8},{4,14},{6,12},{8,2},{10,0},{12,6},{14,4},{1,11},{3,9}... | collective-permute-start | bytes 159752 | tf_op jit(solution)/shard_map/ppermute | solution.py:174
  8.8 8.2 %collective-permute-start.3 = (bf16[208,128]{1,0:T(8,128)(2,1)S(1)}, bf16[208,128]{1,0:T(8,128)(2,1)S(1)}, u32[]{:S(2)}, u32[]{:S(2)}) collective-permute-start(bf16[208,128]{1,0:T(8,128)(2,1)S(1)} %get-tuple-element.17), channel_id=1, source_target_pairs={{0,8},{2,10},{4,12},{6,14},{8,0},{10,2},{12,4},{14,6},{1,9},{3,11}... | collective-permute-start | bytes 159752 | tf_op jit(solution)/shard_map/ppermute | solution.py:174
  10.8 6.6 %collective-permute-start.4 = (bf16[208,128]{1,0:T(8,128)(2,1)S(1)}, bf16[208,128]{1,0:T(8,128)(2,1)S(1)}, u32[]{:S(2)}, u32[]{:S(2)}) collective-permute-start(bf16[208,128]{1,0:T(8,128)(2,1)S(1)} %get-tuple-element.18), channel_id=1, source_target_pairs={{0,6},{2,4},{4,2},{6,0},{8,14},{10,12},{12,10},{14,8},{1,7},{3,5},... | collective-permute-start | bytes 159752 | tf_op jit(solution)/shard_map/ppermute | solution.py:174
  13.1 4.6 %collective-permute-start.5 = (bf16[208,128]{1,0:T(8,128)(2,1)S(1)}, bf16[208,128]{1,0:T(8,128)(2,1)S(1)}, u32[]{:S(2)}, u32[]{:S(2)}) collective-permute-start(bf16[208,128]{1,0:T(8,128)(2,1)S(1)} %get-tuple-element.19), channel_id=1, source_target_pairs={{0,4},{2,6},{4,0},{6,2},{8,12},{10,14},{12,8},{14,10},{1,5},{3,7},... | collective-permute-start | bytes 159752 | tf_op jit(solution)/shard_map/ppermute | solution.py:174
  13.9 4.1 %collective-permute-start.6 = (bf16[208,128]{1,0:T(8,128)(2,1)S(1)}, bf16[208,128]{1,0:T(8,128)(2,1)S(1)}, u32[]{:S(2)}, u32[]{:S(2)}) collective-permute-start(bf16[208,128]{1,0:T(8,128)(2,1)S(1)} %get-tuple-element.20), channel_id=1, source_target_pairs={{0,2},{2,0},{4,6},{6,4},{8,10},{10,8},{12,14},{14,12},{1,3},{3,1},... | collective-permute-start | bytes 159752 | tf_op jit(solution)/shard_map/ppermute | solution.py:174
  18.0 1.3 %collective-permute-start.7 = (bf16[256,128]{1,0:T(8,128)(2,1)S(1)}, bf16[256,128]{1,0:T(8,128)(2,1)S(1)}, u32[]{:S(2)}, u32[]{:S(2)}) collective-permute-start(bf16[256,128]{1,0:T(8,128)(2,1)S(1)} %shard_map.92.refs_8_), channel_id=1, source_target_pairs={{0,1},{1,0},{2,3},{3,2},{4,5},{5,4},{6,7},{7,6},{8,9},{9,8},{10,11... | collective-permute-start | bytes 196616 | tf_op jit(solution)/shard_map/ppermute | solution.py:180

commit v3 on v2

v3 whole, which is shorter than its diff:
```python
import functools
import math

import jax
import jax.numpy as jnp
from jax import lax
from jax.experimental import pallas as pl
from jax.experimental.pallas import tpu as pltpu
from jax.sharding import PartitionSpec as P

DH = 128
BF16 = jnp.bfloat16
F32 = jnp.float32
VMEM = pl.BlockSpec(memory_space=pltpu.VMEM)
HBM = pl.BlockSpec(memory_space=pltpu.HBM)
SMEM = pl.BlockSpec(memory_space=pltpu.SMEM)
NT = (((1,), (1,)), ((), ()))


def near_count(n):
    return n // 2


def hop_order(n):
    return [0] + [2, 4, 1, 7, 3, 5, 6] if n == 8 else list(range(n))


def row_layout(group, small_group, tokens, small_tokens):
    rows = {}
    at = 0
    for name, count in (
        ("k", group * tokens),
        ("vr", group // 2 * tokens),
        ("sk", small_group * small_tokens),
        ("svr", small_tokens),
        ("far", 0),
        ("q", group * tokens),
        ("sq", small_group * small_tokens),
        ("near", 0),
    ):
        rows[name] = at
        at += count
    return rows


def pack_kernel(n, near, group, small_group, rows, *refs):
    sources, outs, held, done = refs[:8], refs[8 : 8 + n], refs[8 + n : 16 + n], refs[16 + n]
    copies = [pltpu.make_async_copy(sources[i], held[i], done.at[i]) for i in range(8)]
    for copy in copies:
        copy.start()
    bk, bq, bv, br, sk, sq, sv, sr = held
    tokens, small_tokens = bk.shape[0], sk.shape[0]
    me = lax.axis_index("seq")

    def columns(j, heads, g):
        first = jnp.bitwise_xor(me, j) % near * heads + g
        return pl.ds(pl.multiple_of(first * DH, DH), DH)

    def put(j, row, value):
        for k in range(j, n, near):
            outs[k][pl.ds(row, value.shape[0]), :] = value

    copies[0].wait()
    for j in range(near):
        for g in range(group):
            put(j, rows["k"] + g * tokens, bk[:, columns(j, group, g)])
    copies[1].wait()
    for j in range(near):
        for g in range(group):
            outs[j][pl.ds(rows["q"] + g * tokens, tokens), :] = bq[:, columns(j, group, g)]
    copies[2].wait()
    copies[3].wait()
    for j in range(near):
        for g in range(0, group, 2):
            pair = []
            for h in (g, g + 1):
                cols = columns(j, group, h)
                pair.append(
                    lax.dot_general(bv[:, cols], br[:, cols], NT, preferred_element_type=F32)
                )
            put(j, rows["vr"] + g // 2 * tokens, jnp.concatenate(pair, axis=1).astype(BF16))
    for i in range(4, 8):
        copies[i].wait()
    for j in range(near):
        pair = []
        for g in range(small_group):
            cols = columns(j, small_group, g)
            put(j, rows["sk"] + g * small_tokens, sk[:, cols])
            outs[j][pl.ds(rows["sq"] + g * small_tokens, small_tokens), :] = sq[:, cols]
            pair.append(
                lax.dot_general(sv[:, cols], sr[:, cols], NT, preferred_element_type=F32)
            )
        put(j, rows["svr"], jnp.concatenate(pair, axis=1).astype(BF16))


def gather_small_kernel(order, near, rows, count, *refs):
    n = len(order)
    blocks, out = refs[:n], refs[n]
    other = 1 - lax.axis_index("head")
    at = 0

    def move(block, first):
        nonlocal at
        out[pl.ds(at, count), :] = block[pl.ds(first, count), :]
        at += count

    of_head = lambda name: pl.multiple_of(rows[name] + other * count, count)
    for block in blocks:
        move(block, of_head("sk"))
    for block in blocks:
        move(block, rows["svr"])
    for i in range(n):
        if order[i] < near:
            move(blocks[i], of_head("sq"))


def attend_head(queries, keys, values):
    scores = lax.dot_general(queries, keys, NT, preferred_element_type=F32)
    scores = scores * (1.0 / math.sqrt(DH))
    probs = jnp.exp(scores - jnp.max(scores, axis=1, keepdims=True))
    totals = jnp.sum(probs, axis=1, keepdims=True)
    out = jnp.dot(probs.astype(BF16), values, preferred_element_type=F32)
    return out / totals


def big_kernel(order, near, group, tokens, lat, rows, *refs):
    n = len(order)
    blocks, out = refs[:n], refs[n]
    here = [b for b, k in zip(blocks, order) if k < near]
    read = lambda some, first: jnp.concatenate(
        [b[pl.ds(first, tokens), :] for b in some], axis=0
    )
    total = None
    for g in range(group):
        if g % 2 == 0:
            values = read(blocks, rows["vr"] + g // 2 * tokens)
        part = attend_head(
            read(here, rows["q"] + g * tokens),
            read(blocks, rows["k"] + g * tokens),
            values[:, g % 2 * lat : (g % 2 + 1) * lat],
        )
        total = part if total is None else total + part
    out[:, :] = total


def small_kernel(order, near, tokens, count, lat, rows, *refs):
    n = len(order)
    blocks = refs[:n]
    theirs, big, guidance, out, latent = refs[n:]
    me, core = lax.axis_index("seq"), lax.axis_index("head")
    weight = guidance[0]
    here = [b for b, k in zip(blocks, order) if k < near]
    of_head = lambda name: pl.multiple_of(rows[name] + core * count, count)
    read = lambda some, first: [b[pl.ds(first, count), :] for b in some]
    join = lambda parts: jnp.concatenate(parts, axis=0)
    keys = join(read(blocks, of_head("sk")) + [theirs[: n * count, :]])
    values = join(read(blocks, rows["svr"]) + [theirs[n * count : 2 * n * count, :]])
    queries = join(read(here, of_head("sq")) + [theirs[2 * n * count :, :]])
    both = attend_head(queries, keys, values)
    small = weight * jnp.where(core == 0, both[:, :lat], both[:, lat : 2 * lat])
    latent[:, :lat] = (1.0 + weight) * big[:, :]
    for i in range(near):
        for side, whose in ((core, i), (1 - core, near + i)):
            part = pl.ds(pl.multiple_of(i * tokens + side * count, count), count)
            term = small[whose * count : (whose + 1) * count, :]
            latent[part, :lat] = latent[part, :lat] - term
    cores = tokens // count
    hops = [k for k in order if k < near]
    for i in range(near):
        even = latent[pl.ds(i * tokens, tokens // 2, stride=2), :lat]
        odd = latent[pl.ds(i * tokens + 1, tokens // 2, stride=2), :lat]
        dest = jnp.bitwise_xor(me, hops[i]) % near
        for c in range(cores):
            out[dest * cores + c] = jnp.concatenate([even, odd], axis=1)


def sum_kernel(x, out):
    total = x[0]
    for i in range(1, x.shape[0]):
        total = total + x[i]
    out[:, :] = total


def call(kernel, out_shape, operands, specs=None, scratch=(), cost=None):
    single = not isinstance(out_shape, (list, tuple))
    return pl.pallas_call(
        kernel,
        out_shape=out_shape,
        in_specs=specs if specs is not None else [VMEM] * len(operands),
        out_specs=VMEM if single else [VMEM] * len(out_shape),
        scratch_shapes=list(scratch),
        cost_estimate=cost,
        compiler_params=pltpu.CompilerParams(vmem_limit_bytes=16 * 2**20),
    )(*operands)


def exchange_shards(bq, bk, bv, sq, sk, sv, br, sr, guidance):
    n, cores = lax.axis_size("seq"), lax.axis_size("head")
    near = near_count(n)
    order = hop_order(n)
    tokens, count = bq.shape[0], sq.shape[0]
    group, small_group = bq.shape[1] // DH // near, sq.shape[1] // DH // near
    lat = br.shape[1]
    rows = row_layout(group, small_group, tokens, count)
    shape = lambda *dims, dtype=BF16: jax.ShapeDtypeStruct(dims, dtype)
    sources = [
        pltpu.with_memory_space_constraint(a, pltpu.HBM)
        for a in (bk, bq, bv, br.T, sk, sq, sv, sr.T)
    ]
    sent = call(
        functools.partial(pack_kernel, n, near, group, small_group, rows),
        [shape(rows["near" if k < near else "far"], DH) for k in range(n)],
        sources,
        specs=[HBM] * len(sources),
        scratch=[pltpu.VMEM(a.shape, a.dtype) for a in sources]
        + [pltpu.SemaphoreType.DMA((len(sources),))],
    )
    blocks = [sent[0]]
    for k in order[1:]:
        blocks.append(lax.ppermute(sent[k], "seq", [(j, j ^ k) for j in range(n)]))
    ours = call(
        functools.partial(gather_small_kernel, order, near, rows, count),
        shape((2 * n + near) * count, DH),
        blocks,
    )
    theirs = lax.ppermute(ours, "head", [(c, c ^ 1) for c in range(cores)])
    big = call(
        functools.partial(big_kernel, order, near, group, tokens, lat, rows),
        shape(near * tokens, lat, dtype=F32),
        blocks,
        cost=pl.CostEstimate(flops=10**9, bytes_accessed=10**6, transcendentals=10**5),
    )
    partial = call(
        functools.partial(small_kernel, order, near, tokens, count, lat, rows),
        shape(near * cores, tokens // 2, 2 * lat, dtype=F32),
        (*blocks, theirs, big, guidance),
        specs=[VMEM] * (n + 2) + [SMEM],
        scratch=[pltpu.VMEM((near * tokens, DH), F32)],
    )
    size = near * cores
    terms = lax.all_to_all(
        partial,
        ("seq", "head"),
        split_axis=0,
        concat_axis=0,
        tiled=True,
        axis_index_groups=[
            list(range(first, first + size)) for first in range(0, n * cores, size)
        ],
    )
    return call(sum_kernel, shape(tokens // 2, 2 * lat, dtype=F32), (terms,))


def fits_exchange(mesh, bq, sq, br):
    groups, n, cores = mesh.shape["groups"], mesh.shape["seq"], mesh.shape["head"]
    near = near_count(n)
    tokens = bq.shape[0] // (groups * n)
    count = sq.shape[0] // (groups * n * cores)
    big_heads, small_heads = bq.shape[1] // DH // cores, sq.shape[1] // DH
    return (
        cores == 2
        and n & (n - 1) == 0
        and near >= 1
        and small_heads == near * cores
        and big_heads % (2 * near) == 0
        and 2 * br.shape[1] == DH
        and count % 16 == 0
        and n * tokens <= 1024
    )


def split_heads(matrix, blocks, parts):
    rows_here, columns = matrix.shape
    shaped = matrix.reshape(blocks, rows_here // blocks, parts, columns // parts)
    shaped = jnp.transpose(shaped, (0, 2, 1, 3))
    return shaped.reshape(blocks * parts, rows_here // blocks, columns // parts)


def copy_heads(matrix, blocks, parts):
    rows_here, columns = matrix.shape
    shaped = jnp.transpose(matrix.reshape(rows_here, parts, columns // parts), (1, 0, 2))
    shaped = jnp.broadcast_to(shaped[None], (blocks, parts, rows_here, columns // parts))
    return shaped.reshape(blocks * parts, rows_here, columns // parts)


def join_heads(stacked, blocks, parts):
    pieces, rows_here, columns = stacked.shape
    shaped = stacked.reshape(blocks, parts, rows_here, columns)
    shaped = jnp.transpose(shaped, (0, 2, 1, 3))
    return shaped.reshape(blocks * rows_here, parts * columns)


def attend(query_rows, key_rows, value_rows):
    query_count = query_rows.shape[0]
    heads_here = query_rows.shape[1] // DH
    key_count = key_rows.shape[0]
    block_height = math.gcd(query_count, 256)
    block_count = query_count // block_height
    query_blocks = query_rows.reshape(block_count, block_height, heads_here, DH)
    key_split = key_rows.reshape(key_count, heads_here, DH)
    value_split = value_rows.reshape(key_count, heads_here, DH)
    score_scale = 1.0 / math.sqrt(DH)

    def one_block(query_block):
        scores = (
            jnp.einsum("qgd,kgd->gqk", query_block, key_split, preferred_element_type=F32)
            * score_scale
        )
        row_max = jnp.max(scores, axis=2, keepdims=True)
        probs = jnp.exp(scores - row_max)
        totals = jnp.sum(probs, axis=2, keepdims=True)
        weights = probs.astype(BF16)
        accumulated = jnp.einsum(
            "gqk,kgd->gqd", weights, value_split, preferred_element_type=F32
        )
        attended = accumulated / totals
        attended = jnp.transpose(attended, (1, 0, 2)).reshape(block_height, heads_here * DH)
        return attended.astype(BF16)

    outputs = lax.map(one_block, query_blocks)
    return outputs.reshape(query_count, heads_here * DH)


def seq_exchange(stacked, split, concat):
    return lax.all_to_all(stacked, "seq", split_axis=split, concat_axis=concat, tiled=True)


def run_model(queries, keys, values, shared):
    seq_count = lax.axis_size("seq")
    heads = queries.shape[1] // DH
    blocks = max(seq_count // heads, 1)
    parts = heads // max(heads // seq_count, 1)
    query_rows = seq_exchange(split_heads(queries, blocks, parts), 0, 1)[0]
    key_rows = seq_exchange(copy_heads(keys, blocks, parts), 0, 1)[0]
    value_rows = seq_exchange(copy_heads(values, blocks, parts), 0, 1)[0]
    if shared:
        key_rows = lax.all_gather(key_rows, "head", axis=0, tiled=True)
        value_rows = lax.all_gather(value_rows, "head", axis=0, tiled=True)
    out = attend(query_rows, key_rows, value_rows)
    return join_heads(seq_exchange(out[None], 1, 0), blocks, parts)


def general_shards(bq, bk, bv, sq, sk, sv, br, sr, guidance):
    big_attention = run_model(bq, bk, bv, False)
    big_partial = jnp.dot(big_attention, br, preferred_element_type=F32)
    small_attention = run_model(sq, sk, sv, True)
    small_latent = jnp.dot(small_attention, sr, preferred_element_type=F32)
    weight_value = guidance[0]
    core_index = lax.axis_index("head")
    placed = lax.dynamic_update_slice(
        jnp.zeros_like(big_partial),
        small_latent,
        (core_index * small_latent.shape[0], jnp.zeros((), jnp.int32)),
    )
    blended = lax.psum((1.0 + weight_value) * big_partial - weight_value * placed, "head")
    return blended.reshape(blended.shape[0] // 2, 2 * blended.shape[1])


def solution(mesh):
    placed = (
        P(("groups", "seq"), "head"),
        P(("groups", "seq"), "head"),
        P(("groups", "seq"), "head"),
        P(("groups", "seq", "head"), None),
        P(("groups", "seq", "head"), None),
        P(("groups", "seq", "head"), None),
        P("head", None),
        P(),
        P("groups"),
    )

    def whole(*arrays):
        fits = fits_exchange(mesh, arrays[0], arrays[3], arrays[6])
        return jax.shard_map(
            exchange_shards if fits else general_shards,
            mesh=mesh,
            in_specs=placed,
            out_specs=P(("groups", "seq"), None),
            check_vma=False,
        )(*arrays)

    return whole
```

time: 32.4 us -> 29.5 us (0.910)
  blocking collectives: 11.9 us -> 7.35 us
  waiting for transfers between devices: 3.58 us -> 4.44 us
  starting transfers between devices: 12.5 us -> 13.1 us
    all_to_all x1, blocking collectives: 11.9 us -> 7.35 us  [exchange_shards(): lax.all_to_all(partial, ('seq', 'head'), split_axis=0, concat_axis=0, til...]
    ppermute x7, waiting for transfers between devices: 3.06 us -> 3.89 us  [exchange_shards(): blocks.append(lax.ppermute(sent[k], 'seq', [(j, j ^ k) for j in range(n)]))]
    ppermute x7, starting transfers between devices: 12.5 us -> 13.1 us  [exchange_shards(): blocks.append(lax.ppermute(sent[k], 'seq', [(j, j ^ k) for j in range(n)]))]
  transfers between devices with their start and end apart: 8 -> 8, of which waited for: 6 -> 3; matrix products, arithmetic and copies ran while one was open for 0% -> 0% of each run, Pallas kernels for 2% -> 2%
where the time goes in v3:
time: 29.5 us; the launch traced here: 29.3 us
  starting transfers between devices  13.1 us (44%)
  blocking collectives  7.35 us (25%)
  waiting for transfers between devices  4.44 us (15%)
  Pallas kernels  3.7 us (13%)
  between operations  0.7 us (2%)
    ppermute x7, starting transfers between devices, exchange_shards(): blocks.append(lax.ppermute(sent[k], 'seq', [(j, j ^ k) for j in range(n)]))  13.1 us
    all_to_all x1, blocking collectives, exchange_shards(): lax.all_to_all(partial, ('seq', 'head'), split_axis=0, concat_axis=0, til...  7.35 us
    ppermute x7, waiting for transfers between devices, exchange_shards(): blocks.append(lax.ppermute(sent[k], 'seq', [(j, j ^ k) for j in range(n)]))  3.89 us
    pallas_call x5, Pallas kernels, call(): pl.pallas_call(kernel, out_shape=out_shape, in_specs=specs if specs is no...  3.7 us
  transfers between devices with their start and end apart: 8, of which 3 were waited for; matrix products, arithmetic and copies ran while one was open for 0% of the time, Pallas kernels for 2%

profile of v3, /device:TPU:0, one launch (start us, length us, event | category | flops | bytes accessed | tf_op | source)
XLA Modules:
  0.0 29.3 jit_solution(2549522130063124291)
XLA Ops:
  0.0 1.8 %shard_map.91 = (bf16[400,128]{1,0:T(8,128)(2,1)S(1)}, bf16[400,128]{1,0:T(8,128)(2,1)S(1)}, bf16[400,128]{1,0:T(8,128)(2,1)S(1)}, bf16[400,128]{1,0:T(8,128)(2,...) custom-call(bf16[32,2048]{1,0:T(8,128)(2,1)} %refs_0_.1, ...), custom_call_target="tpu_custom_call" | custom-call | tf_op jit(solution)/shard_map/pallas_call | solution.py:186
  1.8 4.1 %collective-permute-start.1 = (bf16[240,128]{1,0:T(8,128)(2,1)S(1)}, bf16[240,128]{1,0:T(8,128)(2,1)S(1)}, u32[]{:S(2)}, u32[]{:S(2)}) collective-permute-start(bf16[240,128]{1,0:T(8,128)(2,1)S(1)} %get-tuple-element.15), channel_id=1, source_target_pairs={{0,8},{2,10},{4,12},{6,14},{8,0},{10,2},{12,4},{14,6},{1,9},{3,11}... | collective-permute-start | bytes 184328 | tf_op jit(solution)/shard_map/ppermute | solution.py:220
  5.9 2.3 %collective-permute-start.3 = (bf16[240,128]{1,0:T(8,128)(2,1)S(1)}, bf16[240,128]{1,0:T(8,128)(2,1)S(1)}, u32[]{:S(2)}, u32[]{:S(2)}) collective-permute-start(bf16[240,128]{1,0:T(8,128)(2,1)S(1)} %get-tuple-element.17), channel_id=1, source_target_pairs={{0,14},{2,12},{4,10},{6,8},{8,6},{10,4},{12,2},{14,0},{1,15},{3,13... | collective-permute-start | bytes 184328 | tf_op jit(solution)/shard_map/ppermute | solution.py:220
  8.2 0.0 collective-permute-start
  8.2 0.8 %collective-permute-start.2 = (bf16[400,128]{1,0:T(8,128)(2,1)S(1)}, bf16[400,128]{1,0:T(8,128)(2,1)S(1)}, u32[]{:S(2)}, u32[]{:S(2)}) collective-permute-start(bf16[400,128]{1,0:T(8,128)(2,1)S(1)} %get-tuple-element.16), channel_id=1, source_target_pairs={{0,2},{2,0},{4,6},{6,4},{8,10},{10,8},{12,14},{14,12},{1,3},{3,1},... | collective-permute-start | bytes 307208 | tf_op jit(solution)/shard_map/ppermute | solution.py:220
  9.0 2.7 %collective-permute-start.4 = (bf16[400,128]{1,0:T(8,128)(2,1)S(1)}, bf16[400,128]{1,0:T(8,128)(2,1)S(1)}, u32[]{:S(2)}, u32[]{:S(2)}) collective-permute-start(bf16[400,128]{1,0:T(8,128)(2,1)S(1)} %get-tuple-element.18), channel_id=1, source_target_pairs={{0,6},{2,4},{4,2},{6,0},{8,14},{10,12},{12,10},{14,8},{1,7},{3,5},... | collective-permute-start | bytes 307208 | tf_op jit(solution)/shard_map/ppermute | solution.py:220
  11.7 0.0 collective-permute-done.1.refs_2_
  11.7 1.7 %collective-permute-start.5 = (bf16[240,128]{1,0:T(8,128)(2,1)S(1)}, bf16[240,128]{1,0:T(8,128)(2,1)S(1)}, u32[]{:S(2)}, u32[]{:S(2)}) collective-permute-start(bf16[240,128]{1,0:T(8,128)(2,1)S(1)} %get-tuple-element.19), channel_id=1, source_target_pairs={{0,10},{2,8},{4,14},{6,12},{8,2},{10,0},{12,6},{14,4},{1,11},{3,9}... | collective-permute-start | bytes 184328 | tf_op jit(solution)/shard_map/ppermute | solution.py:220
  13.3 0.0 collective-permute-done.3.refs_4_
  13.4 1.5 %collective-permute-start.6 = (bf16[240,128]{1,0:T(8,128)(2,1)S(1)}, bf16[240,128]{1,0:T(8,128)(2,1)S(1)}, u32[]{:S(2)}, u32[]{:S(2)}) collective-permute-start(bf16[240,128]{1,0:T(8,128)(2,1)S(1)} %get-tuple-element.20), channel_id=1, source_target_pairs={{0,12},{2,14},{4,8},{6,10},{8,4},{10,6},{12,0},{14,2},{1,13},{3,15... | collective-permute-start | bytes 184328 | tf_op jit(solution)/shard_map/ppermute | solution.py:220
  15.5 3.4 %collective-permute-done.5.refs_6_ = bf16[240,128]{1,0:T(8,128)(2,1)S(1)} collective-permute-done((bf16[240,128]{1,0:T(8,128)(2,1)S(1)}, bf16[240,128]{1,0:T(8,128)(2,1)S(1)}, u32[]{:S(2)}, u32[]{:S(2)}) %collective-permute-start.5) | collective-permute-done | bytes 61472 | tf_op jit(solution)/shard_map/ppermute | solution.py:220
  18.9 0.5 %collective-permute-done.6.refs_7_ = bf16[240,128]{1,0:T(8,128)(2,1)S(1)} collective-permute-done((bf16[240,128]{1,0:T(8,128)(2,1)S(1)}, bf16[240,128]{1,0:T(8,128)(2,1)S(1)}, u32[]{:S(2)}, u32[]{:S(2)}) %collective-permute-start.6) | collective-permute-done | bytes 61472 | tf_op jit(solution)/shard_map/ppermute | solution.py:220
  19.4 0.0 collective-permute-done.refs_1_
  19.4 0.0 collective-permute-done.2.refs_3_
  19.4 0.0 collective-permute-done.4.refs_5_
  19.5 0.1 collective-permute-start.7
  19.5 0.7 %shard_map.93.refs_9_ = f32[128,64]{1,0:T(8,128)S(1)} custom-call(bf16[400,128]{1,0:T(8,128)(2,1)S(1)} %get-tuple-element.13.refs_0_, bf16[400,128]{1,0:T(8,128)(2,1)S(1)} %collective-permute-done.refs_1_, bf16[240,128]{1,0:T(8,128)(2,1)S(1)} %collective-permute-done.1.refs_2_, bf16[400,128]{1,0:T(8,128)(2,1)S(1)} %collective-permute-done.2.refs_3_, ...), custom_call_target="tpu_custom_call" | custom-call | flops 1000000000 | bytes 1000000 | tf_op jit(solution)/shard_map/pallas_call | solution.py:186
  20.3 0.5 %collective-permute-done.7.refs_8_ = bf16[320,128]{1,0:T(8,128)(2,1)S(1)} collective-permute-done((bf16[320,128]{1,0:T(8,128)(2,1)S(1)}, bf16[320,128]{1,0:T(8,128)(2,1)S(1)}, u32[]{:S(2)}, u32[]{:S(2)}) %collective-permute-start.7) | collective-permute-done | bytes 81952 | tf_op jit(solution)/shard_map/ppermute | solution.py:226
  20.8 0.6 %shard_map.94 = f32[8,16,128]{2,1,0:T(8,128)S(1)} custom-call(bf16[400,128]{1,0:T(8,128)(2,1)S(1)} %get-tuple-element.13.refs_0_, bf16[400,128]{1,0:T(8,128)(2,1)S(1)} %collective-permute-done.refs_1_, bf16[240,128]{1,0:T(8,128)(2,1)S(1)} %collective-permute-done.1.refs_2_, bf16[400,128]{1,0:T(8,128)(2,1)S(1)} %collective-permute-done.2.refs_3_, ...), custom_call_target="tpu_custom_call" | custom-call | tf_op jit(solution)/shard_map/pallas_call | solution.py:186
  21.4 7.3 %all_to_all.5.x = f32[8,16,128]{2,1,0:T(8,128)S(1)} all-to-all(f32[8,16,128]{2,1,0:T(8,128)S(1)} %shard_map.94), channel_id=1, replica_groups={{0,1,2,3,4,5,6,7},{8,9,10,11,12,13,14,15},{16,17,18,19,20,21,22,23},{24..., dimensions={0} | all-to-all | bytes 131072 | tf_op jit(solution)/shard_map/all_to_all | solution.py:241
  28.7 0.6 %shard_map.95 = f32[16,128]{1,0:T(8,128)} custom-call(f32[8,16,128]{2,1,0:T(8,128)S(1)} %all_to_all.5.x), custom_call_target="tpu_custom_call" | custom-call | tf_op jit(solution)/shard_map/pallas_call | solution.py:186
  (1 shorter events, 0.0 us)
Async XLA Ops:
  1.8 9.9 %collective-permute-start.1 = (bf16[240,128]{1,0:T(8,128)(2,1)S(1)}, bf16[240,128]{1,0:T(8,128)(2,1)S(1)}, u32[]{:S(2)}, u32[]{:S(2)}) collective-permute-start(bf16[240,128]{1,0:T(8,128)(2,1)S(1)} %get-tuple-element.15), channel_id=1, source_target_pairs={{0,8},{2,10},{4,12},{6,14},{8,0},{10,2},{12,4},{14,6},{1,9},{3,11}... | collective-permute-start | bytes 184328 | tf_op jit(solution)/shard_map/ppermute | solution.py:220
  5.9 7.4 %collective-permute-start.3 = (bf16[240,128]{1,0:T(8,128)(2,1)S(1)}, bf16[240,128]{1,0:T(8,128)(2,1)S(1)}, u32[]{:S(2)}, u32[]{:S(2)}) collective-permute-start(bf16[240,128]{1,0:T(8,128)(2,1)S(1)} %get-tuple-element.17), channel_id=1, source_target_pairs={{0,14},{2,12},{4,10},{6,8},{8,6},{10,4},{12,2},{14,0},{1,15},{3,13... | collective-permute-start | bytes 184328 | tf_op jit(solution)/shard_map/ppermute | solution.py:220
  8.2 11.2 %collective-permute-start = (bf16[400,128]{1,0:T(8,128)(2,1)S(1)}, bf16[400,128]{1,0:T(8,128)(2,1)S(1)}, u32[]{:S(2)}, u32[]{:S(2)}) collective-permute-start(bf16[400,128]{1,0:T(8,128)(2,1)S(1)} %get-tuple-element.14), channel_id=1, source_target_pairs={{0,4},{2,6},{4,0},{6,2},{8,12},{10,14},{12,8},{14,10},{1,5},{3,7},... | collective-permute-start | bytes 307208 | tf_op jit(solution)/shard_map/ppermute | solution.py:220
  8.2 11.2 %collective-permute-start.2 = (bf16[400,128]{1,0:T(8,128)(2,1)S(1)}, bf16[400,128]{1,0:T(8,128)(2,1)S(1)}, u32[]{:S(2)}, u32[]{:S(2)}) collective-permute-start(bf16[400,128]{1,0:T(8,128)(2,1)S(1)} %get-tuple-element.16), channel_id=1, source_target_pairs={{0,2},{2,0},{4,6},{6,4},{8,10},{10,8},{12,14},{14,12},{1,3},{3,1},... | collective-permute-start | bytes 307208 | tf_op jit(solution)/shard_map/ppermute | solution.py:220
  9.0 10.4 %collective-permute-start.4 = (bf16[400,128]{1,0:T(8,128)(2,1)S(1)}, bf16[400,128]{1,0:T(8,128)(2,1)S(1)}, u32[]{:S(2)}, u32[]{:S(2)}) collective-permute-start(bf16[400,128]{1,0:T(8,128)(2,1)S(1)} %get-tuple-element.18), channel_id=1, source_target_pairs={{0,6},{2,4},{4,2},{6,0},{8,14},{10,12},{12,10},{14,8},{1,7},{3,5},... | collective-permute-start | bytes 307208 | tf_op jit(solution)/shard_map/ppermute | solution.py:220
  11.7 7.2 %collective-permute-start.5 = (bf16[240,128]{1,0:T(8,128)(2,1)S(1)}, bf16[240,128]{1,0:T(8,128)(2,1)S(1)}, u32[]{:S(2)}, u32[]{:S(2)}) collective-permute-start(bf16[240,128]{1,0:T(8,128)(2,1)S(1)} %get-tuple-element.19), channel_id=1, source_target_pairs={{0,10},{2,8},{4,14},{6,12},{8,2},{10,0},{12,6},{14,4},{1,11},{3,9}... | collective-permute-start | bytes 184328 | tf_op jit(solution)/shard_map/ppermute | solution.py:220
  13.4 6.1 %collective-permute-start.6 = (bf16[240,128]{1,0:T(8,128)(2,1)S(1)}, bf16[240,128]{1,0:T(8,128)(2,1)S(1)}, u32[]{:S(2)}, u32[]{:S(2)}) collective-permute-start(bf16[240,128]{1,0:T(8,128)(2,1)S(1)} %get-tuple-element.20), channel_id=1, source_target_pairs={{0,12},{2,14},{4,8},{6,10},{8,4},{10,6},{12,0},{14,2},{1,13},{3,15... | collective-permute-start | bytes 184328 | tf_op jit(solution)/shard_map/ppermute | solution.py:220
  19.5 1.3 %collective-permute-start.7 = (bf16[320,128]{1,0:T(8,128)(2,1)S(1)}, bf16[320,128]{1,0:T(8,128)(2,1)S(1)}, u32[]{:S(2)}, u32[]{:S(2)}) collective-permute-start(bf16[320,128]{1,0:T(8,128)(2,1)S(1)} %shard_map.92), channel_id=1, source_target_pairs={{0,1},{1,0},{2,3},{3,2},{4,5},{5,4},{6,7},{7,6},{8,9},{9,8},{10,11... | collective-permute-start | bytes 245768 | tf_op jit(solution)/shard_map/ppermute | solution.py:226

commit v4 on v3

--- a/solution.py
+++ b/solution.py
@@ -48,7 +48,7 @@
     copies = [pltpu.make_async_copy(sources[i], held[i], done.at[i]) for i in range(8)]
     for copy in copies:
         copy.start()
-    bk, bq, bv, br, sk, sq, sv, sr = held
+    sv, sr, bv, br, sk, sq, bk, bq = held
     tokens, small_tokens = bk.shape[0], sk.shape[0]
     me = lax.axis_index("seq")
 
@@ -60,37 +60,40 @@
         for k in range(j, n, near):
             outs[k][pl.ds(row, value.shape[0]), :] = value
 
+    def project(values, readout, heads, j, g):
+        first = jnp.bitwise_xor(me, j) % near * heads + g
+        cols = pl.ds(pl.multiple_of(first * DH, DH), 2 * DH)
+        pair = readout[:, cols]
+        none = jnp.zeros((readout.shape[0], DH), BF16)
+        left = jnp.concatenate([pair[:, :DH], none], axis=1)
+        right = jnp.concatenate([none, pair[:, DH:]], axis=1)
+        both = jnp.concatenate([left, right], axis=0)
+        out = lax.dot_general(values[:, cols], both, NT, preferred_element_type=F32)
+        return out.astype(BF16)
+
     copies[0].wait()
-    for j in range(near):
-        for g in range(group):
-            put(j, rows["k"] + g * tokens, bk[:, columns(j, group, g)])
     copies[1].wait()
     for j in range(near):
-        for g in range(group):
-            outs[j][pl.ds(rows["q"] + g * tokens, tokens), :] = bq[:, columns(j, group, g)]
+        put(j, rows["svr"], project(sv, sr, small_group, j, 0))
     copies[2].wait()
     copies[3].wait()
     for j in range(near):
         for g in range(0, group, 2):
-            pair = []
-            for h in (g, g + 1):
-                cols = columns(j, group, h)
-                pair.append(
-                    lax.dot_general(bv[:, cols], br[:, cols], NT, preferred_element_type=F32)
-                )
-            put(j, rows["vr"] + g // 2 * tokens, jnp.concatenate(pair, axis=1).astype(BF16))
-    for i in range(4, 8):
-        copies[i].wait()
+            put(j, rows["vr"] + g // 2 * tokens, project(bv, br, group, j, g))
+    copies[4].wait()
+    copies[5].wait()
     for j in range(near):
-        pair = []
         for g in range(small_group):
             cols = columns(j, small_group, g)
             put(j, rows["sk"] + g * small_tokens, sk[:, cols])
             outs[j][pl.ds(rows["sq"] + g * small_tokens, small_tokens), :] = sq[:, cols]
-            pair.append(
-                lax.dot_general(sv[:, cols], sr[:, cols], NT, preferred_element_type=F32)
-            )
-        put(j, rows["svr"], jnp.concatenate(pair, axis=1).astype(BF16))
+    copies[6].wait()
+    copies[7].wait()
+    for j in range(near):
+        for g in range(group):
+            cols = columns(j, group, g)
+            put(j, rows["k"] + g * tokens, bk[:, cols])
+            outs[j][pl.ds(rows["q"] + g * tokens, tokens), :] = bq[:, cols]
 
 
 def gather_small_kernel(order, near, rows, count, *refs):
@@ -205,7 +208,7 @@
     shape = lambda *dims, dtype=BF16: jax.ShapeDtypeStruct(dims, dtype)
     sources = [
         pltpu.with_memory_space_constraint(a, pltpu.HBM)
-        for a in (bk, bq, bv, br.T, sk, sq, sv, sr.T)
+        for a in (sv, sr.T, bv, br.T, sk, sq, bk, bq)
     ]
     sent = call(
         functools.partial(pack_kernel, n, near, group, small_group, rows),

time: 29.5 us -> 29.3 us (level)
  no operation moved by 1% of the time
where the time goes in v4:
time: 29.3 us; the launch traced here: 29.1 us
  starting transfers between devices  13.1 us (45%)
  blocking collectives  7.35 us (25%)
  waiting for transfers between devices  4.44 us (15%)
  Pallas kernels  3.46 us (12%)
  between operations  0.7 us (2%)
    ppermute x7, starting transfers between devices, exchange_shards(): blocks.append(lax.ppermute(sent[k], 'seq', [(j, j ^ k) for j in range(n)]))  13.1 us
    all_to_all x1, blocking collectives, exchange_shards(): lax.all_to_all(partial, ('seq', 'head'), split_axis=0, concat_axis=0, til...  7.35 us
    ppermute x7, waiting for transfers between devices, exchange_shards(): blocks.append(lax.ppermute(sent[k], 'seq', [(j, j ^ k) for j in range(n)]))  3.9 us
    pallas_call x5, Pallas kernels, call(): pl.pallas_call(kernel, out_shape=out_shape, in_specs=specs if specs is no...  3.46 us
  transfers between devices with their start and end apart: 8, of which 3 were waited for; matrix products, arithmetic and copies ran while one was open for 0% of the time, Pallas kernels for 2%

profile of v4, /device:TPU:0, one launch (start us, length us, event | category | flops | bytes accessed | tf_op | source)
XLA Modules:
  0.0 29.1 jit_solution(13823151686126160625)
XLA Ops:
  0.0 1.6 %shard_map.91 = (bf16[400,128]{1,0:T(8,128)(2,1)S(1)}, bf16[400,128]{1,0:T(8,128)(2,1)S(1)}, bf16[400,128]{1,0:T(8,128)(2,1)S(1)}, bf16[400,128]{1,0:T(8,128)(2,...) custom-call(bf16[16,1024]{1,0:T(8,128)(2,1)} %refs_0_.1, ...), custom_call_target="tpu_custom_call" | custom-call | tf_op jit(solution)/shard_map/pallas_call | solution.py:189
  1.6 4.1 %collective-permute-start.1 = (bf16[240,128]{1,0:T(8,128)(2,1)S(1)}, bf16[240,128]{1,0:T(8,128)(2,1)S(1)}, u32[]{:S(2)}, u32[]{:S(2)}) collective-permute-start(bf16[240,128]{1,0:T(8,128)(2,1)S(1)} %get-tuple-element.15), channel_id=1, source_target_pairs={{0,8},{2,10},{4,12},{6,14},{8,0},{10,2},{12,4},{14,6},{1,9},{3,11}... | collective-permute-start | bytes 184328 | tf_op jit(solution)/shard_map/ppermute | solution.py:223
  5.7 2.3 %collective-permute-start.3 = (bf16[240,128]{1,0:T(8,128)(2,1)S(1)}, bf16[240,128]{1,0:T(8,128)(2,1)S(1)}, u32[]{:S(2)}, u32[]{:S(2)}) collective-permute-start(bf16[240,128]{1,0:T(8,128)(2,1)S(1)} %get-tuple-element.17), channel_id=1, source_target_pairs={{0,14},{2,12},{4,10},{6,8},{8,6},{10,4},{12,2},{14,0},{1,15},{3,13... | collective-permute-start | bytes 184328 | tf_op jit(solution)/shard_map/ppermute | solution.py:223
  7.9 0.0 collective-permute-start
  8.0 0.8 %collective-permute-start.2 = (bf16[400,128]{1,0:T(8,128)(2,1)S(1)}, bf16[400,128]{1,0:T(8,128)(2,1)S(1)}, u32[]{:S(2)}, u32[]{:S(2)}) collective-permute-start(bf16[400,128]{1,0:T(8,128)(2,1)S(1)} %get-tuple-element.16), channel_id=1, source_target_pairs={{0,2},{2,0},{4,6},{6,4},{8,10},{10,8},{12,14},{14,12},{1,3},{3,1},... | collective-permute-start | bytes 307208 | tf_op jit(solution)/shard_map/ppermute | solution.py:223
  8.7 2.7 %collective-permute-start.4 = (bf16[400,128]{1,0:T(8,128)(2,1)S(1)}, bf16[400,128]{1,0:T(8,128)(2,1)S(1)}, u32[]{:S(2)}, u32[]{:S(2)}) collective-permute-start(bf16[400,128]{1,0:T(8,128)(2,1)S(1)} %get-tuple-element.18), channel_id=1, source_target_pairs={{0,6},{2,4},{4,2},{6,0},{8,14},{10,12},{12,10},{14,8},{1,7},{3,5},... | collective-permute-start | bytes 307208 | tf_op jit(solution)/shard_map/ppermute | solution.py:223
  11.4 0.0 collective-permute-done.1.refs_2_
  11.4 1.7 %collective-permute-start.5 = (bf16[240,128]{1,0:T(8,128)(2,1)S(1)}, bf16[240,128]{1,0:T(8,128)(2,1)S(1)}, u32[]{:S(2)}, u32[]{:S(2)}) collective-permute-start(bf16[240,128]{1,0:T(8,128)(2,1)S(1)} %get-tuple-element.19), channel_id=1, source_target_pairs={{0,10},{2,8},{4,14},{6,12},{8,2},{10,0},{12,6},{14,4},{1,11},{3,9}... | collective-permute-start | bytes 184328 | tf_op jit(solution)/shard_map/ppermute | solution.py:223
  13.1 0.0 collective-permute-done.3.refs_4_
  13.1 1.5 %collective-permute-start.6 = (bf16[240,128]{1,0:T(8,128)(2,1)S(1)}, bf16[240,128]{1,0:T(8,128)(2,1)S(1)}, u32[]{:S(2)}, u32[]{:S(2)}) collective-permute-start(bf16[240,128]{1,0:T(8,128)(2,1)S(1)} %get-tuple-element.20), channel_id=1, source_target_pairs={{0,12},{2,14},{4,8},{6,10},{8,4},{10,6},{12,0},{14,2},{1,13},{3,15... | collective-permute-start | bytes 184328 | tf_op jit(solution)/shard_map/ppermute | solution.py:223
  15.3 3.4 %collective-permute-done.5.refs_6_ = bf16[240,128]{1,0:T(8,128)(2,1)S(1)} collective-permute-done((bf16[240,128]{1,0:T(8,128)(2,1)S(1)}, bf16[240,128]{1,0:T(8,128)(2,1)S(1)}, u32[]{:S(2)}, u32[]{:S(2)}) %collective-permute-start.5) | collective-permute-done | bytes 61472 | tf_op jit(solution)/shard_map/ppermute | solution.py:223
  18.7 0.5 %collective-permute-done.6.refs_7_ = bf16[240,128]{1,0:T(8,128)(2,1)S(1)} collective-permute-done((bf16[240,128]{1,0:T(8,128)(2,1)S(1)}, bf16[240,128]{1,0:T(8,128)(2,1)S(1)}, u32[]{:S(2)}, u32[]{:S(2)}) %collective-permute-start.6) | collective-permute-done | bytes 61472 | tf_op jit(solution)/shard_map/ppermute | solution.py:223
  19.2 0.0 collective-permute-done.refs_1_
  19.2 0.0 collective-permute-done.2.refs_3_
  19.2 0.0 collective-permute-done.4.refs_5_
  19.2 0.1 collective-permute-start.7
  19.3 0.7 %shard_map.93.refs_9_ = f32[128,64]{1,0:T(8,128)S(1)} custom-call(bf16[400,128]{1,0:T(8,128)(2,1)S(1)} %get-tuple-element.13.refs_0_, bf16[400,128]{1,0:T(8,128)(2,1)S(1)} %collective-permute-done.refs_1_, bf16[240,128]{1,0:T(8,128)(2,1)S(1)} %collective-permute-done.1.refs_2_, bf16[400,128]{1,0:T(8,128)(2,1)S(1)} %collective-permute-done.2.refs_3_, ...), custom_call_target="tpu_custom_call" | custom-call | flops 1000000000 | bytes 1000000 | tf_op jit(solution)/shard_map/pallas_call | solution.py:189
  20.0 0.5 %collective-permute-done.7.refs_8_ = bf16[320,128]{1,0:T(8,128)(2,1)S(1)} collective-permute-done((bf16[320,128]{1,0:T(8,128)(2,1)S(1)}, bf16[320,128]{1,0:T(8,128)(2,1)S(1)}, u32[]{:S(2)}, u32[]{:S(2)}) %collective-permute-start.7) | collective-permute-done | bytes 81952 | tf_op jit(solution)/shard_map/ppermute | solution.py:229
  20.6 0.6 %shard_map.94 = f32[8,16,128]{2,1,0:T(8,128)S(1)} custom-call(bf16[400,128]{1,0:T(8,128)(2,1)S(1)} %get-tuple-element.13.refs_0_, bf16[400,128]{1,0:T(8,128)(2,1)S(1)} %collective-permute-done.refs_1_, bf16[240,128]{1,0:T(8,128)(2,1)S(1)} %collective-permute-done.1.refs_2_, bf16[400,128]{1,0:T(8,128)(2,1)S(1)} %collective-permute-done.2.refs_3_, ...), custom_call_target="tpu_custom_call" | custom-call | tf_op jit(solution)/shard_map/pallas_call | solution.py:189
  21.1 7.3 %all_to_all.5.x = f32[8,16,128]{2,1,0:T(8,128)S(1)} all-to-all(f32[8,16,128]{2,1,0:T(8,128)S(1)} %shard_map.94), channel_id=1, replica_groups={{0,1,2,3,4,5,6,7},{8,9,10,11,12,13,14,15},{16,17,18,19,20,21,22,23},{24..., dimensions={0} | all-to-all | bytes 131072 | tf_op jit(solution)/shard_map/all_to_all | solution.py:244
  28.5 0.6 %shard_map.95 = f32[16,128]{1,0:T(8,128)} custom-call(f32[8,16,128]{2,1,0:T(8,128)S(1)} %all_to_all.5.x), custom_call_target="tpu_custom_call" | custom-call | tf_op jit(solution)/shard_map/pallas_call | solution.py:189
  (1 shorter events, 0.0 us)
Async XLA Ops:
  1.6 9.9 %collective-permute-start.1 = (bf16[240,128]{1,0:T(8,128)(2,1)S(1)}, bf16[240,128]{1,0:T(8,128)(2,1)S(1)}, u32[]{:S(2)}, u32[]{:S(2)}) collective-permute-start(bf16[240,128]{1,0:T(8,128)(2,1)S(1)} %get-tuple-element.15), channel_id=1, source_target_pairs={{0,8},{2,10},{4,12},{6,14},{8,0},{10,2},{12,4},{14,6},{1,9},{3,11}... | collective-permute-start | bytes 184328 | tf_op jit(solution)/shard_map/ppermute | solution.py:223
  5.7 7.4 %collective-permute-start.3 = (bf16[240,128]{1,0:T(8,128)(2,1)S(1)}, bf16[240,128]{1,0:T(8,128)(2,1)S(1)}, u32[]{:S(2)}, u32[]{:S(2)}) collective-permute-start(bf16[240,128]{1,0:T(8,128)(2,1)S(1)} %get-tuple-element.17), channel_id=1, source_target_pairs={{0,14},{2,12},{4,10},{6,8},{8,6},{10,4},{12,2},{14,0},{1,15},{3,13... | collective-permute-start | bytes 184328 | tf_op jit(solution)/shard_map/ppermute | solution.py:223
  7.9 11.2 %collective-permute-start = (bf16[400,128]{1,0:T(8,128)(2,1)S(1)}, bf16[400,128]{1,0:T(8,128)(2,1)S(1)}, u32[]{:S(2)}, u32[]{:S(2)}) collective-permute-start(bf16[400,128]{1,0:T(8,128)(2,1)S(1)} %get-tuple-element.14), channel_id=1, source_target_pairs={{0,4},{2,6},{4,0},{6,2},{8,12},{10,14},{12,8},{14,10},{1,5},{3,7},... | collective-permute-start | bytes 307208 | tf_op jit(solution)/shard_map/ppermute | solution.py:223
  8.0 11.2 %collective-permute-start.2 = (bf16[400,128]{1,0:T(8,128)(2,1)S(1)}, bf16[400,128]{1,0:T(8,128)(2,1)S(1)}, u32[]{:S(2)}, u32[]{:S(2)}) collective-permute-start(bf16[400,128]{1,0:T(8,128)(2,1)S(1)} %get-tuple-element.16), channel_id=1, source_target_pairs={{0,2},{2,0},{4,6},{6,4},{8,10},{10,8},{12,14},{14,12},{1,3},{3,1},... | collective-permute-start | bytes 307208 | tf_op jit(solution)/shard_map/ppermute | solution.py:223
  8.7 10.5 %collective-permute-start.4 = (bf16[400,128]{1,0:T(8,128)(2,1)S(1)}, bf16[400,128]{1,0:T(8,128)(2,1)S(1)}, u32[]{:S(2)}, u32[]{:S(2)}) collective-permute-start(bf16[400,128]{1,0:T(8,128)(2,1)S(1)} %get-tuple-element.18), channel_id=1, source_target_pairs={{0,6},{2,4},{4,2},{6,0},{8,14},{10,12},{12,10},{14,8},{1,7},{3,5},... | collective-permute-start | bytes 307208 | tf_op jit(solution)/shard_map/ppermute | solution.py:223
  11.4 7.2 %collective-permute-start.5 = (bf16[240,128]{1,0:T(8,128)(2,1)S(1)}, bf16[240,128]{1,0:T(8,128)(2,1)S(1)}, u32[]{:S(2)}, u32[]{:S(2)}) collective-permute-start(bf16[240,128]{1,0:T(8,128)(2,1)S(1)} %get-tuple-element.19), channel_id=1, source_target_pairs={{0,10},{2,8},{4,14},{6,12},{8,2},{10,0},{12,6},{14,4},{1,11},{3,9}... | collective-permute-start | bytes 184328 | tf_op jit(solution)/shard_map/ppermute | solution.py:223
  13.1 6.1 %collective-permute-start.6 = (bf16[240,128]{1,0:T(8,128)(2,1)S(1)}, bf16[240,128]{1,0:T(8,128)(2,1)S(1)}, u32[]{:S(2)}, u32[]{:S(2)}) collective-permute-start(bf16[240,128]{1,0:T(8,128)(2,1)S(1)} %get-tuple-element.20), channel_id=1, source_target_pairs={{0,12},{2,14},{4,8},{6,10},{8,4},{10,6},{12,0},{14,2},{1,13},{3,15... | collective-permute-start | bytes 184328 | tf_op jit(solution)/shard_map/ppermute | solution.py:223
  19.2 1.3 %collective-permute-start.7 = (bf16[320,128]{1,0:T(8,128)(2,1)S(1)}, bf16[320,128]{1,0:T(8,128)(2,1)S(1)}, u32[]{:S(2)}, u32[]{:S(2)}) collective-permute-start(bf16[320,128]{1,0:T(8,128)(2,1)S(1)} %shard_map.92), channel_id=1, source_target_pairs={{0,1},{1,0},{2,3},{3,2},{4,5},{5,4},{6,7},{7,6},{8,9},{9,8},{10,11... | collective-permute-start | bytes 245768 | tf_op jit(solution)/shard_map/ppermute | solution.py:229

commit v5 on v4

--- a/solution.py
+++ b/solution.py
@@ -96,25 +96,16 @@
             outs[j][pl.ds(rows["q"] + g * tokens, tokens), :] = bq[:, cols]
 
 
-def gather_small_kernel(order, near, rows, count, *refs):
+def gather_small_kernel(order, near, rows, *refs):
     n = len(order)
-    blocks, out = refs[:n], refs[n]
-    other = 1 - lax.axis_index("head")
+    blocks, (guidance, out, weight) = refs[:n], refs[n:]
+    weight[:, :] = jnp.full(weight.shape, guidance[0], F32)
     at = 0
-
-    def move(block, first):
-        nonlocal at
-        out[pl.ds(at, count), :] = block[pl.ds(first, count), :]
-        at += count
-
-    of_head = lambda name: pl.multiple_of(rows[name] + other * count, count)
-    for block in blocks:
-        move(block, of_head("sk"))
-    for block in blocks:
-        move(block, rows["svr"])
-    for i in range(n):
-        if order[i] < near:
-            move(blocks[i], of_head("sq"))
+    for block, k in zip(blocks, order):
+        parts = [(rows["sk"], rows["far"])] + ([(rows["sq"], rows["near"])] if k < near else [])
+        for first, last in parts:
+            out[pl.ds(at, last - first), :] = block[pl.ds(first, last - first), :]
+            at += last - first
 
 
 def attend_head(queries, keys, values):
@@ -146,42 +137,57 @@
     out[:, :] = total
 
 
-def small_kernel(order, near, tokens, count, lat, rows, *refs):
+def small_kernel(order, near, small_group, tokens, count, lat, rows, *refs):
     n = len(order)
-    blocks = refs[:n]
-    theirs, big, guidance, out, latent = refs[n:]
-    me, core = lax.axis_index("seq"), lax.axis_index("head")
-    weight = guidance[0]
-    here = [b for b, k in zip(blocks, order) if k < near]
-    of_head = lambda name: pl.multiple_of(rows[name] + core * count, count)
-    read = lambda some, first: [b[pl.ds(first, count), :] for b in some]
-    join = lambda parts: jnp.concatenate(parts, axis=0)
-    keys = join(read(blocks, of_head("sk")) + [theirs[: n * count, :]])
-    values = join(read(blocks, rows["svr"]) + [theirs[n * count : 2 * n * count, :]])
-    queries = join(read(here, of_head("sq")) + [theirs[2 * n * count :, :]])
-    both = attend_head(queries, keys, values)
-    small = weight * jnp.where(core == 0, both[:, :lat], both[:, lat : 2 * lat])
-    latent[:, :lat] = (1.0 + weight) * big[:, :]
+    blocks, theirs, out = refs[:n], refs[n], refs[n + 1]
+    core = lax.axis_index("head")
+    at = 0
+    found = {name: [] for name in ("sk", "svr", "sq")}
+    for block, k in zip(blocks, order):
+        for name, size in (
+            ("sk", small_group * count),
+            ("svr", count),
+            ("sq", small_group * count),
+        ):
+            if name == "sq" and k >= near:
+                continue
+            own = block[pl.ds(rows[name], size), :]
+            found[name].append((own, theirs[pl.ds(at, size), :]))
+            at += size
+
+    def read(name, first):
+        sides = [[p[side][first : first + count] for p in found[name]] for side in (0, 1)]
+        return jnp.concatenate(sides[0] + sides[1], axis=0)
+
+    values = read("svr", 0)
+    total = None
+    for g in range(small_group):
+        part = attend_head(
+            read("sq", g * count), read("sk", g * count), values[:, g * lat : (g + 1) * lat]
+        )
+        total = part if total is None else total + part
     for i in range(near):
         for side, whose in ((core, i), (1 - core, near + i)):
             part = pl.ds(pl.multiple_of(i * tokens + side * count, count), count)
-            term = small[whose * count : (whose + 1) * count, :]
-            latent[part, :lat] = latent[part, :lat] - term
-    cores = tokens // count
-    hops = [k for k in order if k < near]
+            out[part, :] = total[whose * count : (whose + 1) * count, :]
+
+
+def blend_kernel(near, tokens, big, other_big, small, guidance, *refs):
+    outs, latent = refs[:near], refs[near]
+    lat = big.shape[1]
+    weight = guidance[:1, :lat]
+    latent[:, :lat] = (1.0 + weight) * (big[:, :] + other_big[:, :]) - weight * small[:, :]
     for i in range(near):
         even = latent[pl.ds(i * tokens, tokens // 2, stride=2), :lat]
         odd = latent[pl.ds(i * tokens + 1, tokens // 2, stride=2), :lat]
-        dest = jnp.bitwise_xor(me, hops[i]) % near
-        for c in range(cores):
-            out[dest * cores + c] = jnp.concatenate([even, odd], axis=1)
-
-
-def sum_kernel(x, out):
-    total = x[0]
-    for i in range(1, x.shape[0]):
-        total = total + x[i]
-    out[:, :] = total
+        outs[i][:, :] = jnp.concatenate([even, odd], axis=1)
+
+
+def sum_kernel(*refs):
+    total = refs[0][:, :]
+    for x in refs[1:-1]:
+        total = total + x[:, :]
+    refs[-1][:, :] = total
 
 
 def call(kernel, out_shape, operands, specs=None, scratch=(), cost=None):
@@ -221,37 +227,41 @@
     blocks = [sent[0]]
     for k in order[1:]:
         blocks.append(lax.ppermute(sent[k], "seq", [(j, j ^ k) for j in range(n)]))
-    ours = call(
-        functools.partial(gather_small_kernel, order, near, rows, count),
-        shape((2 * n + near) * count, DH),
-        blocks,
-    )
-    theirs = lax.ppermute(ours, "head", [(c, c ^ 1) for c in range(cores)])
+    ours, weight = call(
+        functools.partial(gather_small_kernel, order, near, rows),
+        [
+            shape(n * (rows["far"] - rows["sk"]) + near * (rows["near"] - rows["sq"]), DH),
+            shape(8, DH, dtype=F32),
+        ],
+        (*blocks, guidance),
+        specs=[VMEM] * n + [SMEM],
+    )
+    swap = lambda a: lax.ppermute(a, "head", [(c, c ^ 1) for c in range(cores)])
+    theirs = swap(ours)
     big = call(
         functools.partial(big_kernel, order, near, group, tokens, lat, rows),
         shape(near * tokens, lat, dtype=F32),
         blocks,
         cost=pl.CostEstimate(flops=10**9, bytes_accessed=10**6, transcendentals=10**5),
     )
-    partial = call(
-        functools.partial(small_kernel, order, near, tokens, count, lat, rows),
-        shape(near * cores, tokens // 2, 2 * lat, dtype=F32),
-        (*blocks, theirs, big, guidance),
-        specs=[VMEM] * (n + 2) + [SMEM],
+    other_big = swap(big)
+    small = call(
+        functools.partial(small_kernel, order, near, small_group, tokens, count, lat, rows),
+        shape(near * tokens, lat, dtype=F32),
+        (*blocks, theirs),
+        cost=pl.CostEstimate(flops=10**9, bytes_accessed=10**6, transcendentals=10**5),
+    )
+    hops = [k for k in order if k < near]
+    terms = call(
+        functools.partial(blend_kernel, near, tokens),
+        [shape(tokens // 2, 2 * lat, dtype=F32)] * near,
+        (big, other_big, small, weight),
         scratch=[pltpu.VMEM((near * tokens, DH), F32)],
     )
-    size = near * cores
-    terms = lax.all_to_all(
-        partial,
-        ("seq", "head"),
-        split_axis=0,
-        concat_axis=0,
-        tiled=True,
-        axis_index_groups=[
-            list(range(first, first + size)) for first in range(0, n * cores, size)
-        ],
-    )
-    return call(sum_kernel, shape(tokens // 2, 2 * lat, dtype=F32), (terms,))
+    sums = [terms[0]]
+    for i in range(1, near):
+        sums.append(lax.ppermute(terms[i], "seq", [(j, j ^ hops[i]) for j in range(n)]))
+    return call(sum_kernel, shape(tokens // 2, 2 * lat, dtype=F32), sums)
 
 
 def fits_exchange(mesh, bq, sq, br):

time: 29.3 us -> 28.8 us (0.983)
  blocking collectives: 7.35 us -> 0 us
  starting transfers between devices: 13.1 us -> 17.2 us
  waiting for transfers between devices: 4.44 us -> 7.09 us
    all_to_all x1 -> x0, blocking collectives: 7.35 us -> none  [exchange_shards(): lax.all_to_all(partial, ('seq', 'head'), split_axis=0, concat_axis=0, til...]
    ppermute x1 -> x5, starting transfers between devices: 0.07 us -> 4.18 us  [the longest x3 3.55 us: exchange_shards(): lax.ppermute(terms[i], 'seq', [(j, j ^ hops[i]) for j in range(n)])]
    ppermute x1 -> x5, waiting for transfers between devices: 0.54 us -> 3.2 us  [the longest x3 2.94 us: exchange_shards(): lax.ppermute(terms[i], 'seq', [(j, j ^ hops[i]) for j in range(n)])]
    pallas_call x5 -> x6, Pallas kernels: 3.46 us -> 3.63 us  [call(): pl.pallas_call(kernel, out_shape=out_shape, in_specs=specs if specs is no...]
  transfers between devices with their start and end apart: 8 -> 12, of which waited for: 3 -> 7; matrix products, arithmetic and copies ran while one was open for 0% -> 0% of each run, Pallas kernels for 2% -> 5%
where the time goes in v5:
time: 28.8 us; the launch traced here: 28.7 us
  starting transfers between devices  17.2 us (60%)
  waiting for transfers between devices  7.09 us (25%)
  Pallas kernels  3.63 us (13%)
  between operations  0.71 us (2%)
    ppermute x7, starting transfers between devices, exchange_shards(): blocks.append(lax.ppermute(sent[k], 'seq', [(j, j ^ k) for j in range(n)]))  13.1 us
    ppermute x7, waiting for transfers between devices, exchange_shards(): blocks.append(lax.ppermute(sent[k], 'seq', [(j, j ^ k) for j in range(n)]))  3.9 us
    pallas_call x6, Pallas kernels, call(): pl.pallas_call(kernel, out_shape=out_shape, in_specs=specs if specs is no...  3.63 us
    ppermute x3, starting transfers between devices, exchange_shards(): lax.ppermute(terms[i], 'seq', [(j, j ^ hops[i]) for j in range(n)])  3.55 us
    ppermute x3, waiting for transfers between devices, exchange_shards(): lax.ppermute(terms[i], 'seq', [(j, j ^ hops[i]) for j in range(n)])  2.94 us
    ppermute x2, starting transfers between devices, exchange_shards(): swap = lambda a: lax.ppermute(a, 'head', [(c, c ^ 1) for c in range(cores)])  0.63 us
  transfers between devices with their start and end apart: 12, of which 7 were waited for; matrix products, arithmetic and copies ran while one was open for 0% of the time, Pallas kernels for 5%

profile of v5, /device:TPU:0, one launch (start us, length us, event | category | flops | bytes accessed | tf_op | source)
XLA Modules:
  0.0 28.7 jit_solution(17060989284327887040)
XLA Ops:
  0.0 1.6 %shard_map.91 = (bf16[400,128]{1,0:T(8,128)(2,1)S(1)}, bf16[400,128]{1,0:T(8,128)(2,1)S(1)}, bf16[400,128]{1,0:T(8,128)(2,1)S(1)}, bf16[400,128]{1,0:T(8,128)(2,...) custom-call(bf16[16,1024]{1,0:T(8,128)(2,1)} %refs_0_.1, ...), custom_call_target="tpu_custom_call" | custom-call | tf_op jit(solution)/shard_map/pallas_call | solution.py:195
  1.6 4.1 %collective-permute-start.1 = (bf16[240,128]{1,0:T(8,128)(2,1)S(1)}, bf16[240,128]{1,0:T(8,128)(2,1)S(1)}, u32[]{:S(2)}, u32[]{:S(2)}) collective-permute-start(bf16[240,128]{1,0:T(8,128)(2,1)S(1)} %get-tuple-element.21), channel_id=1, source_target_pairs={{0,8},{2,10},{4,12},{6,14},{8,0},{10,2},{12,4},{14,6},{1,9},{3,11}... | collective-permute-start | bytes 184328 | tf_op jit(solution)/shard_map/ppermute | solution.py:229
  5.7 2.3 %collective-permute-start.3 = (bf16[240,128]{1,0:T(8,128)(2,1)S(1)}, bf16[240,128]{1,0:T(8,128)(2,1)S(1)}, u32[]{:S(2)}, u32[]{:S(2)}) collective-permute-start(bf16[240,128]{1,0:T(8,128)(2,1)S(1)} %get-tuple-element.23), channel_id=1, source_target_pairs={{0,14},{2,12},{4,10},{6,8},{8,6},{10,4},{12,2},{14,0},{1,15},{3,13... | collective-permute-start | bytes 184328 | tf_op jit(solution)/shard_map/ppermute | solution.py:229
  7.9 0.0 collective-permute-start
  8.0 0.8 %collective-permute-start.2 = (bf16[400,128]{1,0:T(8,128)(2,1)S(1)}, bf16[400,128]{1,0:T(8,128)(2,1)S(1)}, u32[]{:S(2)}, u32[]{:S(2)}) collective-permute-start(bf16[400,128]{1,0:T(8,128)(2,1)S(1)} %get-tuple-element.22), channel_id=1, source_target_pairs={{0,2},{2,0},{4,6},{6,4},{8,10},{10,8},{12,14},{14,12},{1,3},{3,1},... | collective-permute-start | bytes 307208 | tf_op jit(solution)/shard_map/ppermute | solution.py:229
  8.7 2.7 %collective-permute-start.4 = (bf16[400,128]{1,0:T(8,128)(2,1)S(1)}, bf16[400,128]{1,0:T(8,128)(2,1)S(1)}, u32[]{:S(2)}, u32[]{:S(2)}) collective-permute-start(bf16[400,128]{1,0:T(8,128)(2,1)S(1)} %get-tuple-element.24), channel_id=1, source_target_pairs={{0,6},{2,4},{4,2},{6,0},{8,14},{10,12},{12,10},{14,8},{1,7},{3,5},... | collective-permute-start | bytes 307208 | tf_op jit(solution)/shard_map/ppermute | solution.py:229
  11.4 0.0 collective-permute-done.1.refs_2_
  11.4 1.7 %collective-permute-start.5 = (bf16[240,128]{1,0:T(8,128)(2,1)S(1)}, bf16[240,128]{1,0:T(8,128)(2,1)S(1)}, u32[]{:S(2)}, u32[]{:S(2)}) collective-permute-start(bf16[240,128]{1,0:T(8,128)(2,1)S(1)} %get-tuple-element.25), channel_id=1, source_target_pairs={{0,10},{2,8},{4,14},{6,12},{8,2},{10,0},{12,6},{14,4},{1,11},{3,9}... | collective-permute-start | bytes 184328 | tf_op jit(solution)/shard_map/ppermute | solution.py:229
  13.1 0.0 collective-permute-done.3.refs_4_
  13.1 1.5 %collective-permute-start.6 = (bf16[240,128]{1,0:T(8,128)(2,1)S(1)}, bf16[240,128]{1,0:T(8,128)(2,1)S(1)}, u32[]{:S(2)}, u32[]{:S(2)}) collective-permute-start(bf16[240,128]{1,0:T(8,128)(2,1)S(1)} %get-tuple-element.26), channel_id=1, source_target_pairs={{0,12},{2,14},{4,8},{6,10},{8,4},{10,6},{12,0},{14,2},{1,13},{3,15... | collective-permute-start | bytes 184328 | tf_op jit(solution)/shard_map/ppermute | solution.py:229
  15.3 3.4 %collective-permute-done.5.refs_6_ = bf16[240,128]{1,0:T(8,128)(2,1)S(1)} collective-permute-done((bf16[240,128]{1,0:T(8,128)(2,1)S(1)}, bf16[240,128]{1,0:T(8,128)(2,1)S(1)}, u32[]{:S(2)}, u32[]{:S(2)}) %collective-permute-start.5) | collective-permute-done | bytes 61472 | tf_op jit(solution)/shard_map/ppermute | solution.py:229
  18.7 0.5 %collective-permute-done.6.refs_7_ = bf16[240,128]{1,0:T(8,128)(2,1)S(1)} collective-permute-done((bf16[240,128]{1,0:T(8,128)(2,1)S(1)}, bf16[240,128]{1,0:T(8,128)(2,1)S(1)}, u32[]{:S(2)}, u32[]{:S(2)}) %collective-permute-start.6) | collective-permute-done | bytes 61472 | tf_op jit(solution)/shard_map/ppermute | solution.py:229
  19.2 0.0 collective-permute-done.refs_1_
  19.2 0.0 collective-permute-done.2.refs_3_
  19.2 0.0 collective-permute-done.4.refs_5_
  19.2 0.1 collective-permute-start.8
  19.3 0.7 %shard_map.92.big = f32[128,64]{1,0:T(8,128)S(1)} custom-call(bf16[400,128]{1,0:T(8,128)(2,1)S(1)} %get-tuple-element.19.refs_0_, bf16[400,128]{1,0:T(8,128)(2,1)S(1)} %collective-permute-done.refs_1_, bf16[240,128]{1,0:T(8,128)(2,1)S(1)} %collective-permute-done.1.refs_2_, bf16[400,128]{1,0:T(8,128)(2,1)S(1)} %collective-permute-done.2.refs_3_, ...), custom_call_target="tpu_custom_call" | custom-call | flops 1000000000 | bytes 1000000 | tf_op jit(solution)/shard_map/pallas_call | solution.py:195
  20.0 0.6 %collective-permute-start.7 = (f32[128,64]{1,0:T(8,128)S(1)}, f32[128,64]{1,0:T(8,128)S(1)}, u32[]{:S(2)}, u32[]{:S(2)}) collective-permute-start(f32[128,64]{1,0:T(8,128)S(1)} %shard_map.92.big), channel_id=1, source_target_pairs={{0,1},{1,0},{2,3},{3,2},{4,5},{5,4},{6,7},{7,6},{8,9},{9,8},{10,11... | collective-permute-start | bytes 98312 | tf_op jit(solution)/shard_map/ppermute | solution.py:239
  20.6 0.1 collective-permute-done.8.refs_8_
  20.6 0.6 %shard_map.94.small = f32[128,64]{1,0:T(8,128)S(1)} custom-call(bf16[400,128]{1,0:T(8,128)(2,1)S(1)} %get-tuple-element.19.refs_0_, bf16[400,128]{1,0:T(8,128)(2,1)S(1)} %collective-permute-done.refs_1_, bf16[240,128]{1,0:T(8,128)(2,1)S(1)} %collective-permute-done.1.refs_2_, bf16[400,128]{1,0:T(8,128)(2,1)S(1)} %collective-permute-done.2.refs_3_, ...), custom_call_target="tpu_custom_call" | custom-call | flops 1000000000 | bytes 1000000 | tf_op jit(solution)/shard_map/pallas_call | solution.py:195
  21.3 0.2 collective-permute-done.7.other_big
  21.5 0.1 shard_map.95
  21.6 1.5 %collective-permute-start.10 = (f32[16,128]{1,0:T(8,128)S(1)}, f32[16,128]{1,0:T(8,128)S(1)}, u32[]{:S(2)}, u32[]{:S(2)}) collective-permute-start(f32[16,128]{1,0:T(8,128)S(1)} %get-tuple-element.31), channel_id=1, source_target_pairs={{0,2},{2,0},{4,6},{6,4},{8,10},{10,8},{12,14},{14,12},{1,3},{3,1},... | collective-permute-start | bytes 24584 | tf_op jit(solution)/shard_map/ppermute | solution.py:263
  23.1 1.4 %collective-permute-start.11 = (f32[16,128]{1,0:T(8,128)S(1)}, f32[16,128]{1,0:T(8,128)S(1)}, u32[]{:S(2)}, u32[]{:S(2)}) collective-permute-start(f32[16,128]{1,0:T(8,128)S(1)} %get-tuple-element.32), channel_id=1, source_target_pairs={{0,6},{2,4},{4,2},{6,0},{8,14},{10,12},{12,10},{14,8},{1,7},{3,5},... | collective-permute-start | bytes 24584 | tf_op jit(solution)/shard_map/ppermute | solution.py:263
  24.4 0.7 %collective-permute-start.9 = (f32[16,128]{1,0:T(8,128)S(1)}, f32[16,128]{1,0:T(8,128)S(1)}, u32[]{:S(2)}, u32[]{:S(2)}) collective-permute-start(f32[16,128]{1,0:T(8,128)S(1)} %get-tuple-element.30), channel_id=1, source_target_pairs={{0,4},{2,6},{4,0},{6,2},{8,12},{10,14},{12,8},{14,10},{1,5},{3,7},... | collective-permute-start | bytes 24584 | tf_op jit(solution)/shard_map/ppermute | solution.py:263
  25.1 0.2 collective-permute-done.10.refs_2_
  25.3 2.3 %collective-permute-done.11.refs_3_ = f32[16,128]{1,0:T(8,128)S(1)} collective-permute-done((f32[16,128]{1,0:T(8,128)S(1)}, f32[16,128]{1,0:T(8,128)S(1)}, u32[]{:S(2)}, u32[]{:S(2)}) %collective-permute-start.11) | collective-permute-done | bytes 8224 | tf_op jit(solution)/shard_map/ppermute | solution.py:263
  27.6 0.5 %collective-permute-done.9.refs_1_ = f32[16,128]{1,0:T(8,128)S(1)} collective-permute-done((f32[16,128]{1,0:T(8,128)S(1)}, f32[16,128]{1,0:T(8,128)S(1)}, u32[]{:S(2)}, u32[]{:S(2)}) %collective-permute-start.9) | collective-permute-done | bytes 8224 | tf_op jit(solution)/shard_map/ppermute | solution.py:263
  28.1 0.6 %shard_map.96 = f32[16,128]{1,0:T(8,128)} custom-call(f32[16,128]{1,0:T(8,128)S(1)} %get-tuple-element.29.refs_0_, f32[16,128]{1,0:T(8,128)S(1)} %collective-permute-done.9.refs_1_, f32[16,128]{1,0:T(8,128)S(1)} %collective-permute-done.10.refs_2_, f32[16,128]{1,0:T(8,128)S(1)} %collective-permute-done.11.refs_3_), custom_call_target="tpu_custom_call" | custom-call | tf_op jit(solution)/shard_map/pallas_call | solution.py:195
  (1 shorter events, 0.0 us)
Async XLA Ops:
  1.6 9.9 %collective-permute-start.1 = (bf16[240,128]{1,0:T(8,128)(2,1)S(1)}, bf16[240,128]{1,0:T(8,128)(2,1)S(1)}, u32[]{:S(2)}, u32[]{:S(2)}) collective-permute-start(bf16[240,128]{1,0:T(8,128)(2,1)S(1)} %get-tuple-element.21), channel_id=1, source_target_pairs={{0,8},{2,10},{4,12},{6,14},{8,0},{10,2},{12,4},{14,6},{1,9},{3,11}... | collective-permute-start | bytes 184328 | tf_op jit(solution)/shard_map/ppermute | solution.py:229
  5.7 7.4 %collective-permute-start.3 = (bf16[240,128]{1,0:T(8,128)(2,1)S(1)}, bf16[240,128]{1,0:T(8,128)(2,1)S(1)}, u32[]{:S(2)}, u32[]{:S(2)}) collective-permute-start(bf16[240,128]{1,0:T(8,128)(2,1)S(1)} %get-tuple-element.23), channel_id=1, source_target_pairs={{0,14},{2,12},{4,10},{6,8},{8,6},{10,4},{12,2},{14,0},{1,15},{3,13... | collective-permute-start | bytes 184328 | tf_op jit(solution)/shard_map/ppermute | solution.py:229
  7.9 11.2 %collective-permute-start = (bf16[400,128]{1,0:T(8,128)(2,1)S(1)}, bf16[400,128]{1,0:T(8,128)(2,1)S(1)}, u32[]{:S(2)}, u32[]{:S(2)}) collective-permute-start(bf16[400,128]{1,0:T(8,128)(2,1)S(1)} %get-tuple-element.20), channel_id=1, source_target_pairs={{0,4},{2,6},{4,0},{6,2},{8,12},{10,14},{12,8},{14,10},{1,5},{3,7},... | collective-permute-start | bytes 307208 | tf_op jit(solution)/shard_map/ppermute | solution.py:229
  8.0 11.2 %collective-permute-start.2 = (bf16[400,128]{1,0:T(8,128)(2,1)S(1)}, bf16[400,128]{1,0:T(8,128)(2,1)S(1)}, u32[]{:S(2)}, u32[]{:S(2)}) collective-permute-start(bf16[400,128]{1,0:T(8,128)(2,1)S(1)} %get-tuple-element.22), channel_id=1, source_target_pairs={{0,2},{2,0},{4,6},{6,4},{8,10},{10,8},{12,14},{14,12},{1,3},{3,1},... | collective-permute-start | bytes 307208 | tf_op jit(solution)/shard_map/ppermute | solution.py:229
  8.7 10.5 %collective-permute-start.4 = (bf16[400,128]{1,0:T(8,128)(2,1)S(1)}, bf16[400,128]{1,0:T(8,128)(2,1)S(1)}, u32[]{:S(2)}, u32[]{:S(2)}) collective-permute-start(bf16[400,128]{1,0:T(8,128)(2,1)S(1)} %get-tuple-element.24), channel_id=1, source_target_pairs={{0,6},{2,4},{4,2},{6,0},{8,14},{10,12},{12,10},{14,8},{1,7},{3,5},... | collective-permute-start | bytes 307208 | tf_op jit(solution)/shard_map/ppermute | solution.py:229
  11.4 7.2 %collective-permute-start.5 = (bf16[240,128]{1,0:T(8,128)(2,1)S(1)}, bf16[240,128]{1,0:T(8,128)(2,1)S(1)}, u32[]{:S(2)}, u32[]{:S(2)}) collective-permute-start(bf16[240,128]{1,0:T(8,128)(2,1)S(1)} %get-tuple-element.25), channel_id=1, source_target_pairs={{0,10},{2,8},{4,14},{6,12},{8,2},{10,0},{12,6},{14,4},{1,11},{3,9}... | collective-permute-start | bytes 184328 | tf_op jit(solution)/shard_map/ppermute | solution.py:229
  13.1 6.1 %collective-permute-start.6 = (bf16[240,128]{1,0:T(8,128)(2,1)S(1)}, bf16[240,128]{1,0:T(8,128)(2,1)S(1)}, u32[]{:S(2)}, u32[]{:S(2)}) collective-permute-start(bf16[240,128]{1,0:T(8,128)(2,1)S(1)} %get-tuple-element.26), channel_id=1, source_target_pairs={{0,12},{2,14},{4,8},{6,10},{8,4},{10,6},{12,0},{14,2},{1,13},{3,15... | collective-permute-start | bytes 184328 | tf_op jit(solution)/shard_map/ppermute | solution.py:229
  19.2 1.4 %collective-permute-start.8 = (bf16[512,128]{1,0:T(8,128)(2,1)S(1)}, bf16[512,128]{1,0:T(8,128)(2,1)S(1)}, u32[]{:S(2)}, u32[]{:S(2)}) collective-permute-start(bf16[512,128]{1,0:T(8,128)(2,1)S(1)} %get-tuple-element.27), channel_id=1, source_target_pairs={{0,1},{1,0},{2,3},{3,2},{4,5},{5,4},{6,7},{7,6},{8,9},{9,8},{10,11... | collective-permute-start | bytes 393224 | tf_op jit(solution)/shard_map/ppermute | solution.py:239
  20.0 1.5 %collective-permute-start.7 = (f32[128,64]{1,0:T(8,128)S(1)}, f32[128,64]{1,0:T(8,128)S(1)}, u32[]{:S(2)}, u32[]{:S(2)}) collective-permute-start(f32[128,64]{1,0:T(8,128)S(1)} %shard_map.92.big), channel_id=1, source_target_pairs={{0,1},{1,0},{2,3},{3,2},{4,5},{5,4},{6,7},{7,6},{8,9},{9,8},{10,11... | collective-permute-start | bytes 98312 | tf_op jit(solution)/shard_map/ppermute | solution.py:239
  21.6 3.7 %collective-permute-start.10 = (f32[16,128]{1,0:T(8,128)S(1)}, f32[16,128]{1,0:T(8,128)S(1)}, u32[]{:S(2)}, u32[]{:S(2)}) collective-permute-start(f32[16,128]{1,0:T(8,128)S(1)} %get-tuple-element.31), channel_id=1, source_target_pairs={{0,2},{2,0},{4,6},{6,4},{8,10},{10,8},{12,14},{14,12},{1,3},{3,1},... | collective-permute-start | bytes 24584 | tf_op jit(solution)/shard_map/ppermute | solution.py:263
  23.1 4.5 %collective-permute-start.11 = (f32[16,128]{1,0:T(8,128)S(1)}, f32[16,128]{1,0:T(8,128)S(1)}, u32[]{:S(2)}, u32[]{:S(2)}) collective-permute-start(f32[16,128]{1,0:T(8,128)S(1)} %get-tuple-element.32), channel_id=1, source_target_pairs={{0,6},{2,4},{4,2},{6,0},{8,14},{10,12},{12,10},{14,8},{1,7},{3,5},... | collective-permute-start | bytes 24584 | tf_op jit(solution)/shard_map/ppermute | solution.py:263
  24.4 3.7 %collective-permute-start.9 = (f32[16,128]{1,0:T(8,128)S(1)}, f32[16,128]{1,0:T(8,128)S(1)}, u32[]{:S(2)}, u32[]{:S(2)}) collective-permute-start(f32[16,128]{1,0:T(8,128)S(1)} %get-tuple-element.30), channel_id=1, source_target_pairs={{0,4},{2,6},{4,0},{6,2},{8,12},{10,14},{12,8},{14,10},{1,5},{3,7},... | collective-permute-start | bytes 24584 | tf_op jit(solution)/shard_map/ppermute | solution.py:263

commit v6 on v5

--- a/solution.py
+++ b/solution.py
@@ -108,13 +108,22 @@
             at += last - first
 
 
-def attend_head(queries, keys, values):
-    scores = lax.dot_general(queries, keys, NT, preferred_element_type=F32)
-    scores = scores * (1.0 / math.sqrt(DH))
-    probs = jnp.exp(scores - jnp.max(scores, axis=1, keepdims=True))
-    totals = jnp.sum(probs, axis=1, keepdims=True)
-    out = jnp.dot(probs.astype(BF16), values, preferred_element_type=F32)
-    return out / totals
+def attend_heads(heads, lat):
+    scale = math.log2(math.e) / math.sqrt(DH)
+    scores = [
+        lax.dot_general(keys, queries, NT, preferred_element_type=F32)
+        for queries, keys, _ in heads
+    ]
+    weights, totals = [], []
+    for x in scores:
+        probs = jnp.exp2((x - jnp.max(x, axis=0, keepdims=True)) * scale)
+        totals.append(jnp.sum(probs, axis=0, keepdims=True))
+        weights.append(probs.astype(BF16))
+    out = None
+    for (_, _, values), weight, total in zip(heads, weights, totals):
+        part = jnp.dot(values, weight, preferred_element_type=F32) / total
+        out = part if out is None else out + part
+    return out
 
 
 def big_kernel(order, near, group, tokens, lat, rows, *refs):
@@ -124,23 +133,24 @@
     read = lambda some, first: jnp.concatenate(
         [b[pl.ds(first, tokens), :] for b in some], axis=0
     )
-    total = None
-    for g in range(group):
-        if g % 2 == 0:
-            values = read(blocks, rows["vr"] + g // 2 * tokens)
-        part = attend_head(
-            read(here, rows["q"] + g * tokens),
-            read(blocks, rows["k"] + g * tokens),
-            values[:, g % 2 * lat : (g % 2 + 1) * lat],
-        )
-        total = part if total is None else total + part
-    out[:, :] = total
+    values = [read(blocks, rows["vr"] + p * tokens).T for p in range(group // 2)]
+    out[:, :] = attend_heads(
+        [
+            (
+                read(here, rows["q"] + g * tokens),
+                read(blocks, rows["k"] + g * tokens),
+                values[g // 2][g % 2 * lat : (g % 2 + 1) * lat, :],
+            )
+            for g in range(group)
+        ],
+        lat,
+    )
 
 
 def small_kernel(order, near, small_group, tokens, count, lat, rows, *refs):
     n = len(order)
     blocks, theirs, out = refs[:n], refs[n], refs[n + 1]
-    core = lax.axis_index("head")
+    first_core = lax.axis_index("head") == 0
     at = 0
     found = {name: [] for name in ("sk", "svr", "sq")}
     for block, k in zip(blocks, order):
@@ -154,29 +164,31 @@
             own = block[pl.ds(rows[name], size), :]
             found[name].append((own, theirs[pl.ds(at, size), :]))
             at += size
-
-    def read(name, first):
-        sides = [[p[side][first : first + count] for p in found[name]] for side in (0, 1)]
-        return jnp.concatenate(sides[0] + sides[1], axis=0)
-
-    values = read("svr", 0)
-    total = None
+    values = jnp.concatenate([p[side] for side in (0, 1) for p in found["svr"]], axis=0).T
+    heads = []
     for g in range(small_group):
-        part = attend_head(
-            read("sq", g * count), read("sk", g * count), values[:, g * lat : (g + 1) * lat]
+        head = slice(g * count, (g + 1) * count)
+        keys = [p[side][head] for side in (0, 1) for p in found["sk"]]
+        queries = []
+        for own, other in found["sq"]:
+            queries.append(jnp.where(first_core, own[head], other[head]))
+            queries.append(jnp.where(first_core, other[head], own[head]))
+        heads.append(
+            (
+                jnp.concatenate(queries, axis=0),
+                jnp.concatenate(keys, axis=0),
+                values[g * lat : (g + 1) * lat, :],
+            )
         )
-        total = part if total is None else total + part
-    for i in range(near):
-        for side, whose in ((core, i), (1 - core, near + i)):
-            part = pl.ds(pl.multiple_of(i * tokens + side * count, count), count)
-            out[part, :] = total[whose * count : (whose + 1) * count, :]
-
-
-def blend_kernel(near, tokens, big, other_big, small, guidance, *refs):
+    out[:, :] = attend_heads(heads, lat)
+
+
+def blend_kernel(near, tokens, big, other_big, small, weight, *refs):
     outs, latent = refs[:near], refs[near]
-    lat = big.shape[1]
-    weight = guidance[:1, :lat]
-    latent[:, :lat] = (1.0 + weight) * (big[:, :] + other_big[:, :]) - weight * small[:, :]
+    lat, width = big.shape
+    scale = weight[:1, :1]
+    blended = (1.0 + scale) * (big[:, :] + other_big[:, :]) - scale * small[:, :]
+    latent[:, :lat] = blended.T
     for i in range(near):
         even = latent[pl.ds(i * tokens, tokens // 2, stride=2), :lat]
         odd = latent[pl.ds(i * tokens + 1, tokens // 2, stride=2), :lat]
@@ -240,14 +252,14 @@
     theirs = swap(ours)
     big = call(
         functools.partial(big_kernel, order, near, group, tokens, lat, rows),
-        shape(near * tokens, lat, dtype=F32),
+        shape(lat, near * tokens, dtype=F32),
         blocks,
         cost=pl.CostEstimate(flops=10**9, bytes_accessed=10**6, transcendentals=10**5),
     )
     other_big = swap(big)
     small = call(
         functools.partial(small_kernel, order, near, small_group, tokens, count, lat, rows),
-        shape(near * tokens, lat, dtype=F32),
+        shape(lat, near * tokens, dtype=F32),
         (*blocks, theirs),
         cost=pl.CostEstimate(flops=10**9, bytes_accessed=10**6, transcendentals=10**5),
     )
@@ -259,7 +271,7 @@
         scratch=[pltpu.VMEM((near * tokens, DH), F32)],
     )
     sums = [terms[0]]
-    for i in range(1, near):
+    for i in (3, 2, 1):
         sums.append(lax.ppermute(terms[i], "seq", [(j, j ^ hops[i]) for j in range(n)]))
     return call(sum_kernel, shape(tokens // 2, 2 * lat, dtype=F32), sums)
 

time: 28.8 us -> 28.2 us (0.979)
  Pallas kernels: 3.63 us -> 3.24 us
    ppermute x3, waiting for transfers between devices: 2.94 us -> 2.5 us  [exchange_shards(): lax.ppermute(terms[i], 'seq', [(j, j ^ hops[i]) for j in range(n)])]
    pallas_call x6, Pallas kernels: 3.63 us -> 3.24 us  [call(): pl.pallas_call(kernel, out_shape=out_shape, in_specs=specs if specs is no...]
  transfers between devices with their start and end apart: 12 -> 12, of which waited for: 7 -> 7; matrix products, arithmetic and copies ran while one was open for 0% -> 0% of each run, Pallas kernels for 5% -> 3%
where the time goes in v6:
time: 28.2 us; the launch traced here: 28 us
  starting transfers between devices  17.2 us (61%)
  waiting for transfers between devices  6.86 us (24%)
  Pallas kernels  3.24 us (11%)
  between operations  0.7 us (2%)
    ppermute x7, starting transfers between devices, exchange_shards(): blocks.append(lax.ppermute(sent[k], 'seq', [(j, j ^ k) for j in range(n)]))  13.1 us
    ppermute x7, waiting for transfers between devices, exchange_shards(): blocks.append(lax.ppermute(sent[k], 'seq', [(j, j ^ k) for j in range(n)]))  3.9 us
    ppermute x3, starting transfers between devices, exchange_shards(): lax.ppermute(terms[i], 'seq', [(j, j ^ hops[i]) for j in range(n)])  3.54 us
    pallas_call x6, Pallas kernels, call(): pl.pallas_call(kernel, out_shape=out_shape, in_specs=specs if specs is no...  3.24 us
    ppermute x3, waiting for transfers between devices, exchange_shards(): lax.ppermute(terms[i], 'seq', [(j, j ^ hops[i]) for j in range(n)])  2.5 us
    ppermute x2, starting transfers between devices, exchange_shards(): swap = lambda a: lax.ppermute(a, 'head', [(c, c ^ 1) for c in range(cores)])  0.63 us
  transfers between devices with their start and end apart: 12, of which 7 were waited for; matrix products, arithmetic and copies ran while one was open for 0% of the time, Pallas kernels for 3%

profile of v6, /device:TPU:0, one launch (start us, length us, event | category | flops | bytes accessed | tf_op | source)
XLA Modules:
  0.0 28.0 jit_solution(8531565923389466676)
XLA Ops:
  0.0 1.6 %shard_map.91 = (bf16[400,128]{1,0:T(8,128)(2,1)S(1)}, bf16[400,128]{1,0:T(8,128)(2,1)S(1)}, bf16[400,128]{1,0:T(8,128)(2,1)S(1)}, bf16[400,128]{1,0:T(8,128)(2,...) custom-call(bf16[16,1024]{1,0:T(8,128)(2,1)} %refs_0_.1, ...), custom_call_target="tpu_custom_call" | custom-call | tf_op jit(solution)/shard_map/pallas_call | solution.py:207
  1.6 4.1 %collective-permute-start.1 = (bf16[240,128]{1,0:T(8,128)(2,1)S(1)}, bf16[240,128]{1,0:T(8,128)(2,1)S(1)}, u32[]{:S(2)}, u32[]{:S(2)}) collective-permute-start(bf16[240,128]{1,0:T(8,128)(2,1)S(1)} %get-tuple-element.21), channel_id=1, source_target_pairs={{0,8},{2,10},{4,12},{6,14},{8,0},{10,2},{12,4},{14,6},{1,9},{3,11}... | collective-permute-start | bytes 184328 | tf_op jit(solution)/shard_map/ppermute | solution.py:241
  5.7 2.3 %collective-permute-start.3 = (bf16[240,128]{1,0:T(8,128)(2,1)S(1)}, bf16[240,128]{1,0:T(8,128)(2,1)S(1)}, u32[]{:S(2)}, u32[]{:S(2)}) collective-permute-start(bf16[240,128]{1,0:T(8,128)(2,1)S(1)} %get-tuple-element.23), channel_id=1, source_target_pairs={{0,14},{2,12},{4,10},{6,8},{8,6},{10,4},{12,2},{14,0},{1,15},{3,13... | collective-permute-start | bytes 184328 | tf_op jit(solution)/shard_map/ppermute | solution.py:241
  7.9 0.0 collective-permute-start
  8.0 0.8 %collective-permute-start.2 = (bf16[400,128]{1,0:T(8,128)(2,1)S(1)}, bf16[400,128]{1,0:T(8,128)(2,1)S(1)}, u32[]{:S(2)}, u32[]{:S(2)}) collective-permute-start(bf16[400,128]{1,0:T(8,128)(2,1)S(1)} %get-tuple-element.22), channel_id=1, source_target_pairs={{0,2},{2,0},{4,6},{6,4},{8,10},{10,8},{12,14},{14,12},{1,3},{3,1},... | collective-permute-start | bytes 307208 | tf_op jit(solution)/shard_map/ppermute | solution.py:241
  8.7 2.7 %collective-permute-start.4 = (bf16[400,128]{1,0:T(8,128)(2,1)S(1)}, bf16[400,128]{1,0:T(8,128)(2,1)S(1)}, u32[]{:S(2)}, u32[]{:S(2)}) collective-permute-start(bf16[400,128]{1,0:T(8,128)(2,1)S(1)} %get-tuple-element.24), channel_id=1, source_target_pairs={{0,6},{2,4},{4,2},{6,0},{8,14},{10,12},{12,10},{14,8},{1,7},{3,5},... | collective-permute-start | bytes 307208 | tf_op jit(solution)/shard_map/ppermute | solution.py:241
  11.4 0.0 collective-permute-done.1.refs_2_
  11.4 1.7 %collective-permute-start.5 = (bf16[240,128]{1,0:T(8,128)(2,1)S(1)}, bf16[240,128]{1,0:T(8,128)(2,1)S(1)}, u32[]{:S(2)}, u32[]{:S(2)}) collective-permute-start(bf16[240,128]{1,0:T(8,128)(2,1)S(1)} %get-tuple-element.25), channel_id=1, source_target_pairs={{0,10},{2,8},{4,14},{6,12},{8,2},{10,0},{12,6},{14,4},{1,11},{3,9}... | collective-permute-start | bytes 184328 | tf_op jit(solution)/shard_map/ppermute | solution.py:241
  13.1 0.0 collective-permute-done.3.refs_4_
  13.1 1.5 %collective-permute-start.6 = (bf16[240,128]{1,0:T(8,128)(2,1)S(1)}, bf16[240,128]{1,0:T(8,128)(2,1)S(1)}, u32[]{:S(2)}, u32[]{:S(2)}) collective-permute-start(bf16[240,128]{1,0:T(8,128)(2,1)S(1)} %get-tuple-element.26), channel_id=1, source_target_pairs={{0,12},{2,14},{4,8},{6,10},{8,4},{10,6},{12,0},{14,2},{1,13},{3,15... | collective-permute-start | bytes 184328 | tf_op jit(solution)/shard_map/ppermute | solution.py:241
  15.3 3.4 %collective-permute-done.5.refs_6_ = bf16[240,128]{1,0:T(8,128)(2,1)S(1)} collective-permute-done((bf16[240,128]{1,0:T(8,128)(2,1)S(1)}, bf16[240,128]{1,0:T(8,128)(2,1)S(1)}, u32[]{:S(2)}, u32[]{:S(2)}) %collective-permute-start.5) | collective-permute-done | bytes 61472 | tf_op jit(solution)/shard_map/ppermute | solution.py:241
  18.7 0.5 %collective-permute-done.6.refs_7_ = bf16[240,128]{1,0:T(8,128)(2,1)S(1)} collective-permute-done((bf16[240,128]{1,0:T(8,128)(2,1)S(1)}, bf16[240,128]{1,0:T(8,128)(2,1)S(1)}, u32[]{:S(2)}, u32[]{:S(2)}) %collective-permute-start.6) | collective-permute-done | bytes 61472 | tf_op jit(solution)/shard_map/ppermute | solution.py:241
  19.2 0.0 collective-permute-done.refs_1_
  19.2 0.0 collective-permute-done.2.refs_3_
  19.2 0.0 collective-permute-done.4.refs_5_
  19.2 0.1 collective-permute-start.8
  19.3 0.5 %shard_map.92.big = f32[64,128]{1,0:T(8,128)S(1)} custom-call(bf16[400,128]{1,0:T(8,128)(2,1)S(1)} %get-tuple-element.19.refs_0_, bf16[400,128]{1,0:T(8,128)(2,1)S(1)} %collective-permute-done.refs_1_, bf16[240,128]{1,0:T(8,128)(2,1)S(1)} %collective-permute-done.1.refs_2_, bf16[400,128]{1,0:T(8,128)(2,1)S(1)} %collective-permute-done.2.refs_3_, ...), custom_call_target="tpu_custom_call" | custom-call | flops 1000000000 | bytes 1000000 | tf_op jit(solution)/shard_map/pallas_call | solution.py:207
  19.8 0.6 %collective-permute-start.7 = (f32[64,128]{1,0:T(8,128)S(1)}, f32[64,128]{1,0:T(8,128)S(1)}, u32[]{:S(2)}, u32[]{:S(2)}) collective-permute-start(f32[64,128]{1,0:T(8,128)S(1)} %shard_map.92.big), channel_id=1, source_target_pairs={{0,1},{1,0},{2,3},{3,2},{4,5},{5,4},{6,7},{7,6},{8,9},{9,8},{10,11... | collective-permute-start | bytes 98312 | tf_op jit(solution)/shard_map/ppermute | solution.py:251
  20.3 0.3 %collective-permute-done.8.refs_8_ = bf16[512,128]{1,0:T(8,128)(2,1)S(1)} collective-permute-done((bf16[512,128]{1,0:T(8,128)(2,1)S(1)}, bf16[512,128]{1,0:T(8,128)(2,1)S(1)}, u32[]{:S(2)}, u32[]{:S(2)}) %collective-permute-start.8) | collective-permute-done | bytes 131104 | tf_op jit(solution)/shard_map/ppermute | solution.py:251
  20.6 0.4 %shard_map.94.small = f32[64,128]{1,0:T(8,128)S(1)} custom-call(bf16[400,128]{1,0:T(8,128)(2,1)S(1)} %get-tuple-element.19.refs_0_, bf16[400,128]{1,0:T(8,128)(2,1)S(1)} %collective-permute-done.refs_1_, bf16[240,128]{1,0:T(8,128)(2,1)S(1)} %collective-permute-done.1.refs_2_, bf16[400,128]{1,0:T(8,128)(2,1)S(1)} %collective-permute-done.2.refs_3_, ...), custom_call_target="tpu_custom_call" | custom-call | flops 1000000000 | bytes 1000000 | tf_op jit(solution)/shard_map/pallas_call | solution.py:207
  21.0 0.2 collective-permute-done.7.other_big
  21.2 0.2 shard_map.95
  21.4 1.5 %collective-permute-start.10 = (f32[16,128]{1,0:T(8,128)S(1)}, f32[16,128]{1,0:T(8,128)S(1)}, u32[]{:S(2)}, u32[]{:S(2)}) collective-permute-start(f32[16,128]{1,0:T(8,128)S(1)} %get-tuple-element.31), channel_id=1, source_target_pairs={{0,2},{2,0},{4,6},{6,4},{8,10},{10,8},{12,14},{14,12},{1,3},{3,1},... | collective-permute-start | bytes 24584 | tf_op jit(solution)/shard_map/ppermute | solution.py:275
  22.9 0.0 collective-permute-start.11
  22.9 2.0 %collective-permute-start.9 = (f32[16,128]{1,0:T(8,128)S(1)}, f32[16,128]{1,0:T(8,128)S(1)}, u32[]{:S(2)}, u32[]{:S(2)}) collective-permute-start(f32[16,128]{1,0:T(8,128)S(1)} %get-tuple-element.30), channel_id=1, source_target_pairs={{0,6},{2,4},{4,2},{6,0},{8,14},{10,12},{12,10},{14,8},{1,7},{3,5},... | collective-permute-start | bytes 24584 | tf_op jit(solution)/shard_map/ppermute | solution.py:275
  24.9 0.2 collective-permute-done.10.refs_2_
  25.1 1.4 %collective-permute-done.11.refs_3_ = f32[16,128]{1,0:T(8,128)S(1)} collective-permute-done((f32[16,128]{1,0:T(8,128)S(1)}, f32[16,128]{1,0:T(8,128)S(1)}, u32[]{:S(2)}, u32[]{:S(2)}) %collective-permute-start.11) | collective-permute-done | bytes 8224 | tf_op jit(solution)/shard_map/ppermute | solution.py:275
  26.5 0.9 %collective-permute-done.9.refs_1_ = f32[16,128]{1,0:T(8,128)S(1)} collective-permute-done((f32[16,128]{1,0:T(8,128)S(1)}, f32[16,128]{1,0:T(8,128)S(1)}, u32[]{:S(2)}, u32[]{:S(2)}) %collective-permute-start.9) | collective-permute-done | bytes 8224 | tf_op jit(solution)/shard_map/ppermute | solution.py:275
  27.4 0.6 %shard_map.96 = f32[16,128]{1,0:T(8,128)} custom-call(f32[16,128]{1,0:T(8,128)S(1)} %get-tuple-element.29.refs_0_, f32[16,128]{1,0:T(8,128)S(1)} %collective-permute-done.9.refs_1_, f32[16,128]{1,0:T(8,128)S(1)} %collective-permute-done.10.refs_2_, f32[16,128]{1,0:T(8,128)S(1)} %collective-permute-done.11.refs_3_), custom_call_target="tpu_custom_call" | custom-call | tf_op jit(solution)/shard_map/pallas_call | solution.py:207
  (1 shorter events, 0.0 us)
Async XLA Ops:
  1.6 9.9 %collective-permute-start.1 = (bf16[240,128]{1,0:T(8,128)(2,1)S(1)}, bf16[240,128]{1,0:T(8,128)(2,1)S(1)}, u32[]{:S(2)}, u32[]{:S(2)}) collective-permute-start(bf16[240,128]{1,0:T(8,128)(2,1)S(1)} %get-tuple-element.21), channel_id=1, source_target_pairs={{0,8},{2,10},{4,12},{6,14},{8,0},{10,2},{12,4},{14,6},{1,9},{3,11}... | collective-permute-start | bytes 184328 | tf_op jit(solution)/shard_map/ppermute | solution.py:241
  5.7 7.4 %collective-permute-start.3 = (bf16[240,128]{1,0:T(8,128)(2,1)S(1)}, bf16[240,128]{1,0:T(8,128)(2,1)S(1)}, u32[]{:S(2)}, u32[]{:S(2)}) collective-permute-start(bf16[240,128]{1,0:T(8,128)(2,1)S(1)} %get-tuple-element.23), channel_id=1, source_target_pairs={{0,14},{2,12},{4,10},{6,8},{8,6},{10,4},{12,2},{14,0},{1,15},{3,13... | collective-permute-start | bytes 184328 | tf_op jit(solution)/shard_map/ppermute | solution.py:241
  7.9 11.2 %collective-permute-start = (bf16[400,128]{1,0:T(8,128)(2,1)S(1)}, bf16[400,128]{1,0:T(8,128)(2,1)S(1)}, u32[]{:S(2)}, u32[]{:S(2)}) collective-permute-start(bf16[400,128]{1,0:T(8,128)(2,1)S(1)} %get-tuple-element.20), channel_id=1, source_target_pairs={{0,4},{2,6},{4,0},{6,2},{8,12},{10,14},{12,8},{14,10},{1,5},{3,7},... | collective-permute-start | bytes 307208 | tf_op jit(solution)/shard_map/ppermute | solution.py:241
  8.0 11.2 %collective-permute-start.2 = (bf16[400,128]{1,0:T(8,128)(2,1)S(1)}, bf16[400,128]{1,0:T(8,128)(2,1)S(1)}, u32[]{:S(2)}, u32[]{:S(2)}) collective-permute-start(bf16[400,128]{1,0:T(8,128)(2,1)S(1)} %get-tuple-element.22), channel_id=1, source_target_pairs={{0,2},{2,0},{4,6},{6,4},{8,10},{10,8},{12,14},{14,12},{1,3},{3,1},... | collective-permute-start | bytes 307208 | tf_op jit(solution)/shard_map/ppermute | solution.py:241
  8.7 10.5 %collective-permute-start.4 = (bf16[400,128]{1,0:T(8,128)(2,1)S(1)}, bf16[400,128]{1,0:T(8,128)(2,1)S(1)}, u32[]{:S(2)}, u32[]{:S(2)}) collective-permute-start(bf16[400,128]{1,0:T(8,128)(2,1)S(1)} %get-tuple-element.24), channel_id=1, source_target_pairs={{0,6},{2,4},{4,2},{6,0},{8,14},{10,12},{12,10},{14,8},{1,7},{3,5},... | collective-permute-start | bytes 307208 | tf_op jit(solution)/shard_map/ppermute | solution.py:241
  11.4 7.2 %collective-permute-start.5 = (bf16[240,128]{1,0:T(8,128)(2,1)S(1)}, bf16[240,128]{1,0:T(8,128)(2,1)S(1)}, u32[]{:S(2)}, u32[]{:S(2)}) collective-permute-start(bf16[240,128]{1,0:T(8,128)(2,1)S(1)} %get-tuple-element.25), channel_id=1, source_target_pairs={{0,10},{2,8},{4,14},{6,12},{8,2},{10,0},{12,6},{14,4},{1,11},{3,9}... | collective-permute-start | bytes 184328 | tf_op jit(solution)/shard_map/ppermute | solution.py:241
  13.1 6.1 %collective-permute-start.6 = (bf16[240,128]{1,0:T(8,128)(2,1)S(1)}, bf16[240,128]{1,0:T(8,128)(2,1)S(1)}, u32[]{:S(2)}, u32[]{:S(2)}) collective-permute-start(bf16[240,128]{1,0:T(8,128)(2,1)S(1)} %get-tuple-element.26), channel_id=1, source_target_pairs={{0,12},{2,14},{4,8},{6,10},{8,4},{10,6},{12,0},{14,2},{1,13},{3,15... | collective-permute-start | bytes 184328 | tf_op jit(solution)/shard_map/ppermute | solution.py:241
  19.2 1.4 %collective-permute-start.8 = (bf16[512,128]{1,0:T(8,128)(2,1)S(1)}, bf16[512,128]{1,0:T(8,128)(2,1)S(1)}, u32[]{:S(2)}, u32[]{:S(2)}) collective-permute-start(bf16[512,128]{1,0:T(8,128)(2,1)S(1)} %get-tuple-element.27), channel_id=1, source_target_pairs={{0,1},{1,0},{2,3},{3,2},{4,5},{5,4},{6,7},{7,6},{8,9},{9,8},{10,11... | collective-permute-start | bytes 393224 | tf_op jit(solution)/shard_map/ppermute | solution.py:251
  19.8 1.4 %collective-permute-start.7 = (f32[64,128]{1,0:T(8,128)S(1)}, f32[64,128]{1,0:T(8,128)S(1)}, u32[]{:S(2)}, u32[]{:S(2)}) collective-permute-start(f32[64,128]{1,0:T(8,128)S(1)} %shard_map.92.big), channel_id=1, source_target_pairs={{0,1},{1,0},{2,3},{3,2},{4,5},{5,4},{6,7},{7,6},{8,9},{9,8},{10,11... | collective-permute-start | bytes 98312 | tf_op jit(solution)/shard_map/ppermute | solution.py:251
  21.4 3.7 %collective-permute-start.10 = (f32[16,128]{1,0:T(8,128)S(1)}, f32[16,128]{1,0:T(8,128)S(1)}, u32[]{:S(2)}, u32[]{:S(2)}) collective-permute-start(f32[16,128]{1,0:T(8,128)S(1)} %get-tuple-element.31), channel_id=1, source_target_pairs={{0,2},{2,0},{4,6},{6,4},{8,10},{10,8},{12,14},{14,12},{1,3},{3,1},... | collective-permute-start | bytes 24584 | tf_op jit(solution)/shard_map/ppermute | solution.py:275
  22.9 3.7 %collective-permute-start.11 = (f32[16,128]{1,0:T(8,128)S(1)}, f32[16,128]{1,0:T(8,128)S(1)}, u32[]{:S(2)}, u32[]{:S(2)}) collective-permute-start(f32[16,128]{1,0:T(8,128)S(1)} %get-tuple-element.32), channel_id=1, source_target_pairs={{0,4},{2,6},{4,0},{6,2},{8,12},{10,14},{12,8},{14,10},{1,5},{3,7},... | collective-permute-start | bytes 24584 | tf_op jit(solution)/shard_map/ppermute | solution.py:275
  22.9 4.5 %collective-permute-start.9 = (f32[16,128]{1,0:T(8,128)S(1)}, f32[16,128]{1,0:T(8,128)S(1)}, u32[]{:S(2)}, u32[]{:S(2)}) collective-permute-start(f32[16,128]{1,0:T(8,128)S(1)} %get-tuple-element.30), channel_id=1, source_target_pairs={{0,6},{2,4},{4,2},{6,0},{8,14},{10,12},{12,10},{14,8},{1,7},{3,5},... | collective-permute-start | bytes 24584 | tf_op jit(solution)/shard_map/ppermute | solution.py:275

commit v7 on v6

--- a/solution.py
+++ b/solution.py
@@ -272,7 +272,8 @@
     )
     sums = [terms[0]]
     for i in (3, 2, 1):
-        sums.append(lax.ppermute(terms[i], "seq", [(j, j ^ hops[i]) for j in range(n)]))
+        pairs = [(j * cores + c, (j ^ hops[i]) * cores + (c ^ 1)) for j in range(n) for c in range(cores)]
+        sums.append(lax.ppermute(terms[i], ("seq", "head"), pairs))
     return call(sum_kernel, shape(tokens // 2, 2 * lat, dtype=F32), sums)
 
 

time: 28.2 us -> 27.6 us (0.979)
  starting transfers between devices: 17.2 us -> 16.9 us
  waiting for transfers between devices: 6.86 us -> 6.57 us
    ppermute x3, starting transfers between devices: 3.54 us -> 3.21 us  [exchange_shards(): sums.append(lax.ppermute(terms[i], ('seq', 'head'), pairs))]
    ppermute x3, waiting for transfers between devices: 2.5 us -> 2.21 us  [exchange_shards(): sums.append(lax.ppermute(terms[i], ('seq', 'head'), pairs))]
  transfers between devices with their start and end apart: 12 -> 12, of which waited for: 7 -> 6; matrix products, arithmetic and copies ran while one was open for 0% -> 0% of each run, Pallas kernels for 3% -> 3%
where the time goes in v7:
time: 27.6 us; the launch traced here: 27.4 us
  starting transfers between devices  16.9 us (61%)
  waiting for transfers between devices  6.57 us (24%)
  Pallas kernels  3.24 us (12%)
  between operations  0.7 us (3%)
    ppermute x7, starting transfers between devices, exchange_shards(): blocks.append(lax.ppermute(sent[k], 'seq', [(j, j ^ k) for j in range(n)]))  13.1 us
    ppermute x7, waiting for transfers between devices, exchange_shards(): blocks.append(lax.ppermute(sent[k], 'seq', [(j, j ^ k) for j in range(n)]))  3.9 us
    pallas_call x6, Pallas kernels, call(): pl.pallas_call(kernel, out_shape=out_shape, in_specs=specs if specs is no...  3.24 us
    ppermute x3, starting transfers between devices, exchange_shards(): sums.append(lax.ppermute(terms[i], ('seq', 'head'), pairs))  3.21 us
    ppermute x3, waiting for transfers between devices, exchange_shards(): sums.append(lax.ppermute(terms[i], ('seq', 'head'), pairs))  2.21 us
    ppermute x2, starting transfers between devices, exchange_shards(): swap = lambda a: lax.ppermute(a, 'head', [(c, c ^ 1) for c in range(cores)])  0.63 us
  transfers between devices with their start and end apart: 12, of which 6 were waited for; matrix products, arithmetic and copies ran while one was open for 0% of the time, Pallas kernels for 3%

profile of v7, /device:TPU:0, one launch (start us, length us, event | category | flops | bytes accessed | tf_op | source)
XLA Modules:
  0.0 27.4 jit_solution(4079167745292999611)
XLA Ops:
  0.0 1.6 %shard_map.91 = (bf16[400,128]{1,0:T(8,128)(2,1)S(1)}, bf16[400,128]{1,0:T(8,128)(2,1)S(1)}, bf16[400,128]{1,0:T(8,128)(2,1)S(1)}, bf16[400,128]{1,0:T(8,128)(2,...) custom-call(bf16[16,1024]{1,0:T(8,128)(2,1)} %refs_0_.1, ...), custom_call_target="tpu_custom_call" | custom-call | tf_op jit(solution)/shard_map/pallas_call | solution.py:207
  1.6 4.1 %collective-permute-start.1 = (bf16[240,128]{1,0:T(8,128)(2,1)S(1)}, bf16[240,128]{1,0:T(8,128)(2,1)S(1)}, u32[]{:S(2)}, u32[]{:S(2)}) collective-permute-start(bf16[240,128]{1,0:T(8,128)(2,1)S(1)} %get-tuple-element.21), channel_id=1, source_target_pairs={{0,8},{2,10},{4,12},{6,14},{8,0},{10,2},{12,4},{14,6},{1,9},{3,11}... | collective-permute-start | bytes 184328 | tf_op jit(solution)/shard_map/ppermute | solution.py:241
  5.7 2.3 %collective-permute-start.3 = (bf16[240,128]{1,0:T(8,128)(2,1)S(1)}, bf16[240,128]{1,0:T(8,128)(2,1)S(1)}, u32[]{:S(2)}, u32[]{:S(2)}) collective-permute-start(bf16[240,128]{1,0:T(8,128)(2,1)S(1)} %get-tuple-element.23), channel_id=1, source_target_pairs={{0,14},{2,12},{4,10},{6,8},{8,6},{10,4},{12,2},{14,0},{1,15},{3,13... | collective-permute-start | bytes 184328 | tf_op jit(solution)/shard_map/ppermute | solution.py:241
  7.9 0.0 collective-permute-start
  8.0 0.8 %collective-permute-start.2 = (bf16[400,128]{1,0:T(8,128)(2,1)S(1)}, bf16[400,128]{1,0:T(8,128)(2,1)S(1)}, u32[]{:S(2)}, u32[]{:S(2)}) collective-permute-start(bf16[400,128]{1,0:T(8,128)(2,1)S(1)} %get-tuple-element.22), channel_id=1, source_target_pairs={{0,2},{2,0},{4,6},{6,4},{8,10},{10,8},{12,14},{14,12},{1,3},{3,1},... | collective-permute-start | bytes 307208 | tf_op jit(solution)/shard_map/ppermute | solution.py:241
  8.7 2.7 %collective-permute-start.4 = (bf16[400,128]{1,0:T(8,128)(2,1)S(1)}, bf16[400,128]{1,0:T(8,128)(2,1)S(1)}, u32[]{:S(2)}, u32[]{:S(2)}) collective-permute-start(bf16[400,128]{1,0:T(8,128)(2,1)S(1)} %get-tuple-element.24), channel_id=1, source_target_pairs={{0,6},{2,4},{4,2},{6,0},{8,14},{10,12},{12,10},{14,8},{1,7},{3,5},... | collective-permute-start | bytes 307208 | tf_op jit(solution)/shard_map/ppermute | solution.py:241
  11.4 0.0 collective-permute-done.1.refs_2_
  11.4 1.7 %collective-permute-start.5 = (bf16[240,128]{1,0:T(8,128)(2,1)S(1)}, bf16[240,128]{1,0:T(8,128)(2,1)S(1)}, u32[]{:S(2)}, u32[]{:S(2)}) collective-permute-start(bf16[240,128]{1,0:T(8,128)(2,1)S(1)} %get-tuple-element.25), channel_id=1, source_target_pairs={{0,10},{2,8},{4,14},{6,12},{8,2},{10,0},{12,6},{14,4},{1,11},{3,9}... | collective-permute-start | bytes 184328 | tf_op jit(solution)/shard_map/ppermute | solution.py:241
  13.1 0.0 collective-permute-done.3.refs_4_
  13.1 1.5 %collective-permute-start.6 = (bf16[240,128]{1,0:T(8,128)(2,1)S(1)}, bf16[240,128]{1,0:T(8,128)(2,1)S(1)}, u32[]{:S(2)}, u32[]{:S(2)}) collective-permute-start(bf16[240,128]{1,0:T(8,128)(2,1)S(1)} %get-tuple-element.26), channel_id=1, source_target_pairs={{0,12},{2,14},{4,8},{6,10},{8,4},{10,6},{12,0},{14,2},{1,13},{3,15... | collective-permute-start | bytes 184328 | tf_op jit(solution)/shard_map/ppermute | solution.py:241
  15.3 3.4 %collective-permute-done.5.refs_6_ = bf16[240,128]{1,0:T(8,128)(2,1)S(1)} collective-permute-done((bf16[240,128]{1,0:T(8,128)(2,1)S(1)}, bf16[240,128]{1,0:T(8,128)(2,1)S(1)}, u32[]{:S(2)}, u32[]{:S(2)}) %collective-permute-start.5) | collective-permute-done | bytes 61472 | tf_op jit(solution)/shard_map/ppermute | solution.py:241
  18.7 0.5 %collective-permute-done.6.refs_7_ = bf16[240,128]{1,0:T(8,128)(2,1)S(1)} collective-permute-done((bf16[240,128]{1,0:T(8,128)(2,1)S(1)}, bf16[240,128]{1,0:T(8,128)(2,1)S(1)}, u32[]{:S(2)}, u32[]{:S(2)}) %collective-permute-start.6) | collective-permute-done | bytes 61472 | tf_op jit(solution)/shard_map/ppermute | solution.py:241
  19.2 0.0 collective-permute-done.refs_1_
  19.2 0.0 collective-permute-done.2.refs_3_
  19.2 0.0 collective-permute-done.4.refs_5_
  19.2 0.1 collective-permute-start.8
  19.3 0.5 %shard_map.92.big = f32[64,128]{1,0:T(8,128)S(1)} custom-call(bf16[400,128]{1,0:T(8,128)(2,1)S(1)} %get-tuple-element.19.refs_0_, bf16[400,128]{1,0:T(8,128)(2,1)S(1)} %collective-permute-done.refs_1_, bf16[240,128]{1,0:T(8,128)(2,1)S(1)} %collective-permute-done.1.refs_2_, bf16[400,128]{1,0:T(8,128)(2,1)S(1)} %collective-permute-done.2.refs_3_, ...), custom_call_target="tpu_custom_call" | custom-call | flops 1000000000 | bytes 1000000 | tf_op jit(solution)/shard_map/pallas_call | solution.py:207
  19.8 0.6 %collective-permute-start.7 = (f32[64,128]{1,0:T(8,128)S(1)}, f32[64,128]{1,0:T(8,128)S(1)}, u32[]{:S(2)}, u32[]{:S(2)}) collective-permute-start(f32[64,128]{1,0:T(8,128)S(1)} %shard_map.92.big), channel_id=1, source_target_pairs={{0,1},{1,0},{2,3},{3,2},{4,5},{5,4},{6,7},{7,6},{8,9},{9,8},{10,11... | collective-permute-start | bytes 98312 | tf_op jit(solution)/shard_map/ppermute | solution.py:251
  20.3 0.3 %collective-permute-done.8.refs_8_ = bf16[512,128]{1,0:T(8,128)(2,1)S(1)} collective-permute-done((bf16[512,128]{1,0:T(8,128)(2,1)S(1)}, bf16[512,128]{1,0:T(8,128)(2,1)S(1)}, u32[]{:S(2)}, u32[]{:S(2)}) %collective-permute-start.8) | collective-permute-done | bytes 131104 | tf_op jit(solution)/shard_map/ppermute | solution.py:251
  20.6 0.4 %shard_map.94.small = f32[64,128]{1,0:T(8,128)S(1)} custom-call(bf16[400,128]{1,0:T(8,128)(2,1)S(1)} %get-tuple-element.19.refs_0_, bf16[400,128]{1,0:T(8,128)(2,1)S(1)} %collective-permute-done.refs_1_, bf16[240,128]{1,0:T(8,128)(2,1)S(1)} %collective-permute-done.1.refs_2_, bf16[400,128]{1,0:T(8,128)(2,1)S(1)} %collective-permute-done.2.refs_3_, ...), custom_call_target="tpu_custom_call" | custom-call | flops 1000000000 | bytes 1000000 | tf_op jit(solution)/shard_map/pallas_call | solution.py:207
  21.0 0.2 collective-permute-done.7.other_big
  21.2 0.2 shard_map.95
  21.4 1.4 %collective-permute-start.10 = (f32[16,128]{1,0:T(8,128)S(1)}, f32[16,128]{1,0:T(8,128)S(1)}, u32[]{:S(2)}, u32[]{:S(2)}) collective-permute-start(f32[16,128]{1,0:T(8,128)S(1)} %get-tuple-element.31), channel_id=1, source_target_pairs={{0,3},{1,2},{2,1},{3,0},{4,7},{5,6},{6,5},{7,4},{8,11},{9,10},{10,... | collective-permute-start | bytes 24584 | tf_op jit(solution)/shard_map/ppermute | solution.py:276
  22.8 0.0 collective-permute-start.11
  22.8 1.8 %collective-permute-start.9 = (f32[16,128]{1,0:T(8,128)S(1)}, f32[16,128]{1,0:T(8,128)S(1)}, u32[]{:S(2)}, u32[]{:S(2)}) collective-permute-start(f32[16,128]{1,0:T(8,128)S(1)} %get-tuple-element.30), channel_id=1, source_target_pairs={{0,7},{1,6},{2,5},{3,4},{4,3},{5,2},{6,1},{7,0},{8,15},{9,14},{10,... | collective-permute-start | bytes 24584 | tf_op jit(solution)/shard_map/ppermute | solution.py:276
  24.6 0.0 collective-permute-done.10.refs_2_
  24.6 1.3 %collective-permute-done.11.refs_3_ = f32[16,128]{1,0:T(8,128)S(1)} collective-permute-done((f32[16,128]{1,0:T(8,128)S(1)}, f32[16,128]{1,0:T(8,128)S(1)}, u32[]{:S(2)}, u32[]{:S(2)}) %collective-permute-start.11) | collective-permute-done | bytes 8224 | tf_op jit(solution)/shard_map/ppermute | solution.py:276
  25.9 0.9 %collective-permute-done.9.refs_1_ = f32[16,128]{1,0:T(8,128)S(1)} collective-permute-done((f32[16,128]{1,0:T(8,128)S(1)}, f32[16,128]{1,0:T(8,128)S(1)}, u32[]{:S(2)}, u32[]{:S(2)}) %collective-permute-start.9) | collective-permute-done | bytes 8224 | tf_op jit(solution)/shard_map/ppermute | solution.py:276
  26.8 0.6 %shard_map.96 = f32[16,128]{1,0:T(8,128)} custom-call(f32[16,128]{1,0:T(8,128)S(1)} %get-tuple-element.29.refs_0_, f32[16,128]{1,0:T(8,128)S(1)} %collective-permute-done.9.refs_1_, f32[16,128]{1,0:T(8,128)S(1)} %collective-permute-done.10.refs_2_, f32[16,128]{1,0:T(8,128)S(1)} %collective-permute-done.11.refs_3_), custom_call_target="tpu_custom_call" | custom-call | tf_op jit(solution)/shard_map/pallas_call | solution.py:207
  (1 shorter events, 0.0 us)
Async XLA Ops:
  1.6 9.9 %collective-permute-start.1 = (bf16[240,128]{1,0:T(8,128)(2,1)S(1)}, bf16[240,128]{1,0:T(8,128)(2,1)S(1)}, u32[]{:S(2)}, u32[]{:S(2)}) collective-permute-start(bf16[240,128]{1,0:T(8,128)(2,1)S(1)} %get-tuple-element.21), channel_id=1, source_target_pairs={{0,8},{2,10},{4,12},{6,14},{8,0},{10,2},{12,4},{14,6},{1,9},{3,11}... | collective-permute-start | bytes 184328 | tf_op jit(solution)/shard_map/ppermute | solution.py:241
  5.7 7.4 %collective-permute-start.3 = (bf16[240,128]{1,0:T(8,128)(2,1)S(1)}, bf16[240,128]{1,0:T(8,128)(2,1)S(1)}, u32[]{:S(2)}, u32[]{:S(2)}) collective-permute-start(bf16[240,128]{1,0:T(8,128)(2,1)S(1)} %get-tuple-element.23), channel_id=1, source_target_pairs={{0,14},{2,12},{4,10},{6,8},{8,6},{10,4},{12,2},{14,0},{1,15},{3,13... | collective-permute-start | bytes 184328 | tf_op jit(solution)/shard_map/ppermute | solution.py:241
  7.9 11.2 %collective-permute-start = (bf16[400,128]{1,0:T(8,128)(2,1)S(1)}, bf16[400,128]{1,0:T(8,128)(2,1)S(1)}, u32[]{:S(2)}, u32[]{:S(2)}) collective-permute-start(bf16[400,128]{1,0:T(8,128)(2,1)S(1)} %get-tuple-element.20), channel_id=1, source_target_pairs={{0,4},{2,6},{4,0},{6,2},{8,12},{10,14},{12,8},{14,10},{1,5},{3,7},... | collective-permute-start | bytes 307208 | tf_op jit(solution)/shard_map/ppermute | solution.py:241
  8.0 11.2 %collective-permute-start.2 = (bf16[400,128]{1,0:T(8,128)(2,1)S(1)}, bf16[400,128]{1,0:T(8,128)(2,1)S(1)}, u32[]{:S(2)}, u32[]{:S(2)}) collective-permute-start(bf16[400,128]{1,0:T(8,128)(2,1)S(1)} %get-tuple-element.22), channel_id=1, source_target_pairs={{0,2},{2,0},{4,6},{6,4},{8,10},{10,8},{12,14},{14,12},{1,3},{3,1},... | collective-permute-start | bytes 307208 | tf_op jit(solution)/shard_map/ppermute | solution.py:241
  8.7 10.5 %collective-permute-start.4 = (bf16[400,128]{1,0:T(8,128)(2,1)S(1)}, bf16[400,128]{1,0:T(8,128)(2,1)S(1)}, u32[]{:S(2)}, u32[]{:S(2)}) collective-permute-start(bf16[400,128]{1,0:T(8,128)(2,1)S(1)} %get-tuple-element.24), channel_id=1, source_target_pairs={{0,6},{2,4},{4,2},{6,0},{8,14},{10,12},{12,10},{14,8},{1,7},{3,5},... | collective-permute-start | bytes 307208 | tf_op jit(solution)/shard_map/ppermute | solution.py:241
  11.4 7.2 %collective-permute-start.5 = (bf16[240,128]{1,0:T(8,128)(2,1)S(1)}, bf16[240,128]{1,0:T(8,128)(2,1)S(1)}, u32[]{:S(2)}, u32[]{:S(2)}) collective-permute-start(bf16[240,128]{1,0:T(8,128)(2,1)S(1)} %get-tuple-element.25), channel_id=1, source_target_pairs={{0,10},{2,8},{4,14},{6,12},{8,2},{10,0},{12,6},{14,4},{1,11},{3,9}... | collective-permute-start | bytes 184328 | tf_op jit(solution)/shard_map/ppermute | solution.py:241
  13.1 6.1 %collective-permute-start.6 = (bf16[240,128]{1,0:T(8,128)(2,1)S(1)}, bf16[240,128]{1,0:T(8,128)(2,1)S(1)}, u32[]{:S(2)}, u32[]{:S(2)}) collective-permute-start(bf16[240,128]{1,0:T(8,128)(2,1)S(1)} %get-tuple-element.26), channel_id=1, source_target_pairs={{0,12},{2,14},{4,8},{6,10},{8,4},{10,6},{12,0},{14,2},{1,13},{3,15... | collective-permute-start | bytes 184328 | tf_op jit(solution)/shard_map/ppermute | solution.py:241
  19.2 1.4 %collective-permute-start.8 = (bf16[512,128]{1,0:T(8,128)(2,1)S(1)}, bf16[512,128]{1,0:T(8,128)(2,1)S(1)}, u32[]{:S(2)}, u32[]{:S(2)}) collective-permute-start(bf16[512,128]{1,0:T(8,128)(2,1)S(1)} %get-tuple-element.27), channel_id=1, source_target_pairs={{0,1},{1,0},{2,3},{3,2},{4,5},{5,4},{6,7},{7,6},{8,9},{9,8},{10,11... | collective-permute-start | bytes 393224 | tf_op jit(solution)/shard_map/ppermute | solution.py:251
  19.8 1.4 %collective-permute-start.7 = (f32[64,128]{1,0:T(8,128)S(1)}, f32[64,128]{1,0:T(8,128)S(1)}, u32[]{:S(2)}, u32[]{:S(2)}) collective-permute-start(f32[64,128]{1,0:T(8,128)S(1)} %shard_map.92.big), channel_id=1, source_target_pairs={{0,1},{1,0},{2,3},{3,2},{4,5},{5,4},{6,7},{7,6},{8,9},{9,8},{10,11... | collective-permute-start | bytes 98312 | tf_op jit(solution)/shard_map/ppermute | solution.py:251
  21.4 3.2 %collective-permute-start.10 = (f32[16,128]{1,0:T(8,128)S(1)}, f32[16,128]{1,0:T(8,128)S(1)}, u32[]{:S(2)}, u32[]{:S(2)}) collective-permute-start(f32[16,128]{1,0:T(8,128)S(1)} %get-tuple-element.31), channel_id=1, source_target_pairs={{0,3},{1,2},{2,1},{3,0},{4,7},{5,6},{6,5},{7,4},{8,11},{9,10},{10,... | collective-permute-start | bytes 24584 | tf_op jit(solution)/shard_map/ppermute | solution.py:276
  22.8 3.1 %collective-permute-start.11 = (f32[16,128]{1,0:T(8,128)S(1)}, f32[16,128]{1,0:T(8,128)S(1)}, u32[]{:S(2)}, u32[]{:S(2)}) collective-permute-start(f32[16,128]{1,0:T(8,128)S(1)} %get-tuple-element.32), channel_id=1, source_target_pairs={{0,5},{1,4},{2,7},{3,6},{4,1},{5,0},{6,3},{7,2},{8,13},{9,12},{10,... | collective-permute-start | bytes 24584 | tf_op jit(solution)/shard_map/ppermute | solution.py:276
  22.8 4.0 %collective-permute-start.9 = (f32[16,128]{1,0:T(8,128)S(1)}, f32[16,128]{1,0:T(8,128)S(1)}, u32[]{:S(2)}, u32[]{:S(2)}) collective-permute-start(f32[16,128]{1,0:T(8,128)S(1)} %get-tuple-element.30), channel_id=1, source_target_pairs={{0,7},{1,6},{2,5},{3,4},{4,3},{5,2},{6,1},{7,0},{8,15},{9,14},{10,... | collective-permute-start | bytes 24584 | tf_op jit(solution)/shard_map/ppermute | solution.py:276

commit v8 on v7

--- a/solution.py
+++ b/solution.py
@@ -188,7 +188,7 @@
     lat, width = big.shape
     scale = weight[:1, :1]
     blended = (1.0 + scale) * (big[:, :] + other_big[:, :]) - scale * small[:, :]
-    latent[:, :lat] = blended.T
+    latent[:width, :lat] = blended.T
     for i in range(near):
         even = latent[pl.ds(i * tokens, tokens // 2, stride=2), :lat]
         odd = latent[pl.ds(i * tokens + 1, tokens // 2, stride=2), :lat]
@@ -268,7 +268,7 @@
         functools.partial(blend_kernel, near, tokens),
         [shape(tokens // 2, 2 * lat, dtype=F32)] * near,
         (big, other_big, small, weight),
-        scratch=[pltpu.VMEM((near * tokens, DH), F32)],
+        scratch=[pltpu.VMEM((near * tokens + 8, DH), F32)],
     )
     sums = [terms[0]]
     for i in (3, 2, 1):

time: 27.6 us -> 27.6 us (level)
  no operation moved by 1% of the time
where the time goes in v8:
time: 27.6 us; the launch traced here: 27.4 us
  starting transfers between devices  16.9 us (61%)
  waiting for transfers between devices  6.57 us (24%)
  Pallas kernels  3.24 us (12%)
  between operations  0.7 us (3%)
    ppermute x7, starting transfers between devices, exchange_shards(): blocks.append(lax.ppermute(sent[k], 'seq', [(j, j ^ k) for j in range(n)]))  13.1 us
    ppermute x7, waiting for transfers between devices, exchange_shards(): blocks.append(lax.ppermute(sent[k], 'seq', [(j, j ^ k) for j in range(n)]))  3.9 us
    pallas_call x6, Pallas kernels, call(): pl.pallas_call(kernel, out_shape=out_shape, in_specs=specs if specs is no...  3.24 us
    ppermute x3, starting transfers between devices, exchange_shards(): sums.append(lax.ppermute(terms[i], ('seq', 'head'), pairs))  3.21 us
    ppermute x3, waiting for transfers between devices, exchange_shards(): sums.append(lax.ppermute(terms[i], ('seq', 'head'), pairs))  2.21 us
    ppermute x2, starting transfers between devices, exchange_shards(): swap = lambda a: lax.ppermute(a, 'head', [(c, c ^ 1) for c in range(cores)])  0.63 us
  transfers between devices with their start and end apart: 12, of which 6 were waited for; matrix products, arithmetic and copies ran while one was open for 0% of the time, Pallas kernels for 3%

profile of v8, /device:TPU:0, one launch (start us, length us, event | category | flops | bytes accessed | tf_op | source)
XLA Modules:
  0.0 27.4 jit_solution(4079167745292999611)
XLA Ops:
  0.0 1.6 %shard_map.91 = (bf16[400,128]{1,0:T(8,128)(2,1)S(1)}, bf16[400,128]{1,0:T(8,128)(2,1)S(1)}, bf16[400,128]{1,0:T(8,128)(2,1)S(1)}, bf16[400,128]{1,0:T(8,128)(2,...) custom-call(bf16[16,1024]{1,0:T(8,128)(2,1)} %refs_0_.1, ...), custom_call_target="tpu_custom_call" | custom-call | tf_op jit(solution)/shard_map/pallas_call | solution.py:207
  1.6 4.1 %collective-permute-start.1 = (bf16[240,128]{1,0:T(8,128)(2,1)S(1)}, bf16[240,128]{1,0:T(8,128)(2,1)S(1)}, u32[]{:S(2)}, u32[]{:S(2)}) collective-permute-start(bf16[240,128]{1,0:T(8,128)(2,1)S(1)} %get-tuple-element.21), channel_id=1, source_target_pairs={{0,8},{2,10},{4,12},{6,14},{8,0},{10,2},{12,4},{14,6},{1,9},{3,11}... | collective-permute-start | bytes 184328 | tf_op jit(solution)/shard_map/ppermute | solution.py:241
  5.7 2.3 %collective-permute-start.3 = (bf16[240,128]{1,0:T(8,128)(2,1)S(1)}, bf16[240,128]{1,0:T(8,128)(2,1)S(1)}, u32[]{:S(2)}, u32[]{:S(2)}) collective-permute-start(bf16[240,128]{1,0:T(8,128)(2,1)S(1)} %get-tuple-element.23), channel_id=1, source_target_pairs={{0,14},{2,12},{4,10},{6,8},{8,6},{10,4},{12,2},{14,0},{1,15},{3,13... | collective-permute-start | bytes 184328 | tf_op jit(solution)/shard_map/ppermute | solution.py:241
  7.9 0.0 collective-permute-start
  8.0 0.8 %collective-permute-start.2 = (bf16[400,128]{1,0:T(8,128)(2,1)S(1)}, bf16[400,128]{1,0:T(8,128)(2,1)S(1)}, u32[]{:S(2)}, u32[]{:S(2)}) collective-permute-start(bf16[400,128]{1,0:T(8,128)(2,1)S(1)} %get-tuple-element.22), channel_id=1, source_target_pairs={{0,2},{2,0},{4,6},{6,4},{8,10},{10,8},{12,14},{14,12},{1,3},{3,1},... | collective-permute-start | bytes 307208 | tf_op jit(solution)/shard_map/ppermute | solution.py:241
  8.7 2.7 %collective-permute-start.4 = (bf16[400,128]{1,0:T(8,128)(2,1)S(1)}, bf16[400,128]{1,0:T(8,128)(2,1)S(1)}, u32[]{:S(2)}, u32[]{:S(2)}) collective-permute-start(bf16[400,128]{1,0:T(8,128)(2,1)S(1)} %get-tuple-element.24), channel_id=1, source_target_pairs={{0,6},{2,4},{4,2},{6,0},{8,14},{10,12},{12,10},{14,8},{1,7},{3,5},... | collective-permute-start | bytes 307208 | tf_op jit(solution)/shard_map/ppermute | solution.py:241
  11.4 0.0 collective-permute-done.1.refs_2_
  11.4 1.7 %collective-permute-start.5 = (bf16[240,128]{1,0:T(8,128)(2,1)S(1)}, bf16[240,128]{1,0:T(8,128)(2,1)S(1)}, u32[]{:S(2)}, u32[]{:S(2)}) collective-permute-start(bf16[240,128]{1,0:T(8,128)(2,1)S(1)} %get-tuple-element.25), channel_id=1, source_target_pairs={{0,10},{2,8},{4,14},{6,12},{8,2},{10,0},{12,6},{14,4},{1,11},{3,9}... | collective-permute-start | bytes 184328 | tf_op jit(solution)/shard_map/ppermute | solution.py:241
  13.1 0.0 collective-permute-done.3.refs_4_
  13.1 1.5 %collective-permute-start.6 = (bf16[240,128]{1,0:T(8,128)(2,1)S(1)}, bf16[240,128]{1,0:T(8,128)(2,1)S(1)}, u32[]{:S(2)}, u32[]{:S(2)}) collective-permute-start(bf16[240,128]{1,0:T(8,128)(2,1)S(1)} %get-tuple-element.26), channel_id=1, source_target_pairs={{0,12},{2,14},{4,8},{6,10},{8,4},{10,6},{12,0},{14,2},{1,13},{3,15... | collective-permute-start | bytes 184328 | tf_op jit(solution)/shard_map/ppermute | solution.py:241
  15.3 3.4 %collective-permute-done.5.refs_6_ = bf16[240,128]{1,0:T(8,128)(2,1)S(1)} collective-permute-done((bf16[240,128]{1,0:T(8,128)(2,1)S(1)}, bf16[240,128]{1,0:T(8,128)(2,1)S(1)}, u32[]{:S(2)}, u32[]{:S(2)}) %collective-permute-start.5) | collective-permute-done | bytes 61472 | tf_op jit(solution)/shard_map/ppermute | solution.py:241
  18.7 0.5 %collective-permute-done.6.refs_7_ = bf16[240,128]{1,0:T(8,128)(2,1)S(1)} collective-permute-done((bf16[240,128]{1,0:T(8,128)(2,1)S(1)}, bf16[240,128]{1,0:T(8,128)(2,1)S(1)}, u32[]{:S(2)}, u32[]{:S(2)}) %collective-permute-start.6) | collective-permute-done | bytes 61472 | tf_op jit(solution)/shard_map/ppermute | solution.py:241
  19.2 0.0 collective-permute-done.refs_1_
  19.2 0.0 collective-permute-done.2.refs_3_
  19.2 0.0 collective-permute-done.4.refs_5_
  19.2 0.1 collective-permute-start.8
  19.3 0.5 %shard_map.92.big = f32[64,128]{1,0:T(8,128)S(1)} custom-call(bf16[400,128]{1,0:T(8,128)(2,1)S(1)} %get-tuple-element.19.refs_0_, bf16[400,128]{1,0:T(8,128)(2,1)S(1)} %collective-permute-done.refs_1_, bf16[240,128]{1,0:T(8,128)(2,1)S(1)} %collective-permute-done.1.refs_2_, bf16[400,128]{1,0:T(8,128)(2,1)S(1)} %collective-permute-done.2.refs_3_, ...), custom_call_target="tpu_custom_call" | custom-call | flops 1000000000 | bytes 1000000 | tf_op jit(solution)/shard_map/pallas_call | solution.py:207
  19.8 0.6 %collective-permute-start.7 = (f32[64,128]{1,0:T(8,128)S(1)}, f32[64,128]{1,0:T(8,128)S(1)}, u32[]{:S(2)}, u32[]{:S(2)}) collective-permute-start(f32[64,128]{1,0:T(8,128)S(1)} %shard_map.92.big), channel_id=1, source_target_pairs={{0,1},{1,0},{2,3},{3,2},{4,5},{5,4},{6,7},{7,6},{8,9},{9,8},{10,11... | collective-permute-start | bytes 98312 | tf_op jit(solution)/shard_map/ppermute | solution.py:251
  20.3 0.3 %collective-permute-done.8.refs_8_ = bf16[512,128]{1,0:T(8,128)(2,1)S(1)} collective-permute-done((bf16[512,128]{1,0:T(8,128)(2,1)S(1)}, bf16[512,128]{1,0:T(8,128)(2,1)S(1)}, u32[]{:S(2)}, u32[]{:S(2)}) %collective-permute-start.8) | collective-permute-done | bytes 131104 | tf_op jit(solution)/shard_map/ppermute | solution.py:251
  20.6 0.4 %shard_map.94.small = f32[64,128]{1,0:T(8,128)S(1)} custom-call(bf16[400,128]{1,0:T(8,128)(2,1)S(1)} %get-tuple-element.19.refs_0_, bf16[400,128]{1,0:T(8,128)(2,1)S(1)} %collective-permute-done.refs_1_, bf16[240,128]{1,0:T(8,128)(2,1)S(1)} %collective-permute-done.1.refs_2_, bf16[400,128]{1,0:T(8,128)(2,1)S(1)} %collective-permute-done.2.refs_3_, ...), custom_call_target="tpu_custom_call" | custom-call | flops 1000000000 | bytes 1000000 | tf_op jit(solution)/shard_map/pallas_call | solution.py:207
  21.0 0.2 collective-permute-done.7.other_big
  21.2 0.2 shard_map.95
  21.4 1.4 %collective-permute-start.10 = (f32[16,128]{1,0:T(8,128)S(1)}, f32[16,128]{1,0:T(8,128)S(1)}, u32[]{:S(2)}, u32[]{:S(2)}) collective-permute-start(f32[16,128]{1,0:T(8,128)S(1)} %get-tuple-element.31), channel_id=1, source_target_pairs={{0,3},{1,2},{2,1},{3,0},{4,7},{5,6},{6,5},{7,4},{8,11},{9,10},{10,... | collective-permute-start | bytes 24584 | tf_op jit(solution)/shard_map/ppermute | solution.py:276
  22.8 0.0 collective-permute-start.11
  22.8 1.8 %collective-permute-start.9 = (f32[16,128]{1,0:T(8,128)S(1)}, f32[16,128]{1,0:T(8,128)S(1)}, u32[]{:S(2)}, u32[]{:S(2)}) collective-permute-start(f32[16,128]{1,0:T(8,128)S(1)} %get-tuple-element.30), channel_id=1, source_target_pairs={{0,7},{1,6},{2,5},{3,4},{4,3},{5,2},{6,1},{7,0},{8,15},{9,14},{10,... | collective-permute-start | bytes 24584 | tf_op jit(solution)/shard_map/ppermute | solution.py:276
  24.6 0.0 collective-permute-done.10.refs_2_
  24.6 1.3 %collective-permute-done.11.refs_3_ = f32[16,128]{1,0:T(8,128)S(1)} collective-permute-done((f32[16,128]{1,0:T(8,128)S(1)}, f32[16,128]{1,0:T(8,128)S(1)}, u32[]{:S(2)}, u32[]{:S(2)}) %collective-permute-start.11) | collective-permute-done | bytes 8224 | tf_op jit(solution)/shard_map/ppermute | solution.py:276
  25.9 0.9 %collective-permute-done.9.refs_1_ = f32[16,128]{1,0:T(8,128)S(1)} collective-permute-done((f32[16,128]{1,0:T(8,128)S(1)}, f32[16,128]{1,0:T(8,128)S(1)}, u32[]{:S(2)}, u32[]{:S(2)}) %collective-permute-start.9) | collective-permute-done | bytes 8224 | tf_op jit(solution)/shard_map/ppermute | solution.py:276
  26.8 0.6 %shard_map.96 = f32[16,128]{1,0:T(8,128)} custom-call(f32[16,128]{1,0:T(8,128)S(1)} %get-tuple-element.29.refs_0_, f32[16,128]{1,0:T(8,128)S(1)} %collective-permute-done.9.refs_1_, f32[16,128]{1,0:T(8,128)S(1)} %collective-permute-done.10.refs_2_, f32[16,128]{1,0:T(8,128)S(1)} %collective-permute-done.11.refs_3_), custom_call_target="tpu_custom_call" | custom-call | tf_op jit(solution)/shard_map/pallas_call | solution.py:207
  (1 shorter events, 0.0 us)
Async XLA Ops:
  1.6 9.9 %collective-permute-start.1 = (bf16[240,128]{1,0:T(8,128)(2,1)S(1)}, bf16[240,128]{1,0:T(8,128)(2,1)S(1)}, u32[]{:S(2)}, u32[]{:S(2)}) collective-permute-start(bf16[240,128]{1,0:T(8,128)(2,1)S(1)} %get-tuple-element.21), channel_id=1, source_target_pairs={{0,8},{2,10},{4,12},{6,14},{8,0},{10,2},{12,4},{14,6},{1,9},{3,11}... | collective-permute-start | bytes 184328 | tf_op jit(solution)/shard_map/ppermute | solution.py:241
  5.7 7.4 %collective-permute-start.3 = (bf16[240,128]{1,0:T(8,128)(2,1)S(1)}, bf16[240,128]{1,0:T(8,128)(2,1)S(1)}, u32[]{:S(2)}, u32[]{:S(2)}) collective-permute-start(bf16[240,128]{1,0:T(8,128)(2,1)S(1)} %get-tuple-element.23), channel_id=1, source_target_pairs={{0,14},{2,12},{4,10},{6,8},{8,6},{10,4},{12,2},{14,0},{1,15},{3,13... | collective-permute-start | bytes 184328 | tf_op jit(solution)/shard_map/ppermute | solution.py:241
  7.9 11.2 %collective-permute-start = (bf16[400,128]{1,0:T(8,128)(2,1)S(1)}, bf16[400,128]{1,0:T(8,128)(2,1)S(1)}, u32[]{:S(2)}, u32[]{:S(2)}) collective-permute-start(bf16[400,128]{1,0:T(8,128)(2,1)S(1)} %get-tuple-element.20), channel_id=1, source_target_pairs={{0,4},{2,6},{4,0},{6,2},{8,12},{10,14},{12,8},{14,10},{1,5},{3,7},... | collective-permute-start | bytes 307208 | tf_op jit(solution)/shard_map/ppermute | solution.py:241
  8.0 11.2 %collective-permute-start.2 = (bf16[400,128]{1,0:T(8,128)(2,1)S(1)}, bf16[400,128]{1,0:T(8,128)(2,1)S(1)}, u32[]{:S(2)}, u32[]{:S(2)}) collective-permute-start(bf16[400,128]{1,0:T(8,128)(2,1)S(1)} %get-tuple-element.22), channel_id=1, source_target_pairs={{0,2},{2,0},{4,6},{6,4},{8,10},{10,8},{12,14},{14,12},{1,3},{3,1},... | collective-permute-start | bytes 307208 | tf_op jit(solution)/shard_map/ppermute | solution.py:241
  8.7 10.5 %collective-permute-start.4 = (bf16[400,128]{1,0:T(8,128)(2,1)S(1)}, bf16[400,128]{1,0:T(8,128)(2,1)S(1)}, u32[]{:S(2)}, u32[]{:S(2)}) collective-permute-start(bf16[400,128]{1,0:T(8,128)(2,1)S(1)} %get-tuple-element.24), channel_id=1, source_target_pairs={{0,6},{2,4},{4,2},{6,0},{8,14},{10,12},{12,10},{14,8},{1,7},{3,5},... | collective-permute-start | bytes 307208 | tf_op jit(solution)/shard_map/ppermute | solution.py:241
  11.4 7.2 %collective-permute-start.5 = (bf16[240,128]{1,0:T(8,128)(2,1)S(1)}, bf16[240,128]{1,0:T(8,128)(2,1)S(1)}, u32[]{:S(2)}, u32[]{:S(2)}) collective-permute-start(bf16[240,128]{1,0:T(8,128)(2,1)S(1)} %get-tuple-element.25), channel_id=1, source_target_pairs={{0,10},{2,8},{4,14},{6,12},{8,2},{10,0},{12,6},{14,4},{1,11},{3,9}... | collective-permute-start | bytes 184328 | tf_op jit(solution)/shard_map/ppermute | solution.py:241
  13.1 6.1 %collective-permute-start.6 = (bf16[240,128]{1,0:T(8,128)(2,1)S(1)}, bf16[240,128]{1,0:T(8,128)(2,1)S(1)}, u32[]{:S(2)}, u32[]{:S(2)}) collective-permute-start(bf16[240,128]{1,0:T(8,128)(2,1)S(1)} %get-tuple-element.26), channel_id=1, source_target_pairs={{0,12},{2,14},{4,8},{6,10},{8,4},{10,6},{12,0},{14,2},{1,13},{3,15... | collective-permute-start | bytes 184328 | tf_op jit(solution)/shard_map/ppermute | solution.py:241
  19.2 1.4 %collective-permute-start.8 = (bf16[512,128]{1,0:T(8,128)(2,1)S(1)}, bf16[512,128]{1,0:T(8,128)(2,1)S(1)}, u32[]{:S(2)}, u32[]{:S(2)}) collective-permute-start(bf16[512,128]{1,0:T(8,128)(2,1)S(1)} %get-tuple-element.27), channel_id=1, source_target_pairs={{0,1},{1,0},{2,3},{3,2},{4,5},{5,4},{6,7},{7,6},{8,9},{9,8},{10,11... | collective-permute-start | bytes 393224 | tf_op jit(solution)/shard_map/ppermute | solution.py:251
  19.8 1.4 %collective-permute-start.7 = (f32[64,128]{1,0:T(8,128)S(1)}, f32[64,128]{1,0:T(8,128)S(1)}, u32[]{:S(2)}, u32[]{:S(2)}) collective-permute-start(f32[64,128]{1,0:T(8,128)S(1)} %shard_map.92.big), channel_id=1, source_target_pairs={{0,1},{1,0},{2,3},{3,2},{4,5},{5,4},{6,7},{7,6},{8,9},{9,8},{10,11... | collective-permute-start | bytes 98312 | tf_op jit(solution)/shard_map/ppermute | solution.py:251
  21.4 3.2 %collective-permute-start.10 = (f32[16,128]{1,0:T(8,128)S(1)}, f32[16,128]{1,0:T(8,128)S(1)}, u32[]{:S(2)}, u32[]{:S(2)}) collective-permute-start(f32[16,128]{1,0:T(8,128)S(1)} %get-tuple-element.31), channel_id=1, source_target_pairs={{0,3},{1,2},{2,1},{3,0},{4,7},{5,6},{6,5},{7,4},{8,11},{9,10},{10,... | collective-permute-start | bytes 24584 | tf_op jit(solution)/shard_map/ppermute | solution.py:276
  22.8 3.1 %collective-permute-start.11 = (f32[16,128]{1,0:T(8,128)S(1)}, f32[16,128]{1,0:T(8,128)S(1)}, u32[]{:S(2)}, u32[]{:S(2)}) collective-permute-start(f32[16,128]{1,0:T(8,128)S(1)} %get-tuple-element.32), channel_id=1, source_target_pairs={{0,5},{1,4},{2,7},{3,6},{4,1},{5,0},{6,3},{7,2},{8,13},{9,12},{10,... | collective-permute-start | bytes 24584 | tf_op jit(solution)/shard_map/ppermute | solution.py:276
  22.8 4.0 %collective-permute-start.9 = (f32[16,128]{1,0:T(8,128)S(1)}, f32[16,128]{1,0:T(8,128)S(1)}, u32[]{:S(2)}, u32[]{:S(2)}) collective-permute-start(f32[16,128]{1,0:T(8,128)S(1)} %get-tuple-element.30), channel_id=1, source_target_pairs={{0,7},{1,6},{2,5},{3,4},{4,3},{5,2},{6,1},{7,0},{8,15},{9,14},{10,... | collective-permute-start | bytes 24584 | tf_op jit(solution)/shard_map/ppermute | solution.py:276

commit v9 on v8

--- a/solution.py
+++ b/solution.py
@@ -22,7 +22,7 @@
 
 
 def hop_order(n):
-    return [0] + [2, 4, 1, 7, 3, 5, 6] if n == 8 else list(range(n))
+    return [0] + [6, 2, 5, 3, 7, 4, 1] if n == 8 else list(range(n))
 
 
 def row_layout(group, small_group, tokens, small_tokens):

time: 27.6 us -> 27.4 us (level)
  waiting for transfers between devices: 6.57 us -> 5.89 us
  starting transfers between devices: 16.9 us -> 17.4 us
    ppermute x3, waiting for transfers between devices: 2.21 us -> 1.43 us  [exchange_shards(): sums.append(lax.ppermute(terms[i], ('seq', 'head'), pairs))]
    ppermute x7, starting transfers between devices: 13.1 us -> 13.6 us  [exchange_shards(): blocks.append(lax.ppermute(sent[k], 'seq', [(j, j ^ k) for j in range(n)]))]
where the time goes in v9:
time: 27.4 us; the launch traced here: 27.2 us
  starting transfers between devices  17.4 us (64%)
  waiting for transfers between devices  5.89 us (21%)
  Pallas kernels  3.25 us (12%)
  between operations  0.7 us (3%)
    ppermute x7, starting transfers between devices, exchange_shards(): blocks.append(lax.ppermute(sent[k], 'seq', [(j, j ^ k) for j in range(n)]))  13.6 us
    ppermute x7, waiting for transfers between devices, exchange_shards(): blocks.append(lax.ppermute(sent[k], 'seq', [(j, j ^ k) for j in range(n)]))  3.99 us
    pallas_call x6, Pallas kernels, call(): pl.pallas_call(kernel, out_shape=out_shape, in_specs=specs if specs is no...  3.25 us
    ppermute x3, starting transfers between devices, exchange_shards(): sums.append(lax.ppermute(terms[i], ('seq', 'head'), pairs))  3.21 us
    ppermute x3, waiting for transfers between devices, exchange_shards(): sums.append(lax.ppermute(terms[i], ('seq', 'head'), pairs))  1.43 us
    ppermute x2, starting transfers between devices, exchange_shards(): swap = lambda a: lax.ppermute(a, 'head', [(c, c ^ 1) for c in range(cores)])  0.63 us
  transfers between devices with their start and end apart: 12, of which 6 were waited for; matrix products, arithmetic and copies ran while one was open for 0% of the time, Pallas kernels for 3%

profile of v9, /device:TPU:0, one launch (start us, length us, event | category | flops | bytes accessed | tf_op | source)
XLA Modules:
  0.0 27.2 jit_solution(5500570861400634422)
XLA Ops:
  0.0 1.6 %shard_map.91 = (bf16[400,128]{1,0:T(8,128)(2,1)S(1)}, bf16[400,128]{1,0:T(8,128)(2,1)S(1)}, bf16[400,128]{1,0:T(8,128)(2,1)S(1)}, bf16[400,128]{1,0:T(8,128)(2,...) custom-call(bf16[16,1024]{1,0:T(8,128)(2,1)} %refs_0_.1, ...), custom_call_target="tpu_custom_call" | custom-call | tf_op jit(solution)/shard_map/pallas_call | solution.py:207
  1.6 5.1 %collective-permute-start = (bf16[240,128]{1,0:T(8,128)(2,1)S(1)}, bf16[240,128]{1,0:T(8,128)(2,1)S(1)}, u32[]{:S(2)}, u32[]{:S(2)}) collective-permute-start(bf16[240,128]{1,0:T(8,128)(2,1)S(1)} %get-tuple-element.20), channel_id=1, source_target_pairs={{0,12},{2,14},{4,8},{6,10},{8,4},{10,6},{12,0},{14,2},{1,13},{3,15... | collective-permute-start | bytes 184328 | tf_op jit(solution)/shard_map/ppermute | solution.py:241
  6.7 0.4 %collective-permute-start.2 = (bf16[240,128]{1,0:T(8,128)(2,1)S(1)}, bf16[240,128]{1,0:T(8,128)(2,1)S(1)}, u32[]{:S(2)}, u32[]{:S(2)}) collective-permute-start(bf16[240,128]{1,0:T(8,128)(2,1)S(1)} %get-tuple-element.22), channel_id=1, source_target_pairs={{0,10},{2,8},{4,14},{6,12},{8,2},{10,0},{12,6},{14,4},{1,11},{3,9}... | collective-permute-start | bytes 184328 | tf_op jit(solution)/shard_map/ppermute | solution.py:241
  7.0 1.3 %collective-permute-start.1 = (bf16[400,128]{1,0:T(8,128)(2,1)S(1)}, bf16[400,128]{1,0:T(8,128)(2,1)S(1)}, u32[]{:S(2)}, u32[]{:S(2)}) collective-permute-start(bf16[400,128]{1,0:T(8,128)(2,1)S(1)} %get-tuple-element.21), channel_id=1, source_target_pairs={{0,4},{2,6},{4,0},{6,2},{8,12},{10,14},{12,8},{14,10},{1,5},{3,7},... | collective-permute-start | bytes 307208 | tf_op jit(solution)/shard_map/ppermute | solution.py:241
  8.4 1.2 %collective-permute-start.3 = (bf16[400,128]{1,0:T(8,128)(2,1)S(1)}, bf16[400,128]{1,0:T(8,128)(2,1)S(1)}, u32[]{:S(2)}, u32[]{:S(2)}) collective-permute-start(bf16[400,128]{1,0:T(8,128)(2,1)S(1)} %get-tuple-element.23), channel_id=1, source_target_pairs={{0,6},{2,4},{4,2},{6,0},{8,14},{10,12},{12,10},{14,8},{1,7},{3,5},... | collective-permute-start | bytes 307208 | tf_op jit(solution)/shard_map/ppermute | solution.py:241
  9.6 0.9 %collective-permute-start.6 = (bf16[400,128]{1,0:T(8,128)(2,1)S(1)}, bf16[400,128]{1,0:T(8,128)(2,1)S(1)}, u32[]{:S(2)}, u32[]{:S(2)}) collective-permute-start(bf16[400,128]{1,0:T(8,128)(2,1)S(1)} %get-tuple-element.26), channel_id=1, source_target_pairs={{0,2},{2,0},{4,6},{6,4},{8,10},{10,8},{12,14},{14,12},{1,3},{3,1},... | collective-permute-start | bytes 307208 | tf_op jit(solution)/shard_map/ppermute | solution.py:241
  10.5 0.0 collective-permute-done.refs_1_
  10.5 3.8 %collective-permute-start.4 = (bf16[240,128]{1,0:T(8,128)(2,1)S(1)}, bf16[240,128]{1,0:T(8,128)(2,1)S(1)}, u32[]{:S(2)}, u32[]{:S(2)}) collective-permute-start(bf16[240,128]{1,0:T(8,128)(2,1)S(1)} %get-tuple-element.24), channel_id=1, source_target_pairs={{0,14},{2,12},{4,10},{6,8},{8,6},{10,4},{12,2},{14,0},{1,15},{3,13... | collective-permute-start | bytes 184328 | tf_op jit(solution)/shard_map/ppermute | solution.py:241
  14.3 0.0 collective-permute-done.2.refs_3_
  14.3 0.8 %collective-permute-start.5 = (bf16[240,128]{1,0:T(8,128)(2,1)S(1)}, bf16[240,128]{1,0:T(8,128)(2,1)S(1)}, u32[]{:S(2)}, u32[]{:S(2)}) collective-permute-start(bf16[240,128]{1,0:T(8,128)(2,1)S(1)} %get-tuple-element.25), channel_id=1, source_target_pairs={{0,8},{2,10},{4,12},{6,14},{8,0},{10,2},{12,4},{14,6},{1,9},{3,11}... | collective-permute-start | bytes 184328 | tf_op jit(solution)/shard_map/ppermute | solution.py:241
  15.8 2.5 %collective-permute-done.4.refs_5_ = bf16[240,128]{1,0:T(8,128)(2,1)S(1)} collective-permute-done((bf16[240,128]{1,0:T(8,128)(2,1)S(1)}, bf16[240,128]{1,0:T(8,128)(2,1)S(1)}, u32[]{:S(2)}, u32[]{:S(2)}) %collective-permute-start.4) | collective-permute-done | bytes 61472 | tf_op jit(solution)/shard_map/ppermute | solution.py:241
  18.3 1.5 %collective-permute-done.5.refs_6_ = bf16[240,128]{1,0:T(8,128)(2,1)S(1)} collective-permute-done((bf16[240,128]{1,0:T(8,128)(2,1)S(1)}, bf16[240,128]{1,0:T(8,128)(2,1)S(1)}, u32[]{:S(2)}, u32[]{:S(2)}) %collective-permute-start.5) | collective-permute-done | bytes 61472 | tf_op jit(solution)/shard_map/ppermute | solution.py:241
  19.8 0.0 collective-permute-done.1.refs_2_
  19.8 0.0 collective-permute-done.3.refs_4_
  19.8 0.0 collective-permute-done.6.refs_7_
  19.8 0.1 collective-permute-start.8
  19.9 0.5 %shard_map.92.big = f32[64,128]{1,0:T(8,128)S(1)} custom-call(bf16[400,128]{1,0:T(8,128)(2,1)S(1)} %get-tuple-element.19.refs_0_, bf16[240,128]{1,0:T(8,128)(2,1)S(1)} %collective-permute-done.refs_1_, bf16[400,128]{1,0:T(8,128)(2,1)S(1)} %collective-permute-done.1.refs_2_, bf16[240,128]{1,0:T(8,128)(2,1)S(1)} %collective-permute-done.2.refs_3_, ...), custom_call_target="tpu_custom_call" | custom-call | flops 1000000000 | bytes 1000000 | tf_op jit(solution)/shard_map/pallas_call | solution.py:207
  20.4 0.6 %collective-permute-start.7 = (f32[64,128]{1,0:T(8,128)S(1)}, f32[64,128]{1,0:T(8,128)S(1)}, u32[]{:S(2)}, u32[]{:S(2)}) collective-permute-start(f32[64,128]{1,0:T(8,128)S(1)} %shard_map.92.big), channel_id=1, source_target_pairs={{0,1},{1,0},{2,3},{3,2},{4,5},{5,4},{6,7},{7,6},{8,9},{9,8},{10,11... | collective-permute-start | bytes 98312 | tf_op jit(solution)/shard_map/ppermute | solution.py:251
  20.9 0.3 %collective-permute-done.8.refs_8_ = bf16[512,128]{1,0:T(8,128)(2,1)S(1)} collective-permute-done((bf16[512,128]{1,0:T(8,128)(2,1)S(1)}, bf16[512,128]{1,0:T(8,128)(2,1)S(1)}, u32[]{:S(2)}, u32[]{:S(2)}) %collective-permute-start.8) | collective-permute-done | bytes 131104 | tf_op jit(solution)/shard_map/ppermute | solution.py:251
  21.2 0.4 %shard_map.94.small = f32[64,128]{1,0:T(8,128)S(1)} custom-call(bf16[400,128]{1,0:T(8,128)(2,1)S(1)} %get-tuple-element.19.refs_0_, bf16[240,128]{1,0:T(8,128)(2,1)S(1)} %collective-permute-done.refs_1_, bf16[400,128]{1,0:T(8,128)(2,1)S(1)} %collective-permute-done.1.refs_2_, bf16[240,128]{1,0:T(8,128)(2,1)S(1)} %collective-permute-done.2.refs_3_, ...), custom_call_target="tpu_custom_call" | custom-call | flops 1000000000 | bytes 1000000 | tf_op jit(solution)/shard_map/pallas_call | solution.py:207
  21.6 0.2 collective-permute-done.7.other_big
  21.8 0.2 shard_map.95
  22.0 0.9 %collective-permute-start.10 = (f32[16,128]{1,0:T(8,128)S(1)}, f32[16,128]{1,0:T(8,128)S(1)}, u32[]{:S(2)}, u32[]{:S(2)}) collective-permute-start(f32[16,128]{1,0:T(8,128)S(1)} %get-tuple-element.31), channel_id=1, source_target_pairs={{0,7},{1,6},{2,5},{3,4},{4,3},{5,2},{6,1},{7,0},{8,15},{9,14},{10,... | collective-permute-start | bytes 24584 | tf_op jit(solution)/shard_map/ppermute | solution.py:276
  22.9 0.6 %collective-permute-start.11 = (f32[16,128]{1,0:T(8,128)S(1)}, f32[16,128]{1,0:T(8,128)S(1)}, u32[]{:S(2)}, u32[]{:S(2)}) collective-permute-start(f32[16,128]{1,0:T(8,128)S(1)} %get-tuple-element.32), channel_id=1, source_target_pairs={{0,5},{1,4},{2,7},{3,6},{4,1},{5,0},{6,3},{7,2},{8,13},{9,12},{10,... | collective-permute-start | bytes 24584 | tf_op jit(solution)/shard_map/ppermute | solution.py:276
  23.5 1.7 %collective-permute-start.9 = (f32[16,128]{1,0:T(8,128)S(1)}, f32[16,128]{1,0:T(8,128)S(1)}, u32[]{:S(2)}, u32[]{:S(2)}) collective-permute-start(f32[16,128]{1,0:T(8,128)S(1)} %get-tuple-element.30), channel_id=1, source_target_pairs={{0,3},{1,2},{2,1},{3,0},{4,7},{5,6},{6,5},{7,4},{8,11},{9,10},{10,... | collective-permute-start | bytes 24584 | tf_op jit(solution)/shard_map/ppermute | solution.py:276
  25.2 0.8 %collective-permute-done.10.refs_2_ = f32[16,128]{1,0:T(8,128)S(1)} collective-permute-done((f32[16,128]{1,0:T(8,128)S(1)}, f32[16,128]{1,0:T(8,128)S(1)}, u32[]{:S(2)}, u32[]{:S(2)}) %collective-permute-start.10) | collective-permute-done | bytes 8224 | tf_op jit(solution)/shard_map/ppermute | solution.py:276
  26.0 0.0 collective-permute-done.11.refs_3_
  26.0 0.6 %collective-permute-done.9.refs_1_ = f32[16,128]{1,0:T(8,128)S(1)} collective-permute-done((f32[16,128]{1,0:T(8,128)S(1)}, f32[16,128]{1,0:T(8,128)S(1)}, u32[]{:S(2)}, u32[]{:S(2)}) %collective-permute-start.9) | collective-permute-done | bytes 8224 | tf_op jit(solution)/shard_map/ppermute | solution.py:276
  26.6 0.6 %shard_map.96 = f32[16,128]{1,0:T(8,128)} custom-call(f32[16,128]{1,0:T(8,128)S(1)} %get-tuple-element.29.refs_0_, f32[16,128]{1,0:T(8,128)S(1)} %collective-permute-done.9.refs_1_, f32[16,128]{1,0:T(8,128)S(1)} %collective-permute-done.10.refs_2_, f32[16,128]{1,0:T(8,128)S(1)} %collective-permute-done.11.refs_3_), custom_call_target="tpu_custom_call" | custom-call | tf_op jit(solution)/shard_map/pallas_call | solution.py:207
  (1 shorter events, 0.0 us)
Async XLA Ops:
  1.6 9.0 %collective-permute-start = (bf16[240,128]{1,0:T(8,128)(2,1)S(1)}, bf16[240,128]{1,0:T(8,128)(2,1)S(1)}, u32[]{:S(2)}, u32[]{:S(2)}) collective-permute-start(bf16[240,128]{1,0:T(8,128)(2,1)S(1)} %get-tuple-element.20), channel_id=1, source_target_pairs={{0,12},{2,14},{4,8},{6,10},{8,4},{10,6},{12,0},{14,2},{1,13},{3,15... | collective-permute-start | bytes 184328 | tf_op jit(solution)/shard_map/ppermute | solution.py:241
  6.7 7.6 %collective-permute-start.2 = (bf16[240,128]{1,0:T(8,128)(2,1)S(1)}, bf16[240,128]{1,0:T(8,128)(2,1)S(1)}, u32[]{:S(2)}, u32[]{:S(2)}) collective-permute-start(bf16[240,128]{1,0:T(8,128)(2,1)S(1)} %get-tuple-element.22), channel_id=1, source_target_pairs={{0,10},{2,8},{4,14},{6,12},{8,2},{10,0},{12,6},{14,4},{1,11},{3,9}... | collective-permute-start | bytes 184328 | tf_op jit(solution)/shard_map/ppermute | solution.py:241
  7.0 12.7 %collective-permute-start.1 = (bf16[400,128]{1,0:T(8,128)(2,1)S(1)}, bf16[400,128]{1,0:T(8,128)(2,1)S(1)}, u32[]{:S(2)}, u32[]{:S(2)}) collective-permute-start(bf16[400,128]{1,0:T(8,128)(2,1)S(1)} %get-tuple-element.21), channel_id=1, source_target_pairs={{0,4},{2,6},{4,0},{6,2},{8,12},{10,14},{12,8},{14,10},{1,5},{3,7},... | collective-permute-start | bytes 307208 | tf_op jit(solution)/shard_map/ppermute | solution.py:241
  8.4 11.4 %collective-permute-start.3 = (bf16[400,128]{1,0:T(8,128)(2,1)S(1)}, bf16[400,128]{1,0:T(8,128)(2,1)S(1)}, u32[]{:S(2)}, u32[]{:S(2)}) collective-permute-start(bf16[400,128]{1,0:T(8,128)(2,1)S(1)} %get-tuple-element.23), channel_id=1, source_target_pairs={{0,6},{2,4},{4,2},{6,0},{8,14},{10,12},{12,10},{14,8},{1,7},{3,5},... | collective-permute-start | bytes 307208 | tf_op jit(solution)/shard_map/ppermute | solution.py:241
  9.6 10.2 %collective-permute-start.6 = (bf16[400,128]{1,0:T(8,128)(2,1)S(1)}, bf16[400,128]{1,0:T(8,128)(2,1)S(1)}, u32[]{:S(2)}, u32[]{:S(2)}) collective-permute-start(bf16[400,128]{1,0:T(8,128)(2,1)S(1)} %get-tuple-element.26), channel_id=1, source_target_pairs={{0,2},{2,0},{4,6},{6,4},{8,10},{10,8},{12,14},{14,12},{1,3},{3,1},... | collective-permute-start | bytes 307208 | tf_op jit(solution)/shard_map/ppermute | solution.py:241
  10.5 7.8 %collective-permute-start.4 = (bf16[240,128]{1,0:T(8,128)(2,1)S(1)}, bf16[240,128]{1,0:T(8,128)(2,1)S(1)}, u32[]{:S(2)}, u32[]{:S(2)}) collective-permute-start(bf16[240,128]{1,0:T(8,128)(2,1)S(1)} %get-tuple-element.24), channel_id=1, source_target_pairs={{0,14},{2,12},{4,10},{6,8},{8,6},{10,4},{12,2},{14,0},{1,15},{3,13... | collective-permute-start | bytes 184328 | tf_op jit(solution)/shard_map/ppermute | solution.py:241
  14.3 5.5 %collective-permute-start.5 = (bf16[240,128]{1,0:T(8,128)(2,1)S(1)}, bf16[240,128]{1,0:T(8,128)(2,1)S(1)}, u32[]{:S(2)}, u32[]{:S(2)}) collective-permute-start(bf16[240,128]{1,0:T(8,128)(2,1)S(1)} %get-tuple-element.25), channel_id=1, source_target_pairs={{0,8},{2,10},{4,12},{6,14},{8,0},{10,2},{12,4},{14,6},{1,9},{3,11}... | collective-permute-start | bytes 184328 | tf_op jit(solution)/shard_map/ppermute | solution.py:241
  19.8 1.4 %collective-permute-start.8 = (bf16[512,128]{1,0:T(8,128)(2,1)S(1)}, bf16[512,128]{1,0:T(8,128)(2,1)S(1)}, u32[]{:S(2)}, u32[]{:S(2)}) collective-permute-start(bf16[512,128]{1,0:T(8,128)(2,1)S(1)} %get-tuple-element.27), channel_id=1, source_target_pairs={{0,1},{1,0},{2,3},{3,2},{4,5},{5,4},{6,7},{7,6},{8,9},{9,8},{10,11... | collective-permute-start | bytes 393224 | tf_op jit(solution)/shard_map/ppermute | solution.py:251
  20.4 1.4 %collective-permute-start.7 = (f32[64,128]{1,0:T(8,128)S(1)}, f32[64,128]{1,0:T(8,128)S(1)}, u32[]{:S(2)}, u32[]{:S(2)}) collective-permute-start(f32[64,128]{1,0:T(8,128)S(1)} %shard_map.92.big), channel_id=1, source_target_pairs={{0,1},{1,0},{2,3},{3,2},{4,5},{5,4},{6,7},{7,6},{8,9},{9,8},{10,11... | collective-permute-start | bytes 98312 | tf_op jit(solution)/shard_map/ppermute | solution.py:251
  22.0 4.0 %collective-permute-start.10 = (f32[16,128]{1,0:T(8,128)S(1)}, f32[16,128]{1,0:T(8,128)S(1)}, u32[]{:S(2)}, u32[]{:S(2)}) collective-permute-start(f32[16,128]{1,0:T(8,128)S(1)} %get-tuple-element.31), channel_id=1, source_target_pairs={{0,7},{1,6},{2,5},{3,4},{4,3},{5,2},{6,1},{7,0},{8,15},{9,14},{10,... | collective-permute-start | bytes 24584 | tf_op jit(solution)/shard_map/ppermute | solution.py:276
  22.9 3.1 %collective-permute-start.11 = (f32[16,128]{1,0:T(8,128)S(1)}, f32[16,128]{1,0:T(8,128)S(1)}, u32[]{:S(2)}, u32[]{:S(2)}) collective-permute-start(f32[16,128]{1,0:T(8,128)S(1)} %get-tuple-element.32), channel_id=1, source_target_pairs={{0,5},{1,4},{2,7},{3,6},{4,1},{5,0},{6,3},{7,2},{8,13},{9,12},{10,... | collective-permute-start | bytes 24584 | tf_op jit(solution)/shard_map/ppermute | solution.py:276
  23.5 3.1 %collective-permute-start.9 = (f32[16,128]{1,0:T(8,128)S(1)}, f32[16,128]{1,0:T(8,128)S(1)}, u32[]{:S(2)}, u32[]{:S(2)}) collective-permute-start(f32[16,128]{1,0:T(8,128)S(1)} %get-tuple-element.30), channel_id=1, source_target_pairs={{0,3},{1,2},{2,1},{3,0},{4,7},{5,6},{6,5},{7,4},{8,11},{9,10},{10,... | collective-permute-start | bytes 24584 | tf_op jit(solution)/shard_map/ppermute | solution.py:276

commit v10 on v9

--- a/solution.py
+++ b/solution.py
@@ -75,11 +75,6 @@
     copies[1].wait()
     for j in range(near):
         put(j, rows["svr"], project(sv, sr, small_group, j, 0))
-    copies[2].wait()
-    copies[3].wait()
-    for j in range(near):
-        for g in range(0, group, 2):
-            put(j, rows["vr"] + g // 2 * tokens, project(bv, br, group, j, g))
     copies[4].wait()
     copies[5].wait()
     for j in range(near):
@@ -87,6 +82,11 @@
             cols = columns(j, small_group, g)
             put(j, rows["sk"] + g * small_tokens, sk[:, cols])
             outs[j][pl.ds(rows["sq"] + g * small_tokens, small_tokens), :] = sq[:, cols]
+    copies[2].wait()
+    copies[3].wait()
+    for j in range(near):
+        for g in range(0, group, 2):
+            put(j, rows["vr"] + g // 2 * tokens, project(bv, br, group, j, g))
     copies[6].wait()
     copies[7].wait()
     for j in range(near):

time: 27.4 us -> 27.4 us (level)
  no operation moved by 1% of the time
where the time goes in v10:
time: 27.4 us; the launch traced here: 27.2 us
  starting transfers between devices  17.4 us (64%)
  waiting for transfers between devices  5.89 us (21%)
  Pallas kernels  3.24 us (12%)
  between operations  0.7 us (3%)
    ppermute x7, starting transfers between devices, exchange_shards(): blocks.append(lax.ppermute(sent[k], 'seq', [(j, j ^ k) for j in range(n)]))  13.6 us
    ppermute x7, waiting for transfers between devices, exchange_shards(): blocks.append(lax.ppermute(sent[k], 'seq', [(j, j ^ k) for j in range(n)]))  3.99 us
    pallas_call x6, Pallas kernels, call(): pl.pallas_call(kernel, out_shape=out_shape, in_specs=specs if specs is no...  3.24 us
    ppermute x3, starting transfers between devices, exchange_shards(): sums.append(lax.ppermute(terms[i], ('seq', 'head'), pairs))  3.21 us
    ppermute x3, waiting for transfers between devices, exchange_shards(): sums.append(lax.ppermute(terms[i], ('seq', 'head'), pairs))  1.43 us
    ppermute x2, starting transfers between devices, exchange_shards(): swap = lambda a: lax.ppermute(a, 'head', [(c, c ^ 1) for c in range(cores)])  0.63 us
  transfers between devices with their start and end apart: 12, of which 6 were waited for; matrix products, arithmetic and copies ran while one was open for 0% of the time, Pallas kernels for 3%

profile of v10, /device:TPU:0, one launch (start us, length us, event | category | flops | bytes accessed | tf_op | source)
XLA Modules:
  0.0 27.2 jit_solution(4521589034132950023)
XLA Ops:
  0.0 1.6 %shard_map.91 = (bf16[400,128]{1,0:T(8,128)(2,1)S(1)}, bf16[400,128]{1,0:T(8,128)(2,1)S(1)}, bf16[400,128]{1,0:T(8,128)(2,1)S(1)}, bf16[400,128]{1,0:T(8,128)(2,...) custom-call(bf16[16,1024]{1,0:T(8,128)(2,1)} %refs_0_.1, ...), custom_call_target="tpu_custom_call" | custom-call | tf_op jit(solution)/shard_map/pallas_call | solution.py:207
  1.6 5.1 %collective-permute-start = (bf16[240,128]{1,0:T(8,128)(2,1)S(1)}, bf16[240,128]{1,0:T(8,128)(2,1)S(1)}, u32[]{:S(2)}, u32[]{:S(2)}) collective-permute-start(bf16[240,128]{1,0:T(8,128)(2,1)S(1)} %get-tuple-element.20), channel_id=1, source_target_pairs={{0,12},{2,14},{4,8},{6,10},{8,4},{10,6},{12,0},{14,2},{1,13},{3,15... | collective-permute-start | bytes 184328 | tf_op jit(solution)/shard_map/ppermute | solution.py:241
  6.7 0.4 %collective-permute-start.2 = (bf16[240,128]{1,0:T(8,128)(2,1)S(1)}, bf16[240,128]{1,0:T(8,128)(2,1)S(1)}, u32[]{:S(2)}, u32[]{:S(2)}) collective-permute-start(bf16[240,128]{1,0:T(8,128)(2,1)S(1)} %get-tuple-element.22), channel_id=1, source_target_pairs={{0,10},{2,8},{4,14},{6,12},{8,2},{10,0},{12,6},{14,4},{1,11},{3,9}... | collective-permute-start | bytes 184328 | tf_op jit(solution)/shard_map/ppermute | solution.py:241
  7.0 1.3 %collective-permute-start.1 = (bf16[400,128]{1,0:T(8,128)(2,1)S(1)}, bf16[400,128]{1,0:T(8,128)(2,1)S(1)}, u32[]{:S(2)}, u32[]{:S(2)}) collective-permute-start(bf16[400,128]{1,0:T(8,128)(2,1)S(1)} %get-tuple-element.21), channel_id=1, source_target_pairs={{0,4},{2,6},{4,0},{6,2},{8,12},{10,14},{12,8},{14,10},{1,5},{3,7},... | collective-permute-start | bytes 307208 | tf_op jit(solution)/shard_map/ppermute | solution.py:241
  8.4 1.2 %collective-permute-start.3 = (bf16[400,128]{1,0:T(8,128)(2,1)S(1)}, bf16[400,128]{1,0:T(8,128)(2,1)S(1)}, u32[]{:S(2)}, u32[]{:S(2)}) collective-permute-start(bf16[400,128]{1,0:T(8,128)(2,1)S(1)} %get-tuple-element.23), channel_id=1, source_target_pairs={{0,6},{2,4},{4,2},{6,0},{8,14},{10,12},{12,10},{14,8},{1,7},{3,5},... | collective-permute-start | bytes 307208 | tf_op jit(solution)/shard_map/ppermute | solution.py:241
  9.6 0.9 %collective-permute-start.6 = (bf16[400,128]{1,0:T(8,128)(2,1)S(1)}, bf16[400,128]{1,0:T(8,128)(2,1)S(1)}, u32[]{:S(2)}, u32[]{:S(2)}) collective-permute-start(bf16[400,128]{1,0:T(8,128)(2,1)S(1)} %get-tuple-element.26), channel_id=1, source_target_pairs={{0,2},{2,0},{4,6},{6,4},{8,10},{10,8},{12,14},{14,12},{1,3},{3,1},... | collective-permute-start | bytes 307208 | tf_op jit(solution)/shard_map/ppermute | solution.py:241
  10.5 0.0 collective-permute-done.refs_1_
  10.5 3.8 %collective-permute-start.4 = (bf16[240,128]{1,0:T(8,128)(2,1)S(1)}, bf16[240,128]{1,0:T(8,128)(2,1)S(1)}, u32[]{:S(2)}, u32[]{:S(2)}) collective-permute-start(bf16[240,128]{1,0:T(8,128)(2,1)S(1)} %get-tuple-element.24), channel_id=1, source_target_pairs={{0,14},{2,12},{4,10},{6,8},{8,6},{10,4},{12,2},{14,0},{1,15},{3,13... | collective-permute-start | bytes 184328 | tf_op jit(solution)/shard_map/ppermute | solution.py:241
  14.3 0.0 collective-permute-done.2.refs_3_
  14.3 0.8 %collective-permute-start.5 = (bf16[240,128]{1,0:T(8,128)(2,1)S(1)}, bf16[240,128]{1,0:T(8,128)(2,1)S(1)}, u32[]{:S(2)}, u32[]{:S(2)}) collective-permute-start(bf16[240,128]{1,0:T(8,128)(2,1)S(1)} %get-tuple-element.25), channel_id=1, source_target_pairs={{0,8},{2,10},{4,12},{6,14},{8,0},{10,2},{12,4},{14,6},{1,9},{3,11}... | collective-permute-start | bytes 184328 | tf_op jit(solution)/shard_map/ppermute | solution.py:241
  15.8 2.5 %collective-permute-done.4.refs_5_ = bf16[240,128]{1,0:T(8,128)(2,1)S(1)} collective-permute-done((bf16[240,128]{1,0:T(8,128)(2,1)S(1)}, bf16[240,128]{1,0:T(8,128)(2,1)S(1)}, u32[]{:S(2)}, u32[]{:S(2)}) %collective-permute-start.4) | collective-permute-done | bytes 61472 | tf_op jit(solution)/shard_map/ppermute | solution.py:241
  18.3 1.5 %collective-permute-done.5.refs_6_ = bf16[240,128]{1,0:T(8,128)(2,1)S(1)} collective-permute-done((bf16[240,128]{1,0:T(8,128)(2,1)S(1)}, bf16[240,128]{1,0:T(8,128)(2,1)S(1)}, u32[]{:S(2)}, u32[]{:S(2)}) %collective-permute-start.5) | collective-permute-done | bytes 61472 | tf_op jit(solution)/shard_map/ppermute | solution.py:241
  19.8 0.0 collective-permute-done.1.refs_2_
  19.8 0.0 collective-permute-done.3.refs_4_
  19.8 0.0 collective-permute-done.6.refs_7_
  19.8 0.1 collective-permute-start.8
  19.9 0.5 %shard_map.92.big = f32[64,128]{1,0:T(8,128)S(1)} custom-call(bf16[400,128]{1,0:T(8,128)(2,1)S(1)} %get-tuple-element.19.refs_0_, bf16[240,128]{1,0:T(8,128)(2,1)S(1)} %collective-permute-done.refs_1_, bf16[400,128]{1,0:T(8,128)(2,1)S(1)} %collective-permute-done.1.refs_2_, bf16[240,128]{1,0:T(8,128)(2,1)S(1)} %collective-permute-done.2.refs_3_, ...), custom_call_target="tpu_custom_call" | custom-call | flops 1000000000 | bytes 1000000 | tf_op jit(solution)/shard_map/pallas_call | solution.py:207
  20.4 0.6 %collective-permute-start.7 = (f32[64,128]{1,0:T(8,128)S(1)}, f32[64,128]{1,0:T(8,128)S(1)}, u32[]{:S(2)}, u32[]{:S(2)}) collective-permute-start(f32[64,128]{1,0:T(8,128)S(1)} %shard_map.92.big), channel_id=1, source_target_pairs={{0,1},{1,0},{2,3},{3,2},{4,5},{5,4},{6,7},{7,6},{8,9},{9,8},{10,11... | collective-permute-start | bytes 98312 | tf_op jit(solution)/shard_map/ppermute | solution.py:251
  20.9 0.3 %collective-permute-done.8.refs_8_ = bf16[512,128]{1,0:T(8,128)(2,1)S(1)} collective-permute-done((bf16[512,128]{1,0:T(8,128)(2,1)S(1)}, bf16[512,128]{1,0:T(8,128)(2,1)S(1)}, u32[]{:S(2)}, u32[]{:S(2)}) %collective-permute-start.8) | collective-permute-done | bytes 131104 | tf_op jit(solution)/shard_map/ppermute | solution.py:251
  21.2 0.4 %shard_map.94.small = f32[64,128]{1,0:T(8,128)S(1)} custom-call(bf16[400,128]{1,0:T(8,128)(2,1)S(1)} %get-tuple-element.19.refs_0_, bf16[240,128]{1,0:T(8,128)(2,1)S(1)} %collective-permute-done.refs_1_, bf16[400,128]{1,0:T(8,128)(2,1)S(1)} %collective-permute-done.1.refs_2_, bf16[240,128]{1,0:T(8,128)(2,1)S(1)} %collective-permute-done.2.refs_3_, ...), custom_call_target="tpu_custom_call" | custom-call | flops 1000000000 | bytes 1000000 | tf_op jit(solution)/shard_map/pallas_call | solution.py:207
  21.6 0.2 collective-permute-done.7.other_big
  21.8 0.2 shard_map.95
  22.0 0.9 %collective-permute-start.10 = (f32[16,128]{1,0:T(8,128)S(1)}, f32[16,128]{1,0:T(8,128)S(1)}, u32[]{:S(2)}, u32[]{:S(2)}) collective-permute-start(f32[16,128]{1,0:T(8,128)S(1)} %get-tuple-element.31), channel_id=1, source_target_pairs={{0,7},{1,6},{2,5},{3,4},{4,3},{5,2},{6,1},{7,0},{8,15},{9,14},{10,... | collective-permute-start | bytes 24584 | tf_op jit(solution)/shard_map/ppermute | solution.py:276
  22.9 0.6 %collective-permute-start.11 = (f32[16,128]{1,0:T(8,128)S(1)}, f32[16,128]{1,0:T(8,128)S(1)}, u32[]{:S(2)}, u32[]{:S(2)}) collective-permute-start(f32[16,128]{1,0:T(8,128)S(1)} %get-tuple-element.32), channel_id=1, source_target_pairs={{0,5},{1,4},{2,7},{3,6},{4,1},{5,0},{6,3},{7,2},{8,13},{9,12},{10,... | collective-permute-start | bytes 24584 | tf_op jit(solution)/shard_map/ppermute | solution.py:276
  23.5 1.7 %collective-permute-start.9 = (f32[16,128]{1,0:T(8,128)S(1)}, f32[16,128]{1,0:T(8,128)S(1)}, u32[]{:S(2)}, u32[]{:S(2)}) collective-permute-start(f32[16,128]{1,0:T(8,128)S(1)} %get-tuple-element.30), channel_id=1, source_target_pairs={{0,3},{1,2},{2,1},{3,0},{4,7},{5,6},{6,5},{7,4},{8,11},{9,10},{10,... | collective-permute-start | bytes 24584 | tf_op jit(solution)/shard_map/ppermute | solution.py:276
  25.2 0.8 %collective-permute-done.10.refs_2_ = f32[16,128]{1,0:T(8,128)S(1)} collective-permute-done((f32[16,128]{1,0:T(8,128)S(1)}, f32[16,128]{1,0:T(8,128)S(1)}, u32[]{:S(2)}, u32[]{:S(2)}) %collective-permute-start.10) | collective-permute-done | bytes 8224 | tf_op jit(solution)/shard_map/ppermute | solution.py:276
  26.0 0.0 collective-permute-done.11.refs_3_
  26.0 0.6 %collective-permute-done.9.refs_1_ = f32[16,128]{1,0:T(8,128)S(1)} collective-permute-done((f32[16,128]{1,0:T(8,128)S(1)}, f32[16,128]{1,0:T(8,128)S(1)}, u32[]{:S(2)}, u32[]{:S(2)}) %collective-permute-start.9) | collective-permute-done | bytes 8224 | tf_op jit(solution)/shard_map/ppermute | solution.py:276
  26.6 0.6 %shard_map.96 = f32[16,128]{1,0:T(8,128)} custom-call(f32[16,128]{1,0:T(8,128)S(1)} %get-tuple-element.29.refs_0_, f32[16,128]{1,0:T(8,128)S(1)} %collective-permute-done.9.refs_1_, f32[16,128]{1,0:T(8,128)S(1)} %collective-permute-done.10.refs_2_, f32[16,128]{1,0:T(8,128)S(1)} %collective-permute-done.11.refs_3_), custom_call_target="tpu_custom_call" | custom-call | tf_op jit(solution)/shard_map/pallas_call | solution.py:207
  (1 shorter events, 0.0 us)
Async XLA Ops:
  1.6 9.0 %collective-permute-start = (bf16[240,128]{1,0:T(8,128)(2,1)S(1)}, bf16[240,128]{1,0:T(8,128)(2,1)S(1)}, u32[]{:S(2)}, u32[]{:S(2)}) collective-permute-start(bf16[240,128]{1,0:T(8,128)(2,1)S(1)} %get-tuple-element.20), channel_id=1, source_target_pairs={{0,12},{2,14},{4,8},{6,10},{8,4},{10,6},{12,0},{14,2},{1,13},{3,15... | collective-permute-start | bytes 184328 | tf_op jit(solution)/shard_map/ppermute | solution.py:241
  6.7 7.6 %collective-permute-start.2 = (bf16[240,128]{1,0:T(8,128)(2,1)S(1)}, bf16[240,128]{1,0:T(8,128)(2,1)S(1)}, u32[]{:S(2)}, u32[]{:S(2)}) collective-permute-start(bf16[240,128]{1,0:T(8,128)(2,1)S(1)} %get-tuple-element.22), channel_id=1, source_target_pairs={{0,10},{2,8},{4,14},{6,12},{8,2},{10,0},{12,6},{14,4},{1,11},{3,9}... | collective-permute-start | bytes 184328 | tf_op jit(solution)/shard_map/ppermute | solution.py:241
  7.0 12.7 %collective-permute-start.1 = (bf16[400,128]{1,0:T(8,128)(2,1)S(1)}, bf16[400,128]{1,0:T(8,128)(2,1)S(1)}, u32[]{:S(2)}, u32[]{:S(2)}) collective-permute-start(bf16[400,128]{1,0:T(8,128)(2,1)S(1)} %get-tuple-element.21), channel_id=1, source_target_pairs={{0,4},{2,6},{4,0},{6,2},{8,12},{10,14},{12,8},{14,10},{1,5},{3,7},... | collective-permute-start | bytes 307208 | tf_op jit(solution)/shard_map/ppermute | solution.py:241
  8.4 11.4 %collective-permute-start.3 = (bf16[400,128]{1,0:T(8,128)(2,1)S(1)}, bf16[400,128]{1,0:T(8,128)(2,1)S(1)}, u32[]{:S(2)}, u32[]{:S(2)}) collective-permute-start(bf16[400,128]{1,0:T(8,128)(2,1)S(1)} %get-tuple-element.23), channel_id=1, source_target_pairs={{0,6},{2,4},{4,2},{6,0},{8,14},{10,12},{12,10},{14,8},{1,7},{3,5},... | collective-permute-start | bytes 307208 | tf_op jit(solution)/shard_map/ppermute | solution.py:241
  9.6 10.2 %collective-permute-start.6 = (bf16[400,128]{1,0:T(8,128)(2,1)S(1)}, bf16[400,128]{1,0:T(8,128)(2,1)S(1)}, u32[]{:S(2)}, u32[]{:S(2)}) collective-permute-start(bf16[400,128]{1,0:T(8,128)(2,1)S(1)} %get-tuple-element.26), channel_id=1, source_target_pairs={{0,2},{2,0},{4,6},{6,4},{8,10},{10,8},{12,14},{14,12},{1,3},{3,1},... | collective-permute-start | bytes 307208 | tf_op jit(solution)/shard_map/ppermute | solution.py:241
  10.5 7.8 %collective-permute-start.4 = (bf16[240,128]{1,0:T(8,128)(2,1)S(1)}, bf16[240,128]{1,0:T(8,128)(2,1)S(1)}, u32[]{:S(2)}, u32[]{:S(2)}) collective-permute-start(bf16[240,128]{1,0:T(8,128)(2,1)S(1)} %get-tuple-element.24), channel_id=1, source_target_pairs={{0,14},{2,12},{4,10},{6,8},{8,6},{10,4},{12,2},{14,0},{1,15},{3,13... | collective-permute-start | bytes 184328 | tf_op jit(solution)/shard_map/ppermute | solution.py:241
  14.3 5.5 %collective-permute-start.5 = (bf16[240,128]{1,0:T(8,128)(2,1)S(1)}, bf16[240,128]{1,0:T(8,128)(2,1)S(1)}, u32[]{:S(2)}, u32[]{:S(2)}) collective-permute-start(bf16[240,128]{1,0:T(8,128)(2,1)S(1)} %get-tuple-element.25), channel_id=1, source_target_pairs={{0,8},{2,10},{4,12},{6,14},{8,0},{10,2},{12,4},{14,6},{1,9},{3,11}... | collective-permute-start | bytes 184328 | tf_op jit(solution)/shard_map/ppermute | solution.py:241
  19.8 1.4 %collective-permute-start.8 = (bf16[512,128]{1,0:T(8,128)(2,1)S(1)}, bf16[512,128]{1,0:T(8,128)(2,1)S(1)}, u32[]{:S(2)}, u32[]{:S(2)}) collective-permute-start(bf16[512,128]{1,0:T(8,128)(2,1)S(1)} %get-tuple-element.27), channel_id=1, source_target_pairs={{0,1},{1,0},{2,3},{3,2},{4,5},{5,4},{6,7},{7,6},{8,9},{9,8},{10,11... | collective-permute-start | bytes 393224 | tf_op jit(solution)/shard_map/ppermute | solution.py:251
  20.4 1.4 %collective-permute-start.7 = (f32[64,128]{1,0:T(8,128)S(1)}, f32[64,128]{1,0:T(8,128)S(1)}, u32[]{:S(2)}, u32[]{:S(2)}) collective-permute-start(f32[64,128]{1,0:T(8,128)S(1)} %shard_map.92.big), channel_id=1, source_target_pairs={{0,1},{1,0},{2,3},{3,2},{4,5},{5,4},{6,7},{7,6},{8,9},{9,8},{10,11... | collective-permute-start | bytes 98312 | tf_op jit(solution)/shard_map/ppermute | solution.py:251
  22.0 4.0 %collective-permute-start.10 = (f32[16,128]{1,0:T(8,128)S(1)}, f32[16,128]{1,0:T(8,128)S(1)}, u32[]{:S(2)}, u32[]{:S(2)}) collective-permute-start(f32[16,128]{1,0:T(8,128)S(1)} %get-tuple-element.31), channel_id=1, source_target_pairs={{0,7},{1,6},{2,5},{3,4},{4,3},{5,2},{6,1},{7,0},{8,15},{9,14},{10,... | collective-permute-start | bytes 24584 | tf_op jit(solution)/shard_map/ppermute | solution.py:276
  22.9 3.1 %collective-permute-start.11 = (f32[16,128]{1,0:T(8,128)S(1)}, f32[16,128]{1,0:T(8,128)S(1)}, u32[]{:S(2)}, u32[]{:S(2)}) collective-permute-start(f32[16,128]{1,0:T(8,128)S(1)} %get-tuple-element.32), channel_id=1, source_target_pairs={{0,5},{1,4},{2,7},{3,6},{4,1},{5,0},{6,3},{7,2},{8,13},{9,12},{10,... | collective-permute-start | bytes 24584 | tf_op jit(solution)/shard_map/ppermute | solution.py:276
  23.5 3.1 %collective-permute-start.9 = (f32[16,128]{1,0:T(8,128)S(1)}, f32[16,128]{1,0:T(8,128)S(1)}, u32[]{:S(2)}, u32[]{:S(2)}) collective-permute-start(f32[16,128]{1,0:T(8,128)S(1)} %get-tuple-element.30), channel_id=1, source_target_pairs={{0,3},{1,2},{2,1},{3,0},{4,7},{5,6},{6,5},{7,4},{8,11},{9,10},{10,... | collective-permute-start | bytes 24584 | tf_op jit(solution)/shard_map/ppermute | solution.py:276
